TPU v7x, 128 devices: a whole 4x4x4 slice. The times are simulated.
128 devices in a mesh: tm: 4 (over z_lo, core), py: 4 (over y), pz: 8 (over z_hi, x).
Axes of the slice: x: 4, y: 4, z: 4 (z_hi: 2, z_lo: 2; z = z_hi * 2 + z_lo), core: 2. Of those that a mesh axis runs over, the one named last changes fastest.
Arguments:
- fine_state: float32 [4, 3, 2, 16, 32, 3, 1, 1024], P('tm', None, None, None, ('py', 'pz')), may hold values from -12 to 12
- fine_terms: float32 [4, 3, 2, 16, 32, 3, 1, 1024], P('tm', None, None, None, ('py', 'pz')), may hold values from -12 to 12
Outputs:
- fine_nodes: float32 [4, 2, 2, 16, 32, 3, 1, 1024], P('tm', None, None, None, ('py', 'pz'))
- fine_term: float32 [4, 2, 16, 32, 3, 1, 1024], P('tm', None, None, ('py', 'pz'))
- coarse_nodes: float32 [4, 2, 2, 8, 32, 3, 1, 512], P('tm', None, None, None, ('py', 'pz'))
All inputs are finite; a program needn't handle non-finite values.
Results may differ from a plain program's by a relative error of at most 0.0003.
Values sent between devices are 32-bit elements; how exact they have to be, the bound alone decides.
A program may use at most 192 MiB of HBM per device.

v0:
```python
import math

import jax
import jax.numpy as jnp
from jax import lax
from jax.sharding import PartitionSpec as P

EDGE = 1024


VISCOSITY = 0.5
TIME_STEP = 0.2
WEIGHTS = ((5.0 / 24.0, 1.0 / 3.0, -1.0 / 24.0), (-1.0 / 24.0, 1.0 / 3.0, 5.0 / 24.0))
PRECISE = lax.Precision.HIGHEST


def shifted(block, axis, distance):
    devices = range(lax.axis_size(axis))
    route = [(i - distance, i) for i in devices if i - distance in devices]
    return lax.ppermute(block, axis, route)


def signed(count):
    positions = jnp.arange(count)
    return jnp.where(positions < count // 2, positions, positions - count).astype(jnp.float32)


def angles(rows_in, columns_in, extent):
    return (
        2.0
        * math.pi
        / extent
        * (rows_in[:, None] * columns_in[None, :] % extent).astype(jnp.float32)
    )


def circle(rows_count, columns_count, extent):
    phase = angles(
        jnp.arange(rows_count, dtype=jnp.int32), jnp.arange(columns_count, dtype=jnp.int32), extent
    )
    return (jnp.cos(phase), jnp.sin(phase))


def fourier_lead(real_part, imag_part, sign, extent, kept, want_imag):
    rows_in = real_part.shape[0]
    others = real_part.shape[1:]
    columns = math.prod(others)
    bits = extent.bit_length() - 1
    first = 2 ** (bits // 2)
    second = extent // first
    filled = rows_in // second
    outer = kept // first
    first_cos, first_sin = circle(first, first, first)
    first_cos = first_cos[:, :filled]
    first_sin = first_sin[:, :filled]
    twist_cos, twist_sin = circle(first, second, extent)
    second_cos, second_sin = circle(second, second, second)
    second_cos = second_cos[:, :outer]
    second_sin = second_sin[:, :outer]
    real_in = real_part.reshape(filled, second * columns)
    section_real = jnp.dot(
        first_cos, real_in, precision=PRECISE, preferred_element_type=jnp.float32
    )
    section_imag = sign * jnp.dot(
        first_sin, real_in, precision=PRECISE, preferred_element_type=jnp.float32
    )
    if imag_part is not None:
        imag_in = imag_part.reshape(filled, second * columns)
        section_real = section_real - sign * jnp.dot(
            first_sin, imag_in, precision=PRECISE, preferred_element_type=jnp.float32
        )
        section_imag = section_imag + jnp.dot(
            first_cos, imag_in, precision=PRECISE, preferred_element_type=jnp.float32
        )
    section_real = section_real.reshape(first, second, columns)
    section_imag = section_imag.reshape(first, second, columns)
    turned_real = section_real * twist_cos[:, :, None] - sign * section_imag * twist_sin[:, :, None]
    turned_imag = section_imag * twist_cos[:, :, None] + sign * section_real * twist_sin[:, :, None]
    scale = 1.0 / math.sqrt(extent)
    final_real = jnp.einsum(
        "kbl,bm->mkl", turned_real, second_cos, precision=PRECISE
    ) - sign * jnp.einsum("kbl,bm->mkl", turned_imag, second_sin, precision=PRECISE)
    result_real = (final_real * scale).reshape((kept,) + others)
    if not want_imag:
        return (result_real, None)
    final_imag = jnp.einsum(
        "kbl,bm->mkl", turned_imag, second_cos, precision=PRECISE
    ) + sign * jnp.einsum("kbl,bm->mkl", turned_real, second_sin, precision=PRECISE)
    return (result_real, (final_imag * scale).reshape((kept,) + others))


def along_rows(real_part, imag_part, sign):
    extent = real_part.shape[-1]
    moved_real, moved_imag = fourier_lead(
        jnp.moveaxis(real_part, -1, 0), jnp.moveaxis(imag_part, -1, 0), sign, extent, extent, True
    )
    return (jnp.moveaxis(moved_real, 0, -1), jnp.moveaxis(moved_imag, 0, -1))


def level_tables(extent, groups, place):
    half_len = extent // 2
    across = half_len // groups
    all_x = jnp.arange(half_len, dtype=jnp.int32)
    weight = jnp.where(all_x == 0, 1.0, 2.0).astype(jnp.float32).reshape(half_len, 1, 1, 1)
    mode_x = (jnp.arange(across, dtype=jnp.int32) * groups + place).astype(jnp.float32)
    mode_y = signed(extent)
    wave_x = (2.0 * math.pi / EDGE * mode_x)[:, None, None, None]
    wave_y = 2.0 * math.pi / EDGE * mode_y
    wave_sq = wave_x * wave_x + wave_y * wave_y
    kept = (jnp.abs(mode_x)[:, None, None, None] <= extent // 3) & (jnp.abs(mode_y) <= extent // 3)
    anchor = (mode_x[:, None, None, None] == 0) & (mode_y == 0)
    dealias = jnp.where(kept & ~anchor, 1.0, 0.0).astype(jnp.float32)
    wave_safe = jnp.where(anchor, jnp.float32(1.0), wave_sq)
    return {
        "weight": weight,
        "wave_x": wave_x,
        "wave_y": wave_y,
        "wave_sq": wave_sq[:, :, None],
        "dealias": dealias[:, :, None],
        "wave_safe": wave_safe,
    }


def grid_layout(stacked):
    dims_in = stacked.shape
    rows_py = lax.axis_size("py")
    rows_pz = lax.axis_size("pz")
    groups = rows_py * rows_pz
    local_y = dims_in[5] // groups
    shaped = stacked.reshape(2, dims_in[1], 1, dims_in[3], dims_in[4], groups, local_y)
    moved = lax.all_to_all(shaped, ("py", "pz"), split_axis=5, concat_axis=2, tiled=True)
    return moved.reshape(2, dims_in[1], groups, dims_in[3], dims_in[4], local_y)


def mode_layout(stacked):
    dims_in = stacked.shape
    extent = dims_in[5] * dims_in[2]
    shaped = stacked.reshape(2, dims_in[1], dims_in[2], dims_in[3], dims_in[4], 1, dims_in[5])
    moved = lax.all_to_all(shaped, ("py", "pz"), split_axis=2, concat_axis=5, tiled=True)
    return moved.reshape(2, dims_in[1], 1, dims_in[3], dims_in[4], extent)


def to_grid(spectrum, tables):
    real_y, imag_y = along_rows(spectrum[0], spectrum[1], 1.0)
    spread = grid_layout(jnp.stack([real_y, imag_y]))
    half_len = spread.shape[1] * spread.shape[2]
    extent = 2 * half_len
    modes_real = spread[0].reshape((half_len,) + spread.shape[3:]) * tables["weight"]
    modes_imag = spread[1].reshape((half_len,) + spread.shape[3:]) * tables["weight"]
    grid_real, unused = fourier_lead(modes_real, modes_imag, 1.0, extent, extent, False)
    return grid_real


def to_modes(physical, across):
    extent = physical.shape[0]
    half_len = extent // 2
    real_x, imag_x = fourier_lead(physical, None, -1.0, extent, half_len, True)
    shape_out = (across, half_len // across) + physical.shape[1:]
    stacked = jnp.stack([real_x.reshape(shape_out), imag_x.reshape(shape_out)])
    spectral = mode_layout(stacked)
    real_y, imag_y = along_rows(spectral[0], spectral[1], -1.0)
    return jnp.stack([real_y, imag_y])


def nonlinear(spectrum, tables):
    wave_x, wave_y = (tables["wave_x"], tables["wave_y"])
    comp_x, comp_y, comp_z = (spectrum[:, :, :, 0], spectrum[:, :, :, 1], spectrum[:, :, :, 2])
    curled = jnp.stack(
        [wave_y * comp_z, -wave_x * comp_z, wave_x * comp_y - wave_y * comp_x], axis=3
    )
    vorticity = jnp.stack([-curled[1], curled[0]])
    physical = to_grid(jnp.concatenate([spectrum, vorticity], axis=3), tables)
    velocity, spin = (physical[:, :3], physical[:, 3:])
    crossed = jnp.stack(
        [
            velocity[:, 1] * spin[:, 2] - velocity[:, 2] * spin[:, 1],
            velocity[:, 2] * spin[:, 0] - velocity[:, 0] * spin[:, 2],
            velocity[:, 0] * spin[:, 1] - velocity[:, 1] * spin[:, 0],
        ],
        axis=1,
    )
    spectral = to_modes(crossed, spectrum.shape[1]) * tables["dealias"]
    along_k = wave_x * spectral[:, :, :, 0] + wave_y * spectral[:, :, :, 1]
    ratio = along_k / tables["wave_safe"]
    return jnp.stack(
        [
            spectral[:, :, :, 0] - wave_x * ratio,
            spectral[:, :, :, 1] - wave_y * ratio,
            spectral[:, :, :, 2],
        ],
        axis=3,
    )


def restrict(values):
    extent = values.shape[-1]
    quarter = extent // 4
    lower_x = values[:, : values.shape[1] // 2]
    return 0.5 * jnp.concatenate(
        [lower_x[..., :quarter], lower_x[..., extent - quarter :]], axis=-1
    )


def interpolate(values):
    quarter = values.shape[-1] // 2
    middle = jnp.zeros(values.shape[:-1] + (2 * quarter,), values.dtype)
    widened = jnp.concatenate([values[..., :quarter], middle, values[..., quarter:]], axis=-1)
    padding = [(0, 0), (0, values.shape[1]), (0, 0), (0, 0), (0, 0), (0, 0)]
    return 2.0 * jnp.pad(widened, padding)


def node_sweep(old, old_terms, start_value, start_term, wave_sq, evaluate):
    half_step = 0.5 * TIME_STEP
    divisor = 1.0 + half_step * VISCOSITY * wave_sq
    slopes = [old_terms[node] - VISCOSITY * wave_sq * old[node] for node in range(3)]
    section_one = start_value + half_step * (
        VISCOSITY * wave_sq * old[1] + start_term - old_terms[0]
    )
    section_one = section_one + TIME_STEP * (
        WEIGHTS[0][0] * slopes[0] + WEIGHTS[0][1] * slopes[1] + WEIGHTS[0][2] * slopes[2]
    )
    node_one = section_one / divisor
    term_one = evaluate(node_one)
    section_two = node_one + half_step * (VISCOSITY * wave_sq * old[2] + term_one - old_terms[1])
    section_two = section_two + TIME_STEP * (
        WEIGHTS[1][0] * slopes[0] + WEIGHTS[1][1] * slopes[1] + WEIGHTS[1][2] * slopes[2]
    )
    return (node_one, term_one, section_two / divisor)


def shards(fine_state, fine_terms):
    states = fine_state[0]
    terms = fine_terms[0]
    groups = lax.axis_size("py") * lax.axis_size("pz")
    place = lax.axis_index(("py", "pz"))
    time_rank = lax.axis_index("tm")
    fine_tables = level_tables(EDGE, groups, place)
    coarse_tables = level_tables(EDGE // 2, groups, place)
    passed_state, passed_term = shifted((states[2], terms[2]), "tm", 1)
    old = [states[node] for node in range(3)]
    old_terms = [terms[node] for node in range(3)]
    coarse_old = [restrict(entry_value) for entry_value in old]
    coarse_terms = [restrict(entry_value) for entry_value in old_terms]

    def coarse_eval(values):
        return nonlinear(values, coarse_tables)

    def fine_eval(values):
        return nonlinear(values, fine_tables)

    begin = coarse_old[0]
    turns = lax.axis_size("tm")
    for turn_index in range(turns):
        coarse_one, unused, coarse_two = node_sweep(
            coarse_old,
            coarse_terms,
            begin,
            coarse_eval(begin),
            coarse_tables["wave_sq"],
            coarse_eval,
        )
        if turn_index + 1 < turns:
            handed = shifted(coarse_two, "tm", 1)
            begin = jnp.where(time_rank == 0, coarse_old[0], handed)
    coarse_new = [begin, coarse_one, coarse_two]
    corrected = [old[node] + interpolate(coarse_new[node] - coarse_old[node]) for node in range(3)]
    start_value = jnp.where(time_rank == 0, old[0], passed_state)
    start_term = jnp.where(time_rank == 0, old_terms[0], passed_term)
    fine_one, term_one, fine_two = node_sweep(
        corrected, old_terms, start_value, start_term, fine_tables["wave_sq"], fine_eval
    )
    return (
        jnp.stack([fine_one, fine_two])[None],
        term_one[None],
        jnp.stack([coarse_one, coarse_two])[None],
    )


def solution(mesh):
    placed = (
        P("tm", None, None, None, ("py", "pz"), None, None, None),
        P("tm", None, None, None, ("py", "pz"), None, None, None),
    )
    return jax.shard_map(
        shards,
        mesh=mesh,
        in_specs=placed,
        out_specs=(
            P("tm", None, None, None, ("py", "pz"), None, None, None),
            P("tm", None, None, ("py", "pz"), None, None, None),
            P("tm", None, None, None, ("py", "pz"), None, None, None),
        ),
        check_vma=False,
    )
```

profile of v0, /device:TPU:32, one launch (start us, length us, event | category | flops | bytes accessed | tf_op | source)
XLA Modules:
  0.0 753.2 jit_solution(5099522825225964728)
XLA Ops:
  18.5 9.7 %all-to-all-start = ((f32[32,1,1536]{2,1,0:T(1,128)}), f32[32,1,1536]{2,1,0:T(1,128)S(1)}, u32[]{:S(2)}, u32[]{:S(2)}) async-start(f32[32,1,1536]{2,1,0:T(1,128)} %reshape.3764), calls=%async_computation | async-start | bytes 393216 | tf_op jit(solution)/shard_map/all_to_all | solution.py:131
  51.9 9.8 %copy.2148 = f32[2,8,32,3,1,1,16]{6,1,5,4,3,0,2:T(8,128)S(1)} copy(f32[2,8,32,3,1,1,16]{2,1,6,3,0,5,4:T(8,128)S(1)} %maximum_bitcast_fusion.2) | data formatting | bytes 196608 | tf_op jit(solution)/shard_map/reshape | solution.py:138
  62.6 8.2 %all-to-all-start.1 = ((f32[32,1,768]{2,1,0:T(1,128)}), f32[32,1,768]{2,1,0:T(1,128)S(1)}, u32[]{:S(2)}, u32[]{:S(2)}) async-start(f32[32,1,768]{2,1,0:T(1,128)} %reshape.3766), calls=%async_computation.1 | async-start | bytes 196608 | tf_op jit(solution)/shard_map/all_to_all | solution.py:139
  70.9 10.0 %all-to-all-done.1 = f32[32,1,768]{2,1,0:T(1,128)S(1)} async-done(((f32[32,1,768]{2,1,0:T(1,128)}), f32[32,1,768]{2,1,0:T(1,128)S(1)}, u32[]{:S(2)}, u32[]{:S(2)}) %all-to-all-start.1) | async-done | bytes 98336 | tf_op jit(solution)/shard_map/all_to_all | solution.py:139
  103.6 14.3 %all_to_all.270 = f32[32,1,1536]{2,1,0:T(1,128)S(1)} all-to-all(f32[32,1,1536]{2,1,0:T(1,128)S(1)} %reshape.3768), channel_id=1, replica_groups=mesh['tm'=4,'py'=4,'pz'=8] {'py','pz'}, dimensions={0} | all-to-all | bytes 393216 | tf_op jit(solution)/shard_map/all_to_all | solution.py:131
  131.2 13.8 %all_to_all.271 = f32[32,1,768]{2,1,0:T(1,128)S(1)} all-to-all(f32[32,1,768]{2,1,0:T(1,128)S(1)} %reshape.3770), channel_id=1, replica_groups=mesh['tm'=4,'py'=4,'pz'=8] {'py','pz'}, dimensions={0} | all-to-all | bytes 196608 | tf_op jit(solution)/shard_map/all_to_all | solution.py:139
  175.7 14.3 %all_to_all.272 = f32[32,1,1536]{2,1,0:T(1,128)S(1)} all-to-all(f32[32,1,1536]{2,1,0:T(1,128)S(1)} %reshape.3772), channel_id=1, replica_groups=mesh['tm'=4,'py'=4,'pz'=8] {'py','pz'}, dimensions={0} | all-to-all | bytes 393216 | tf_op jit(solution)/shard_map/all_to_all | solution.py:131
  203.2 13.7 %all_to_all.273 = f32[32,1,768]{2,1,0:T(1,128)S(1)} all-to-all(f32[32,1,768]{2,1,0:T(1,128)S(1)} %reshape.3774), channel_id=1, replica_groups=mesh['tm'=4,'py'=4,'pz'=8] {'py','pz'}, dimensions={0} | all-to-all | bytes 196608 | tf_op jit(solution)/shard_map/all_to_all | solution.py:139
  241.2 14.3 %all_to_all.274 = f32[32,1,1536]{2,1,0:T(1,128)S(1)} all-to-all(f32[32,1,1536]{2,1,0:T(1,128)S(1)} %reshape.3776), channel_id=1, replica_groups=mesh['tm'=4,'py'=4,'pz'=8] {'py','pz'}, dimensions={0} | all-to-all | bytes 393216 | tf_op jit(solution)/shard_map/all_to_all | solution.py:131
  268.8 13.8 %all_to_all.275 = f32[32,1,768]{2,1,0:T(1,128)S(1)} all-to-all(f32[32,1,768]{2,1,0:T(1,128)S(1)} %reshape.3778), channel_id=1, replica_groups=mesh['tm'=4,'py'=4,'pz'=8] {'py','pz'}, dimensions={0} | all-to-all | bytes 196608 | tf_op jit(solution)/shard_map/all_to_all | solution.py:139
  346.5 9.4 %all-to-all-done.9 = f32[32,1,768]{2,1,0:T(1,128)S(1)} async-done(((f32[32,1,768]{2,1,0:T(1,128)}), f32[32,1,768]{2,1,0:T(1,128)S(1)}, u32[]{:S(2)}, u32[]{:S(2)}) %all-to-all-start.9) | async-done | bytes 98336 | tf_op jit(solution)/shard_map/all_to_all | solution.py:139
  385.8 9.8 %all-to-all-done.10 = f32[32,1,1536]{2,1,0:T(1,128)S(1)} async-done(((f32[32,1,1536]{2,1,0:T(1,128)}), f32[32,1,1536]{2,1,0:T(1,128)S(1)}, u32[]{:S(2)}, u32[]{:S(2)}) %all-to-all-start.10) | async-done | bytes 196640 | tf_op jit(solution)/shard_map/all_to_all | solution.py:131
  413.5 10.1 %all-to-all-done.11 = f32[32,1,768]{2,1,0:T(1,128)S(1)} async-done(((f32[32,1,768]{2,1,0:T(1,128)}), f32[32,1,768]{2,1,0:T(1,128)S(1)}, u32[]{:S(2)}, u32[]{:S(2)}) %all-to-all-start.11) | async-done | bytes 98336 | tf_op jit(solution)/shard_map/all_to_all | solution.py:139
  460.0 9.7 %all-to-all-done.12 = f32[32,1,1536]{2,1,0:T(1,128)S(1)} async-done(((f32[32,1,1536]{2,1,0:T(1,128)}), f32[32,1,1536]{2,1,0:T(1,128)S(1)}, u32[]{:S(2)}, u32[]{:S(2)}) %all-to-all-start.12) | async-done | bytes 196640 | tf_op jit(solution)/shard_map/all_to_all | solution.py:131
  488.2 9.4 %all-to-all-done.13 = f32[32,1,768]{2,1,0:T(1,128)S(1)} async-done(((f32[32,1,768]{2,1,0:T(1,128)}), f32[32,1,768]{2,1,0:T(1,128)S(1)}, u32[]{:S(2)}, u32[]{:S(2)}) %all-to-all-start.13) | async-done | bytes 98336 | tf_op jit(solution)/shard_map/all_to_all | solution.py:139
  527.5 9.8 %all-to-all-done.14 = f32[32,1,1536]{2,1,0:T(1,128)S(1)} async-done(((f32[32,1,1536]{2,1,0:T(1,128)}), f32[32,1,1536]{2,1,0:T(1,128)S(1)}, u32[]{:S(2)}, u32[]{:S(2)}) %all-to-all-start.14) | async-done | bytes 196640 | tf_op jit(solution)/shard_map/all_to_all | solution.py:131
  555.9 9.4 %all-to-all-done.15 = f32[32,1,768]{2,1,0:T(1,128)S(1)} async-done(((f32[32,1,768]{2,1,0:T(1,128)}), f32[32,1,768]{2,1,0:T(1,128)S(1)}, u32[]{:S(2)}, u32[]{:S(2)}) %all-to-all-start.15) | async-done | bytes 98336 | tf_op jit(solution)/shard_map/all_to_all | solution.py:139
  581.6 6.0 copy.2547
  587.6 6.9 reshape.3676
  595.7 6.0 copy.2548
  601.7 7.1 reshape.3677
  638.2 10.6 %all-to-all-done.16 = f32[32,1,6144]{2,1,0:T(1,128)S(1)} async-done(((f32[32,1,6144]{2,1,0:T(1,128)}), f32[32,1,6144]{2,1,0:T(1,128)S(1)}, u32[]{:S(2)}, u32[]{:S(2)}) %all-to-all-start.16) | async-done | bytes 786464 | tf_op jit(solution)/shard_map/all_to_all | solution.py:131
  696.1 10.2 %all-to-all-done.17 = f32[32,1,3072]{2,1,0:T(1,128)S(1)} async-done(((f32[32,1,3072]{2,1,0:T(1,128)}), f32[32,1,3072]{2,1,0:T(1,128)S(1)}, u32[]{:S(2)}, u32[]{:S(2)}) %all-to-all-start.17) | async-done | bytes 393248 | tf_op jit(solution)/shard_map/all_to_all | solution.py:139
  728.7 6.3 reshape.3689
  (1132 shorter events, 502.3 us)
Async XLA Ops:
  2.7 30.5 %copy-start.3 = (f32[1,1,2,16,1,3,1,1024]{7,6,5,4,3,2,1,0:T(1,128)}, f32[1,1,2,16,1,3,1,1024]{7,6,5,4,3,2,1,0:T(1,128)S(1)}, u32[]{:S(2)}) copy-start(f32[1,1,2,16,1,3,1,1024]{7,6,5,4,3,2,1,0:T(1,128)S(1)} %get-tuple-element.52) | copy-start | bytes 1179652
  18.5 20.2 %all-to-all-start = ((f32[32,1,1536]{2,1,0:T(1,128)}), f32[32,1,1536]{2,1,0:T(1,128)S(1)}, u32[]{:S(2)}, u32[]{:S(2)}) async-start(f32[32,1,1536]{2,1,0:T(1,128)} %reshape.3764), calls=%async_computation | async-start | bytes 393216 | tf_op jit(solution)/shard_map/all_to_all | solution.py:131
  28.5 477.4 %copy-start.36 = (f32[16,32]{1,0:T(8,128)}, f32[16,32]{1,0:T(8,128)S(1)}, u32[]{:S(2)}) copy-start(f32[16,32]{1,0:T(8,128)S(1)} %broadcast_multiply_fusion.1) | copy-start | bytes 6148
  51.8 19.0 %copy-start.60 = (pred[512]{0:T(512)(128)(4,1)S(1)}, pred[512]{0:T(512)(128)(4,1)}, u32[]{:S(2)}) copy-start(pred[512]{0:T(512)(128)(4,1)} %get-tuple-element.285) | copy-start | bytes 1540
  62.6 18.4 %all-to-all-start.1 = ((f32[32,1,768]{2,1,0:T(1,128)}), f32[32,1,768]{2,1,0:T(1,128)S(1)}, u32[]{:S(2)}, u32[]{:S(2)}) async-start(f32[32,1,768]{2,1,0:T(1,128)} %reshape.3766), calls=%async_computation.1 | async-start | bytes 196608 | tf_op jit(solution)/shard_map/all_to_all | solution.py:139
  70.9 438.0 %copy-start.34 = (f32[8,512]{1,0:T(8,128)}, f32[8,512]{1,0:T(8,128)S(1)}, u32[]{:S(2)}) copy-start(f32[8,512]{1,0:T(8,128)S(1)} %get-tuple-element.269) | copy-start | bytes 49156
  157.2 5.9 collective-permute-start.1
  294.1 5.9 collective-permute-start.2
  313.3 14.4 %all-to-all-start.8 = ((f32[32,1,1536]{2,1,0:T(1,128)}), f32[32,1,1536]{2,1,0:T(1,128)S(1)}, u32[]{:S(2)}, u32[]{:S(2)}) async-start(f32[32,1,1536]{2,1,0:T(1,128)} %reshape.3780), calls=%async_computation.8 | async-start | bytes 393216 | tf_op jit(solution)/shard_map/all_to_all | solution.py:131
  317.2 261.5 %collective-permute-start = (f32[2,16,1,3,1,1024]{5,1,3,0,4,2:T(8,128)}, f32[2,16,1,3,1,1024]{5,1,3,0,4,2:T(8,128)}, u32[]{:S(2)}, u32[]{:S(2)}) collective-permute-start(f32[2,16,1,3,1,1024]{5,1,3,0,4,2:T(8,128)} %bitcast.1723), channel_id=1, source_target_pairs={{0,32},{32,64},{64,96},{1,33},{33,65},{65,97},{2,34},{34,66},{66,9... | collective-permute-start | bytes 1179656 | tf_op jit(solution)/shard_map/ppermute | solution.py:20
  319.1 259.6 %collective-permute-start.4 = (f32[2,16,1,3,1,1024]{5,1,3,0,4,2:T(8,128)}, f32[2,16,1,3,1,1024]{5,1,3,0,4,2:T(8,128)}, u32[]{:S(2)}, u32[]{:S(2)}) collective-permute-start(f32[2,16,1,3,1,1024]{5,1,3,0,4,2:T(8,128)} %bitcast.1722), channel_id=1, source_target_pairs={{0,32},{32,64},{64,96},{1,33},{33,65},{65,97},{2,34},{34,66},{66,9... | collective-permute-start | bytes 1179656 | tf_op jit(solution)/shard_map/ppermute | solution.py:20
  341.5 14.3 %all-to-all-start.9 = ((f32[32,1,768]{2,1,0:T(1,128)}), f32[32,1,768]{2,1,0:T(1,128)S(1)}, u32[]{:S(2)}, u32[]{:S(2)}) async-start(f32[32,1,768]{2,1,0:T(1,128)} %reshape.3782), calls=%async_computation.9 | async-start | bytes 196608 | tf_op jit(solution)/shard_map/all_to_all | solution.py:139
  380.8 14.7 %all-to-all-start.10 = ((f32[32,1,1536]{2,1,0:T(1,128)}), f32[32,1,1536]{2,1,0:T(1,128)S(1)}, u32[]{:S(2)}, u32[]{:S(2)}) async-start(f32[32,1,1536]{2,1,0:T(1,128)} %reshape.3784), calls=%async_computation.10 | async-start | bytes 393216 | tf_op jit(solution)/shard_map/all_to_all | solution.py:131
  409.5 14.2 %all-to-all-start.11 = ((f32[32,1,768]{2,1,0:T(1,128)}), f32[32,1,768]{2,1,0:T(1,128)S(1)}, u32[]{:S(2)}, u32[]{:S(2)}) async-start(f32[32,1,768]{2,1,0:T(1,128)} %reshape.3786), calls=%async_computation.11 | async-start | bytes 196608 | tf_op jit(solution)/shard_map/all_to_all | solution.py:139
  435.1 5.9 collective-permute-start.3
  455.0 14.8 %all-to-all-start.12 = ((f32[32,1,1536]{2,1,0:T(1,128)}), f32[32,1,1536]{2,1,0:T(1,128)S(1)}, u32[]{:S(2)}, u32[]{:S(2)}) async-start(f32[32,1,1536]{2,1,0:T(1,128)} %reshape.3788), calls=%async_computation.12 | async-start | bytes 393216 | tf_op jit(solution)/shard_map/all_to_all | solution.py:131
  483.6 14.0 %all-to-all-start.13 = ((f32[32,1,768]{2,1,0:T(1,128)}), f32[32,1,768]{2,1,0:T(1,128)S(1)}, u32[]{:S(2)}, u32[]{:S(2)}) async-start(f32[32,1,768]{2,1,0:T(1,128)} %reshape.3790), calls=%async_computation.13 | async-start | bytes 196608 | tf_op jit(solution)/shard_map/all_to_all | solution.py:139
  521.3 5.5 copy-start.44
  522.6 14.8 %all-to-all-start.14 = ((f32[32,1,1536]{2,1,0:T(1,128)}), f32[32,1,1536]{2,1,0:T(1,128)S(1)}, u32[]{:S(2)}, u32[]{:S(2)}) async-start(f32[32,1,1536]{2,1,0:T(1,128)} %reshape.3792), calls=%async_computation.14 | async-start | bytes 393216 | tf_op jit(solution)/shard_map/all_to_all | solution.py:131
  551.2 14.1 %all-to-all-start.15 = ((f32[32,1,768]{2,1,0:T(1,128)}), f32[32,1,768]{2,1,0:T(1,128)S(1)}, u32[]{:S(2)}, u32[]{:S(2)}) async-start(f32[32,1,768]{2,1,0:T(1,128)} %reshape.3794), calls=%async_computation.15 | async-start | bytes 196608 | tf_op jit(solution)/shard_map/all_to_all | solution.py:139
  632.0 16.9 %all-to-all-start.16 = ((f32[32,1,6144]{2,1,0:T(1,128)}), f32[32,1,6144]{2,1,0:T(1,128)S(1)}, u32[]{:S(2)}, u32[]{:S(2)}) async-start(f32[32,1,6144]{2,1,0:T(1,128)} %reshape.3796), calls=%async_computation.16 | async-start | bytes 1572864 | tf_op jit(solution)/shard_map/all_to_all | solution.py:131
  689.1 6.1 copy-start.45
  690.6 15.7 %all-to-all-start.17 = ((f32[32,1,3072]{2,1,0:T(1,128)}), f32[32,1,3072]{2,1,0:T(1,128)S(1)}, u32[]{:S(2)}, u32[]{:S(2)}) async-start(f32[32,1,3072]{2,1,0:T(1,128)} %reshape.3798), calls=%async_computation.17 | async-start | bytes 786432 | tf_op jit(solution)/shard_map/all_to_all | solution.py:139
  741.9 7.0 copy-start.30
  (54 other events, 155.6 us)
where the time goes:
time: 764 us; the launch traced here: 753 us
  local copies, waits for them, and re-layouts  321 us (42%)
  waiting for transfers between devices  117 us (15%)
  matrix products  109 us (14%)
  blocking collectives  84.3 us (11%)
  starting transfers between devices  70.2 us (9%)
  other arithmetic  44 us (6%)
  between operations  8.12 us (1%)
    all_to_all x6, waiting for transfers between devices, mode_layout(): lax.all_to_all(shaped, ('py', 'pz'), split_axis=2, concat_axis=5, tiled=T...  58.6 us
    all_to_all x6, waiting for transfers between devices, grid_layout(): lax.all_to_all(shaped, ('py', 'pz'), split_axis=5, concat_axis=2, tiled=T...  47.1 us
    all_to_all x3, blocking collectives, grid_layout(): lax.all_to_all(shaped, ('py', 'pz'), split_axis=5, concat_axis=2, tiled=T...  42.9 us
    all_to_all x3, blocking collectives, mode_layout(): lax.all_to_all(shaped, ('py', 'pz'), split_axis=2, concat_axis=5, tiled=T...  41.4 us
    reshape x27, local copies, waits for them, and re-layouts, fourier_lead(): real_in = real_part.reshape(filled, second * columns)  36.7 us
    unnamed x163, local copies, waits for them, and re-layouts  34.7 us
    all_to_all x6, starting transfers between devices, grid_layout(): lax.all_to_all(shaped, ('py', 'pz'), split_axis=5, concat_axis=2, tiled=T...  30.3 us
    reshape x18, local copies, waits for them, and re-layouts, fourier_lead(): imag_in = imag_part.reshape(filled, second * columns)  30.1 us
  transfers between devices with their start and end apart: 17, of which 15 were waited for; matrix products, arithmetic and copies ran while one was open for 21% of the time, Pallas kernels for 0%

commit v1 on v0

v1 whole, which is shorter than its diff:
```python
import math

import jax
import jax.numpy as jnp
import ml_dtypes
import numpy as np
from jax import lax
from jax.experimental import pallas as pl
from jax.experimental.pallas import tpu as pltpu
from jax.sharding import PartitionSpec as P

EDGE = 1024
VISCOSITY = 0.5
TIME_STEP = 0.2
HALF_STEP = 0.5 * TIME_STEP
WEIGHTS = ((5.0 / 24.0, 1.0 / 3.0, -1.0 / 24.0), (-1.0 / 24.0, 1.0 / 3.0, 5.0 / 24.0))
UNIT = 2.0 * math.pi / EDGE
GROUP = 32
ROWS = 256
LANES = 128
F32 = jnp.float32
BF16 = jnp.bfloat16
MESH = pl.DeviceIdType.MESH
TERM_ONE = [TIME_STEP * w for w in WEIGHTS[0]]
TERM_ONE[0] -= HALF_STEP
TERM_TWO = [TIME_STEP * w for w in WEIGHTS[1]]
TERM_TWO[1] -= HALF_STEP
STATE_ONE = [-TIME_STEP * w for w in WEIGHTS[0]]
STATE_ONE[1] += HALF_STEP
STATE_TWO = [-TIME_STEP * w for w in WEIGHTS[1]]
STATE_TWO[2] += HALF_STEP


def halves(table):
    high = table.astype(ml_dtypes.bfloat16)
    low = (table - high.astype(np.float64)).astype(ml_dtypes.bfloat16)
    return high, low


def lane_circle(extent):
    inner = extent // GROUP
    modes = inner // 2
    pairs = 64 // modes
    fore = np.zeros((2, pairs, modes, 2, pairs, inner))
    back = np.zeros((2, pairs, inner, 2, pairs, modes))
    phase = 2.0 * math.pi * np.outer(np.arange(modes), np.arange(inner)) / inner
    kept = (np.arange(modes) * GROUP <= extent // 3)[None, :]
    for pair in range(pairs):
        cosine, sine = 2.0 / extent * np.cos(phase), 2.0 / extent * np.sin(phase)
        fore[0, pair, :, 0, pair] = cosine
        fore[1, pair, :, 0, pair] = -sine
        fore[0, pair, :, 1, pair] = sine
        fore[1, pair, :, 1, pair] = cosine
        target = pair
        sources = [(pair, pair)]
        if extent < EDGE:
            slot, rest = divmod(pair, 2)
            sources = [(((1, 2, 0, 1)[slot]) * 2 + rest, pair)]
        for source, target in sources:
            cosine = 1.0 / extent * np.cos(phase).T * kept
            sine = 1.0 / extent * np.sin(phase).T * kept
            back[0, source, :, 0, target] = cosine
            back[1, source, :, 0, target] = sine
            back[0, source, :, 1, target] = -sine
            back[1, source, :, 1, target] = cosine
    fore = fore.reshape(128, 256)
    back = back.reshape(256, 128)
    return fore, back


def constant_tables():
    index = np.arange(ROWS)
    phase = 2.0 * math.pi * np.outer(index, index) / ROWS
    along_y = np.concatenate([np.cos(phase), np.sin(phase)], axis=1)
    small = 2.0 * math.pi * np.outer(np.arange(GROUP), np.arange(GROUP)) / GROUP
    eye = np.eye(8)
    along_x = np.concatenate([np.kron(np.cos(small), eye), -np.kron(np.sin(small), eye)], axis=1)
    along_y_high, along_y_low = halves(along_y)
    along_x_high, along_x_low = halves(along_x)
    out = [along_y_high, along_y_low, along_x_high, along_x_low]
    out += [np.ascontiguousarray(along_x_high.T), np.ascontiguousarray(along_x_low.T)]
    lane = np.arange(LANES)
    for extent in (EDGE // 2, EDGE):
        fore, back = lane_circle(extent)
        fore_high, fore_low = halves(fore)
        back_high, back_low = halves(back)
        out += [np.concatenate([fore_high, fore_high], axis=0), fore_low]
        out += [np.concatenate([back_high, back_low], axis=1)]
        inner = extent // GROUP
        turn = 2.0 * math.pi * np.outer(index // 8, lane % inner) / extent
        out += [np.cos(turn).astype(np.float32), np.sin(turn).astype(np.float32)]
        if extent < EDGE:
            offset = (lane % 16) // 8
        else:
            offset = np.array([0, 2, 1, 3])[(lane % 64) // 16]
        turn = 2.0 * math.pi * np.outer(index, offset) / extent
        out += [np.cos(turn).astype(np.float32), np.sin(turn).astype(np.float32)]
    return out


def split(value):
    high = value.astype(BF16)
    return high, (value - high.astype(F32)).astype(BF16)


def dot(left, right):
    return jnp.dot(left, right, preferred_element_type=F32)


def roll(value, shift):
    return pltpu.roll(value, shift % LANES, axis=1)


def lanes_like(value):
    return lax.broadcasted_iota(jnp.int32, value.shape, 1)


def swap(value, distance):
    bit = (lanes_like(value) // distance) % 2
    return jnp.where(bit == 1, roll(value, distance), roll(value, -distance))


def butterfly(value, distance):
    bit = (lanes_like(value) // distance) % 2
    return jnp.where(bit == 1, -value, value) + swap(value, distance)


def turned(value):
    other = roll(value, 64)
    return jnp.where(lanes_like(value) < 64, -other, other)


def tile(index):
    return pl.ds(index * LANES, LANES)


def chunks(size):
    return [pl.ds(start, size) for start in range(0, ROWS, size)]


def iterate(
    state_ref, terms_ref,
    y_high, y_low, x_high, x_low, xt_high, xt_low,
    fore_high_c, fore_low_c, back_c, turn_xc_c, turn_xs_c, turn_yc_c, turn_ys_c,
    fore_high_f, fore_low_f, back_f, turn_xc_f, turn_xs_f, turn_yc_f, turn_ys_f,
    nodes_out, term_out, coarse_out,
    rhs_high, rhs_low, grid_buf, cross_high, cross_low,
    fore_send, fore_recv, back_send, back_recv, hand_send, hand_recv,
    fine_send, fine_recv, fine_back_send, fine_back_recv, start_send, start_recv,
    right_one, right_two, mix_one, mix_two,
    curl_one, curl_two, keep_same, keep_cross, damp_c, cos_c, sin_c,
    pre_one, pre_two, old_one, old_two, begin, node_c,
    ky_f, damp_f, stiff_f, cos_f, sin_f, same_x, same_y, cross_f, mask_f,
    right_one_f, right_two_f, node_f,
    fore_sent, fore_got, back_sent, back_got, hand_sems, fine_sems, start_sems,
):
    rank = lax.axis_index("tm")
    place = lax.axis_index("py") * 8 + lax.axis_index("pz")

    def device(time_rank, position):
        return (time_rank, position // 8, position % 8)

    barrier = pltpu.get_barrier_semaphore()

    @pl.when(rank > 0)
    def _():
        def greet_back(step, carry):
            pl.semaphore_signal(
                barrier, inc=1, device_id=device(rank - 1, (place + step) % GROUP), device_id_type=MESH
            )
            return carry

        lax.fori_loop(0, GROUP, greet_back, 0)

    def greet(step, carry):
        pl.semaphore_signal(
            barrier, inc=1, device_id=device(rank, (place + step) % GROUP), device_id_type=MESH
        )
        return carry

    lax.fori_loop(1, GROUP, greet, 0)

    def block(position):
        return pl.ds(pl.multiple_of(position * 8, 8), 8)

    def post(source, target, sent, got, time_rank, first):
        def one(step, carry):
            position = (place + step) % GROUP
            pltpu.make_async_remote_copy(
                src_ref=source.at[block(position)],
                dst_ref=target.at[block(place)],
                send_sem=sent,
                recv_sem=got,
                device_id=device(time_rank, position),
                device_id_type=MESH,
            ).start()
            return carry

        if first == 1:
            pltpu.make_async_copy(source.at[block(place)], target.at[block(place)], got).start()
        lax.fori_loop(first, GROUP, one, 0)

    def receive(target, got):
        pltpu.make_async_copy(target, target, got).wait()

    def drain(source, sent, first):
        part = source.at[pl.ds(0, (GROUP - first) * 8)]
        pltpu.make_async_copy(part, part, sent).wait()

    place_f32 = place.astype(F32)
    row = lax.broadcasted_iota(jnp.int32, (ROWS, LANES), 0)
    lane = lax.broadcasted_iota(jnp.int32, (ROWS, LANES), 1)

    def wave_tables(extent, mode_x, mode_y):
        wave_x, wave_y = UNIT * mode_x, UNIT * mode_y
        wave_sq = wave_x * wave_x + wave_y * wave_y
        anchor = (mode_x == 0) & (mode_y == 0)
        kept = (mode_x <= extent // 3) & (jnp.abs(mode_y) <= extent // 3) & ~anchor
        mask = jnp.where(kept, 1.0, 0.0).astype(F32)
        inverse = mask / jnp.where(anchor, 1.0, wave_sq)
        damp = 1.0 / (1.0 + HALF_STEP * VISCOSITY * wave_sq)
        return wave_x, wave_y, wave_sq, mask, inverse, damp

    slot = (lane % 64) // 16
    mode_x = (lane % 8).astype(F32) * GROUP + place_f32
    mode_y = (row - 256 * ((lane % 16) // 8)).astype(F32)
    wave_x, wave_y, wave_sq, mask, inverse, damp = wave_tables(EDGE // 2, mode_x, mode_y)
    curl_one[...] = jnp.where(slot == 1, -wave_x, jnp.where(slot == 2, wave_x, wave_y))
    curl_two[...] = jnp.where(slot == 2, -wave_y, 0.0)
    same = jnp.where(slot == 2, mask, jnp.where(slot == 1, wave_x * wave_x, wave_y * wave_y) * inverse)
    keep_same[...] = same * (HALF_STEP * damp)
    keep_cross[...] = jnp.where(slot == 2, 0.0, -wave_x * wave_y * inverse) * (HALF_STEP * damp)
    damp_c[...] = damp
    weight = jnp.where(mode_x == 0, 0.5, 1.0)
    cos_c[...] = turn_yc_c[...] * weight
    sin_c[...] = turn_ys_c[...] * weight

    def coarse_tile(ref, base, scale, target):
        for half in range(2):
            pieces = []
            for part in range(2):
                for component in (0, 1, 2, 0):
                    for quarter in (0, 3):
                        start = base + part * 384 + component * 8 + 2 * quarter + half
                        pieces.append(ref[pl.ds(start, 8, stride=24), :])
            target[pl.ds(half * 128, 128), :] = scale * jnp.concatenate(pieces, axis=0).T

    def fine_tile(ref, component, target):
        for half in range(2):
            pieces = []
            for part in range(2):
                for quarter in range(4):
                    start = part * 384 + component * 8 + 2 * quarter + half
                    pieces.append(ref[pl.ds(start, 16, stride=24), :])
            target[pl.ds(half * 128, 128), tile(component)] = jnp.concatenate(pieces, axis=0).T

    def y_product(count, target):
        for start in range(0, count * LANES, 256):
            width = min(256, count * LANES - start)
            part = pl.ds(start, width)
            high, low = rhs_high[:, part], rhs_low[:, part]
            target[:, part] = dot(y_high[...], high) + dot(y_high[...], low) + dot(y_low[...], high)

    def stack(rows, index, first, second):
        high, low = split(first)
        rhs_high[rows, tile(index)] = high
        rhs_low[rows, tile(index)] = low
        high, low = split(second)
        lower = pl.ds(rows.start + ROWS, rows.size)
        rhs_high[lower, tile(index)] = high
        rhs_low[lower, tile(index)] = low

    def spread_coarse(source, target):
        for rows in chunks(64):
            velocity = source[rows, :]
            rotated = turned(velocity)
            back_two, back_one, ahead = roll(rotated, -32), roll(rotated, -16), roll(rotated, 16)
            position = (lanes_like(velocity) % 64) // 16
            chosen = jnp.where(position == 0, back_two, jnp.where(position == 1, back_one, ahead))
            vorticity = curl_one[rows, :] * chosen + curl_two[rows, :] * back_one
            for index, field in enumerate((velocity, vorticity)):
                mixed = butterfly(field, 8)
                mixed_turned = turned(mixed)
                cosine, sine = cos_c[rows, :], sin_c[rows, :]
                stack(
                    rows,
                    index,
                    mixed * cosine + mixed_turned * sine,
                    mixed_turned * cosine - mixed * sine,
                )
        y_product(2, target)

    def grid_stage(source, count, target, fore_high, fore_low, back, cosine_ref, sine_ref):
        cosine, sine = cosine_ref[...], sine_ref[...]
        every = pl.ds(0, ROWS)
        for index in range(count):
            high, low = split(source[:, tile(index)])
            inner = dot(jnp.concatenate([high, low], axis=1), fore_high[...]) + dot(high, fore_low[...])
            real, imag = inner[:, :LANES], inner[:, LANES:]
            stack(every, index, real * cosine - imag * sine, real * sine + imag * cosine)
        for start in range(0, count * LANES, 256):
            part = pl.ds(start, 256)
            high, low = rhs_high[:, part], rhs_low[:, part]
            grid_buf[:, part] = dot(x_high[...], high) + dot(x_high[...], low) + dot(x_low[...], high)
        if count == 2:
            speed, spin = grid_buf[:, tile(0)], grid_buf[:, tile(1)]
            crossed = [speed * roll(spin, -32) - roll(speed, -32) * spin]
        else:
            fields = [grid_buf[:, tile(index)] for index in range(6)]
            crossed = [
                fields[1] * fields[5] - fields[2] * fields[4],
                fields[2] * fields[3] - fields[0] * fields[5],
                fields[0] * fields[4] - fields[1] * fields[3],
            ]
        for index, value in enumerate(crossed):
            high, low = split(value)
            both = dot(xt_high[...], jnp.concatenate([high, low], axis=1))
            outer = both[:, :LANES] + both[:, LANES:] + dot(xt_low[...], high)
            real, imag = outer[:ROWS], outer[ROWS:]
            ready = jnp.concatenate([real * cosine + imag * sine, imag * cosine - real * sine], axis=1)
            high, low = split(ready)
            both = dot(high, back[...])
            target[:, tile(index)] = both[:, :LANES] + both[:, LANES:] + dot(low, back[:, :LANES])

    def gather_y(source, count):
        for index in range(count):
            for rows in chunks(128):
                value = source[rows, tile(index)]
                stack(rows, index, value, -turned(value))
        y_product(count, grid_buf)

    def finish_coarse(start_ref, right_ref, target):
        gather_y(back_recv.at[0] if start_ref is begin else back_recv.at[1], 1)
        for rows in chunks(128):
            value = grid_buf[rows, tile(0)]
            value = value * turn_yc_c[rows, :] - turned(value) * turn_ys_c[rows, :]
            value = butterfly(value, 8)
            position = (lanes_like(value) % 64) // 16
            partner = jnp.where(
                position == 0, roll(value, -16), jnp.where(position == 1, roll(value, 16), roll(value, 32))
            )
            term = keep_same[rows, :] * value + keep_cross[rows, :] * partner
            target[rows, :] = damp_c[rows, :] * start_ref[rows, :] + right_ref[rows, :] + term

    coarse_tile(state_ref, 0, 0.5, begin)

    @pl.when(rank == 0)
    def _():
        spread_coarse(begin, fore_send.at[0])

    @pl.when(rank < 3)
    def _():
        pl.semaphore_wait(barrier, 2 * GROUP - 1)

    @pl.when(rank == 3)
    def _():
        pl.semaphore_wait(barrier, GROUP - 1)

    @pl.when(rank == 0)
    def _():
        post(fore_send.at[0], fore_recv.at[0], fore_sent.at[0], fore_got.at[0], rank, 1)

    def combine(a, carry):
        wave_x = UNIT * (a.astype(F32) * GROUP + place_f32)
        sub = lax.broadcasted_iota(jnp.int32, (8, LANES), 0)
        mode = sub * 128 + lax.broadcasted_iota(jnp.int32, (8, LANES), 1)
        wave_y = UNIT * jnp.where(mode < EDGE // 2, mode, mode - EDGE).astype(F32)
        stiff = VISCOSITY * (wave_x * wave_x + wave_y * wave_y)
        for part in range(2):
            for component in range(3):
                base = pl.multiple_of(a * 24 + (part * 384 + component * 8), 8)
                rows = pl.ds(base, 8)
                states = [state_ref[pl.ds(base + node * 768, 8), :] for node in range(3)]
                terms = [terms_ref[pl.ds(base + node * 768, 8), :] for node in range(3)]
                one = sum(w * s for w, s in zip(STATE_ONE, states))
                two = sum(w * s for w, s in zip(STATE_TWO, states))
                mix_one[rows, :] = one
                mix_two[rows, :] = two
                right_one[rows, :] = sum(w * t for w, t in zip(TERM_ONE, terms)) + stiff * one
                right_two[rows, :] = sum(w * t for w, t in zip(TERM_TWO, terms)) + stiff * two
                start_send[rows, :] = states[2] + HALF_STEP * terms[2]
        return carry

    lax.fori_loop(0, 16, combine, 0, unroll=2)

    @pl.when(rank < 3)
    def _():
        pltpu.make_async_remote_copy(
            src_ref=start_send,
            dst_ref=start_recv,
            send_sem=start_sems.at[0],
            recv_sem=start_sems.at[1],
            device_id=device(rank + 1, place),
            device_id_type=MESH,
        ).start()

    coarse_tile(right_one, 0, 0.5, pre_one)
    pre_one[...] = pre_one[...] * damp_c[...]

    coarse_tables = (fore_high_c, fore_low_c, back_c, turn_xc_c, turn_xs_c)
    receive(fore_recv.at[0], fore_got.at[0])
    grid_stage(fore_recv.at[0], 2, back_send.at[0], *coarse_tables)
    post(back_send.at[0], back_recv.at[0], back_sent.at[0], back_got.at[0], rank, 1)

    @pl.when(rank > 0)
    def _():
        pltpu.make_async_copy(hand_recv, hand_recv, hand_sems.at[1]).wait()
        begin[...] = hand_recv[...]

    coarse_tile(right_two, 0, 0.5, pre_two)
    pre_two[...] = pre_two[...] * damp_c[...]
    receive(back_recv.at[0], back_got.at[0])
    finish_coarse(begin, pre_one, node_c)
    spread_coarse(node_c, fore_send.at[1])
    post(fore_send.at[1], fore_recv.at[1], fore_sent.at[1], fore_got.at[1], rank, 1)

    coarse_tile(mix_one, 0, 0.5, old_one)
    coarse_tile(mix_two, 0, 0.5, old_two)
    receive(fore_recv.at[1], fore_got.at[1])
    grid_stage(fore_recv.at[1], 2, back_send.at[1], *coarse_tables)
    post(back_send.at[1], back_recv.at[1], back_sent.at[1], back_got.at[1], rank, 1)

    quarter = (lane % 64) // 16
    mode_x = (lane % 16).astype(F32) * GROUP + place_f32
    mode_y = (row + 256 * quarter - jnp.where(quarter >= 2, EDGE, 0)).astype(F32)
    wave_x, wave_y, wave_sq, mask, inverse, damp = wave_tables(EDGE, mode_x, mode_y)
    ky_f[...] = wave_y
    damp_f[...] = damp
    stiff_f[...] = (2.0 * VISCOSITY) * wave_sq
    same_x[...] = wave_y * wave_y * inverse
    same_y[...] = wave_x * wave_x * inverse
    cross_f[...] = -wave_x * wave_y * inverse
    mask_f[...] = mask
    weight = jnp.where(mode_x == 0, 0.5, 1.0)
    cos_f[...] = turn_yc_f[...] * weight
    sin_f[...] = turn_ys_f[...] * weight

    receive(back_recv.at[1], back_got.at[1])
    finish_coarse(node_c, pre_two, hand_send)

    @pl.when(rank < 3)
    def _():
        spread_coarse(hand_send, fore_send.at[2])
        post(fore_send.at[2], fore_recv.at[0], fore_sent.at[2], fore_got.at[0], rank + 1, 0)
        pltpu.make_async_remote_copy(
            src_ref=hand_send,
            dst_ref=hand_recv,
            send_sem=hand_sems.at[0],
            recv_sem=hand_sems.at[1],
            device_id=device(rank + 1, place),
            device_id_type=MESH,
        ).start()

    @pl.when(rank == 0)
    def _():
        first = pl.ds(0, 768)
        right_one[...] = right_one[...] + state_ref[first, :] + HALF_STEP * terms_ref[first, :]

    @pl.when(rank > 0)
    def _():
        pltpu.make_async_copy(start_recv, start_recv, start_sems.at[1]).wait()
        right_one[...] = right_one[...] + start_recv[...]

    for component in range(3):
        fine_tile(right_one, component, right_one_f)
        fine_tile(right_two, component, right_two_f)

    for rows in chunks(64):
        news = [begin[rows, :], node_c[rows, :], hand_send[rows, :]]
        change_one = sum(w * n for w, n in zip(STATE_ONE, news)) - old_one[rows, :]
        change_two = sum(w * n for w, n in zip(STATE_TWO, news)) - old_two[rows, :]
        inner = lanes_like(change_one) % 64
        stiff, damping = stiff_f[rows, :], damp_f[rows, :]
        fields = []
        for component in range(3):

            def placed(change):
                low = jnp.where(inner < 8, roll(change, -16 * component), 0.0)
                high = roll(change, 40 - 16 * component)
                return jnp.where((inner >= 48) & (inner < 56), high, low)

            value = right_one_f[rows, tile(component)] + stiff * placed(change_one)
            value = value * damping
            node_f[rows, tile(component)] = value
            right_two_f[rows, tile(component)] = right_two_f[rows, tile(component)] + stiff * placed(change_two)
            fields.append(value)
        rotated = [turned(value) for value in fields]
        ky = ky_f[rows, :]
        kx = UNIT * ((lanes_like(ky) % 16).astype(F32) * GROUP + place_f32)
        fields += [ky * rotated[2], -kx * rotated[2], kx * rotated[1] - ky * rotated[0]]
        position = (lanes_like(ky) % 64) // 16
        cosine, sine = cos_f[rows, :], sin_f[rows, :]
        for index, field in enumerate(fields):
            mixed = butterfly(field, 32)
            mixed = jnp.where(position == 3, turned(mixed), mixed)
            mixed = butterfly(mixed, 16)
            mixed_turned = turned(mixed)
            stack(
                rows, index, mixed * cosine + mixed_turned * sine, mixed_turned * cosine - mixed * sine
            )
    y_product(6, fine_send)
    post(fine_send, fine_recv, fine_sems.at[0], fine_sems.at[1], rank, 1)

    def give_back(source, component, target, base):
        for half in range(2):
            block_t = source[pl.ds(half * 128, 128), tile(component)].T
            for part in range(2):
                for quarter in range(4):
                    start = base + part * 384 + component * 8 + 2 * quarter + half
                    first = (part * 4 + quarter) * 16
                    target[pl.ds(start, 16, stride=24), :] = block_t[first : first + 16]

    def give_back_coarse(source, base):
        for half in range(2):
            block_t = source[pl.ds(half * 128, 128), :].T
            for part in range(2):
                for component in range(3):
                    for quarter in range(2):
                        start = base + part * 96 + component * 4 + 2 * quarter + half
                        first = part * 64 + component * 16 + quarter * 8
                        coarse_out[pl.ds(start, 8, stride=12), :] = block_t[first : first + 8]

    give_back_coarse(node_c, 0)
    give_back_coarse(hand_send, 192)
    receive(fine_recv, fine_sems.at[1])
    grid_stage(
        fine_recv, 6, fine_back_send, fore_high_f, fore_low_f, back_f, turn_xc_f, turn_xs_f
    )
    post(fine_back_send, fine_back_recv, fine_sems.at[2], fine_sems.at[3], rank, 1)
    for component in range(3):
        give_back(node_f, component, nodes_out, 0)
    receive(fine_back_recv, fine_sems.at[3])
    gather_y(fine_back_recv, 3)
    for rows in chunks(64):
        cosine, sine = turn_yc_f[rows, :], turn_ys_f[rows, :]
        modes = []
        for component in range(3):
            value = grid_buf[rows, tile(component)]
            value = value * cosine - turned(value) * sine
            value = butterfly(value, 16)
            position = (lanes_like(value) % 64) // 16
            value = jnp.where(position == 3, -turned(value), value)
            modes.append(butterfly(value, 32))
        cross = cross_f[rows, :]
        results = [
            same_x[rows, :] * modes[0] + cross * modes[1],
            same_y[rows, :] * modes[1] + cross * modes[0],
            mask_f[rows, :] * modes[2],
        ]
        for component, value in enumerate(results):
            part = tile(component)
            right_one_f[rows, part] = value
            total = node_f[rows, part] + HALF_STEP * value + right_two_f[rows, part]
            node_f[rows, part] = total * damp_f[rows, :]
    for component in range(3):
        give_back(right_one_f, component, term_out, 0)
        give_back(node_f, component, nodes_out, 768)

    @pl.when(rank == 0)
    def _():
        drain(fore_send.at[0], fore_sent.at[0], 1)

    drain(fore_send.at[1], fore_sent.at[1], 1)
    for index in range(2):
        drain(back_send.at[index], back_sent.at[index], 1)
    drain(fine_send, fine_sems.at[0], 1)
    drain(fine_back_send, fine_sems.at[2], 1)

    @pl.when(rank < 3)
    def _():
        drain(fore_send.at[2], fore_sent.at[2], 0)
        pltpu.make_async_copy(hand_send, hand_send, hand_sems.at[0]).wait()
        pltpu.make_async_copy(start_send, start_send, start_sems.at[0]).wait()


def shards(fine_state, fine_terms):
    tables = [jnp.asarray(table) for table in constant_tables()]
    full, natural, wide = (ROWS, LANES), (768, LANES), (ROWS, 3 * LANES)
    dma = pltpu.SemaphoreType.DMA
    scratch = [
        pltpu.VMEM((2 * ROWS, 6 * LANES), BF16),
        pltpu.VMEM((2 * ROWS, 6 * LANES), BF16),
        pltpu.VMEM((ROWS, 6 * LANES), F32),
        pltpu.VMEM(wide, BF16),
        pltpu.VMEM(wide, BF16),
        pltpu.VMEM((3, ROWS, 2 * LANES), F32),
        pltpu.VMEM((2, ROWS, 2 * LANES), F32),
        pltpu.VMEM((2, ROWS, LANES), F32),
        pltpu.VMEM((2, ROWS, LANES), F32),
        pltpu.VMEM(full, F32),
        pltpu.VMEM(full, F32),
        pltpu.VMEM((ROWS, 6 * LANES), F32),
        pltpu.VMEM((ROWS, 6 * LANES), F32),
        pltpu.VMEM(wide, F32),
        pltpu.VMEM(wide, F32),
    ]
    scratch += [pltpu.VMEM(natural, F32)] * 6
    scratch += [pltpu.VMEM(full, F32)] * (7 + 6 + 9)
    scratch += [pltpu.VMEM(wide, F32)] * 3
    scratch += [dma((3,)), dma((2,)), dma((2,)), dma((2,)), dma((2,)), dma((4,)), dma((2,))]
    outs = pl.pallas_call(
        iterate,
        out_shape=(
            jax.ShapeDtypeStruct((1536, LANES), F32),
            jax.ShapeDtypeStruct((768, LANES), F32),
            jax.ShapeDtypeStruct((384, LANES), F32),
        ),
        in_specs=[pl.BlockSpec(memory_space=pltpu.VMEM)] * (2 + len(tables)),
        out_specs=[pl.BlockSpec(memory_space=pltpu.VMEM)] * 3,
        scratch_shapes=scratch,
        compiler_params=pltpu.CompilerParams(
            collective_id=0, has_side_effects=True, vmem_limit_bytes=44 * 1024 * 1024
        ),
        name="iterate",
    )(fine_state.reshape(2304, LANES), fine_terms.reshape(2304, LANES), *tables)
    return (
        outs[0].reshape(1, 2, 2, 16, 1, 3, 1, 1024),
        outs[1].reshape(1, 2, 16, 1, 3, 1, 1024),
        outs[2].reshape(1, 2, 2, 8, 1, 3, 1, 512),
    )


def solution(mesh):
    split_over = P("tm", None, None, None, ("py", "pz"), None, None, None)
    return jax.shard_map(
        shards,
        mesh=mesh,
        in_specs=(split_over, split_over),
        out_specs=(
            split_over,
            P("tm", None, None, ("py", "pz"), None, None, None),
            split_over,
        ),
        check_vma=False,
    )
```

time: 764 us -> 178 us (0.23)
  the two profiles are of different devices: /device:TPU:32 before, /device:TPU:33 now
where the time goes in v1:
time: 178 us
  Pallas kernels  154 us (87%)
  local copies, waits for them, and re-layouts  23.1 us (13%)
    pallas_call x1, Pallas kernels, shards(): pl.pallas_call(iterate, out_shape=(jax.ShapeDtypeStruct((1536, LANES), F3...  154 us
    unnamed x47, local copies, waits for them, and re-layouts  23.1 us

profile of v1, /device:TPU:33, one launch (start us, length us, event | category | flops | bytes accessed | tf_op | source)
XLA Modules:
  0.0 177.6 jit_solution(1672920000875782275)
XLA Ops:
  0.6 1.3 copy-done
  1.9 1.3 copy-done.1
  3.2 0.9 copy-done.2
  4.1 0.9 copy-done.3
  5.1 0.9 copy-done.4
  6.0 0.9 copy-done.5
  7.0 0.9 copy-done.6
  7.9 0.9 copy-done.7
  8.9 0.9 copy-done.8
  9.8 0.9 copy-done.9
  10.7 0.9 copy-done.10
  11.6 0.9 copy-done.11
  12.5 0.9 copy-done.12
  13.4 0.9 copy-done.13
  14.3 0.9 copy-done.14
  15.2 0.9 copy-done.15
  16.1 0.9 copy-done.16
  17.0 0.9 copy-done.17
  17.9 0.9 copy-done.18
  18.8 0.9 copy-done.19
  19.7 0.8 copy-done.20
  20.6 0.8 copy-done.21
  21.4 153.9 %iterate.1 = (f32[1536,128]{1,0:T(8,128)S(1)}, f32[768,128]{1,0:T(8,128)S(1)}, f32[384,128]{1,0:T(8,128)S(1)}) custom-call(f32[2304,128]{1,0:T(8,128)S(1)} %bitcast.5, f32[2304,128]{1,0:T(8,128)S(1)} %bitcast.6, bf16[256,512]{1,0:T(8,128)(2,1)S(1)} %copy-done.7, bf16[256,512]{1,0:T(8,128)(2,1)S(1)} %copy-done.6, bf16[256,512]{1,0:T(8,128)(2,1)S(1)} %copy-done.5, ...), custom_call_target="tpu_custom_call" | custom-call | tf_op jit(solution)/shard_map/iterate/pallas_call | solution.py:601
  175.3 0.9 copy.34
  (24 shorter events, 1.5 us)
Async XLA Ops:
  0.6 1.3 copy-start
  1.9 1.3 copy-start.1
  3.2 0.9 copy-start.2
  4.1 0.9 copy-start.3
  5.1 0.9 copy-start.4
  6.0 0.9 copy-start.5
  7.0 0.9 copy-start.6
  7.9 0.9 copy-start.7
  8.9 0.9 copy-start.8
  9.8 0.9 copy-start.9
  10.7 0.9 copy-start.10
  11.6 0.9 copy-start.11
  12.5 0.9 copy-start.12
  13.4 0.9 copy-start.13
  14.3 0.9 copy-start.14
  15.2 0.9 copy-start.15
  16.1 0.9 copy-start.16
  17.0 0.9 copy-start.17
  17.9 0.9 copy-start.18
  18.8 0.9 copy-start.19
  19.7 0.8 copy-start.20
  20.6 0.8 copy-start.21

commit v2 on v1

--- a/solution.py
+++ b/solution.py
@@ -75,27 +75,28 @@
     small = 2.0 * math.pi * np.outer(np.arange(GROUP), np.arange(GROUP)) / GROUP
     eye = np.eye(8)
     along_x = np.concatenate([np.kron(np.cos(small), eye), -np.kron(np.sin(small), eye)], axis=1)
-    along_y_high, along_y_low = halves(along_y)
-    along_x_high, along_x_low = halves(along_x)
-    out = [along_y_high, along_y_low, along_x_high, along_x_low]
-    out += [np.ascontiguousarray(along_x_high.T), np.ascontiguousarray(along_x_low.T)]
+    matrices = list(halves(along_y)) + list(halves(along_x))
+    matrices.append(np.concatenate(halves(along_x.T), axis=1))
     lane = np.arange(LANES)
+    turns, inner_parts = [], []
     for extent in (EDGE // 2, EDGE):
         fore, back = lane_circle(extent)
         fore_high, fore_low = halves(fore)
         back_high, back_low = halves(back)
-        out += [np.concatenate([fore_high, fore_high], axis=0), fore_low]
-        out += [np.concatenate([back_high, back_low], axis=1)]
+        inner_parts.append(
+            np.concatenate([fore_high, fore_high, fore_low, np.concatenate([back_high, back_low], axis=1)], axis=0)
+        )
         inner = extent // GROUP
         turn = 2.0 * math.pi * np.outer(index // 8, lane % inner) / extent
-        out += [np.cos(turn).astype(np.float32), np.sin(turn).astype(np.float32)]
+        turns += [np.cos(turn), np.sin(turn)]
         if extent < EDGE:
             offset = (lane % 16) // 8
         else:
             offset = np.array([0, 2, 1, 3])[(lane % 64) // 16]
         turn = 2.0 * math.pi * np.outer(index, offset) / extent
-        out += [np.cos(turn).astype(np.float32), np.sin(turn).astype(np.float32)]
-    return out
+        turns += [np.cos(turn), np.sin(turn)]
+    matrices.append(np.concatenate(inner_parts, axis=1))
+    return np.concatenate(matrices, axis=0), np.concatenate(turns, axis=0).astype(np.float32)
 
 
 def split(value):
@@ -139,10 +140,7 @@
 
 
 def iterate(
-    state_ref, terms_ref,
-    y_high, y_low, x_high, x_low, xt_high, xt_low,
-    fore_high_c, fore_low_c, back_c, turn_xc_c, turn_xs_c, turn_yc_c, turn_ys_c,
-    fore_high_f, fore_low_f, back_f, turn_xc_f, turn_xs_f, turn_yc_f, turn_ys_f,
+    state_hbm, terms_hbm, matrices_hbm, turns_hbm,
     nodes_out, term_out, coarse_out,
     rhs_high, rhs_low, grid_buf, cross_high, cross_low,
     fore_send, fore_recv, back_send, back_recv, hand_send, hand_recv,
@@ -152,8 +150,34 @@
     pre_one, pre_two, old_one, old_two, begin, node_c,
     ky_f, damp_f, stiff_f, cos_f, sin_f, same_x, same_y, cross_f, mask_f,
     right_one_f, right_two_f, node_f,
-    fore_sent, fore_got, back_sent, back_got, hand_sems, fine_sems, start_sems,
+    state_ref, terms_ref, matrices, turns,
+    fore_sent, fore_got, back_sent, back_got, hand_sems, fine_sems, start_sems, load_sems,
 ):
+    loads = []
+    for source, target, start, size in (
+        (state_hbm, state_ref, 0, 768),
+        (matrices_hbm, matrices, 0, 512),
+        (turns_hbm, turns, 0, 1024),
+        (state_hbm, state_ref, 768, 1536),
+        (terms_hbm, terms_ref, 0, 2304),
+        (matrices_hbm, matrices, 512, 1664),
+        (turns_hbm, turns, 1024, 1024),
+    ):
+        rows = pl.ds(start, size)
+        loads.append(pltpu.make_async_copy(source.at[rows], target.at[rows], load_sems.at[len(loads)]))
+        loads[-1].start()
+
+    def matrix(start, size, first=0, width=512):
+        return matrices.at[pl.ds(start, size), pl.ds(first, width)]
+
+    y_high, y_low = matrix(0, 256), matrix(256, 256)
+    x_high, x_low = matrix(512, 256), matrix(768, 256)
+    xt_high, xt_low = matrix(1024, 512, 0, 256), matrix(1024, 512, 256, 256)
+    fore_high_c, fore_low_c, back_c = (matrix(*rows, 0, 256) for rows in ((1536, 256), (1792, 128), (1920, 256)))
+    fore_high_f, fore_low_f, back_f = (matrix(*rows, 256, 256) for rows in ((1536, 256), (1792, 128), (1920, 256)))
+    turn_xc_c, turn_xs_c, turn_yc_c, turn_ys_c, turn_xc_f, turn_xs_f, turn_yc_f, turn_ys_f = (
+        turns.at[pl.ds(start, ROWS), :] for start in range(0, 8 * ROWS, ROWS)
+    )
     rank = lax.axis_index("tm")
     place = lax.axis_index("py") * 8 + lax.axis_index("pz")
 
@@ -221,6 +245,7 @@
         damp = 1.0 / (1.0 + HALF_STEP * VISCOSITY * wave_sq)
         return wave_x, wave_y, wave_sq, mask, inverse, damp
 
+    loads[2].wait()
     slot = (lane % 64) // 16
     mode_x = (lane % 8).astype(F32) * GROUP + place_f32
     mode_y = (row - 256 * ((lane % 16) // 8)).astype(F32)
@@ -342,7 +367,9 @@
             term = keep_same[rows, :] * value + keep_cross[rows, :] * partner
             target[rows, :] = damp_c[rows, :] * start_ref[rows, :] + right_ref[rows, :] + term
 
+    loads[0].wait()
     coarse_tile(state_ref, 0, 0.5, begin)
+    loads[1].wait()
 
     @pl.when(rank == 0)
     def _():
@@ -381,6 +408,8 @@
                 start_send[rows, :] = states[2] + HALF_STEP * terms[2]
         return carry
 
+    for index in (3, 4, 5, 6):
+        loads[index].wait()
     lax.fori_loop(0, 16, combine, 0, unroll=2)
 
     @pl.when(rank < 3)
@@ -465,39 +494,42 @@
         fine_tile(right_one, component, right_one_f)
         fine_tile(right_two, component, right_two_f)
 
-    for rows in chunks(64):
-        news = [begin[rows, :], node_c[rows, :], hand_send[rows, :]]
-        change_one = sum(w * n for w, n in zip(STATE_ONE, news)) - old_one[rows, :]
-        change_two = sum(w * n for w, n in zip(STATE_TWO, news)) - old_two[rows, :]
-        inner = lanes_like(change_one) % 64
-        stiff, damping = stiff_f[rows, :], damp_f[rows, :]
-        fields = []
-        for component in range(3):
-
-            def placed(change):
-                low = jnp.where(inner < 8, roll(change, -16 * component), 0.0)
-                high = roll(change, 40 - 16 * component)
-                return jnp.where((inner >= 48) & (inner < 56), high, low)
-
-            value = right_one_f[rows, tile(component)] + stiff * placed(change_one)
-            value = value * damping
-            node_f[rows, tile(component)] = value
-            right_two_f[rows, tile(component)] = right_two_f[rows, tile(component)] + stiff * placed(change_two)
-            fields.append(value)
-        rotated = [turned(value) for value in fields]
-        ky = ky_f[rows, :]
-        kx = UNIT * ((lanes_like(ky) % 16).astype(F32) * GROUP + place_f32)
-        fields += [ky * rotated[2], -kx * rotated[2], kx * rotated[1] - ky * rotated[0]]
-        position = (lanes_like(ky) % 64) // 16
-        cosine, sine = cos_f[rows, :], sin_f[rows, :]
-        for index, field in enumerate(fields):
-            mixed = butterfly(field, 32)
-            mixed = jnp.where(position == 3, turned(mixed), mixed)
-            mixed = butterfly(mixed, 16)
-            mixed_turned = turned(mixed)
-            stack(
-                rows, index, mixed * cosine + mixed_turned * sine, mixed_turned * cosine - mixed * sine
-            )
+    def spread_fine():
+        for rows in chunks(64):
+            news = [begin[rows, :], node_c[rows, :], hand_send[rows, :]]
+            change_one = sum(w * n for w, n in zip(STATE_ONE, news)) - old_one[rows, :]
+            change_two = sum(w * n for w, n in zip(STATE_TWO, news)) - old_two[rows, :]
+            inner = lanes_like(change_one) % 64
+            stiff, damping = stiff_f[rows, :], damp_f[rows, :]
+            fields = []
+            for component in range(3):
+
+                def placed(change):
+                    low = jnp.where(inner < 8, roll(change, -16 * component), 0.0)
+                    high = roll(change, 40 - 16 * component)
+                    return jnp.where((inner >= 48) & (inner < 56), high, low)
+
+                value = right_one_f[rows, tile(component)] + stiff * placed(change_one)
+                value = value * damping
+                node_f[rows, tile(component)] = value
+                right_two_f[rows, tile(component)] = right_two_f[rows, tile(component)] + stiff * placed(change_two)
+                fields.append(value)
+            rotated = [turned(value) for value in fields]
+            ky = ky_f[rows, :]
+            kx = UNIT * ((lanes_like(ky) % 16).astype(F32) * GROUP + place_f32)
+            fields += [ky * rotated[2], -kx * rotated[2], kx * rotated[1] - ky * rotated[0]]
+            position = (lanes_like(ky) % 64) // 16
+            cosine, sine = cos_f[rows, :], sin_f[rows, :]
+            for index, field in enumerate(fields):
+                mixed = butterfly(field, 32)
+                mixed = jnp.where(position == 3, turned(mixed), mixed)
+                mixed = butterfly(mixed, 16)
+                mixed_turned = turned(mixed)
+                stack(
+                    rows, index, mixed * cosine + mixed_turned * sine, mixed_turned * cosine - mixed * sine
+                )
+
+    spread_fine()
     y_product(6, fine_send)
     post(fine_send, fine_recv, fine_sems.at[0], fine_sems.at[1], rank, 1)
 
@@ -531,27 +563,30 @@
         give_back(node_f, component, nodes_out, 0)
     receive(fine_back_recv, fine_sems.at[3])
     gather_y(fine_back_recv, 3)
-    for rows in chunks(64):
-        cosine, sine = turn_yc_f[rows, :], turn_ys_f[rows, :]
-        modes = []
-        for component in range(3):
-            value = grid_buf[rows, tile(component)]
-            value = value * cosine - turned(value) * sine
-            value = butterfly(value, 16)
-            position = (lanes_like(value) % 64) // 16
-            value = jnp.where(position == 3, -turned(value), value)
-            modes.append(butterfly(value, 32))
-        cross = cross_f[rows, :]
-        results = [
-            same_x[rows, :] * modes[0] + cross * modes[1],
-            same_y[rows, :] * modes[1] + cross * modes[0],
-            mask_f[rows, :] * modes[2],
-        ]
-        for component, value in enumerate(results):
-            part = tile(component)
-            right_one_f[rows, part] = value
-            total = node_f[rows, part] + HALF_STEP * value + right_two_f[rows, part]
-            node_f[rows, part] = total * damp_f[rows, :]
+    def finish_fine():
+        for rows in chunks(64):
+            cosine, sine = turn_yc_f[rows, :], turn_ys_f[rows, :]
+            modes = []
+            for component in range(3):
+                value = grid_buf[rows, tile(component)]
+                value = value * cosine - turned(value) * sine
+                value = butterfly(value, 16)
+                position = (lanes_like(value) % 64) // 16
+                value = jnp.where(position == 3, -turned(value), value)
+                modes.append(butterfly(value, 32))
+            cross = cross_f[rows, :]
+            results = [
+                same_x[rows, :] * modes[0] + cross * modes[1],
+                same_y[rows, :] * modes[1] + cross * modes[0],
+                mask_f[rows, :] * modes[2],
+            ]
+            for component, value in enumerate(results):
+                part = tile(component)
+                right_one_f[rows, part] = value
+                total = node_f[rows, part] + HALF_STEP * value + right_two_f[rows, part]
+                node_f[rows, part] = total * damp_f[rows, :]
+
+    finish_fine()
     for component in range(3):
         give_back(right_one_f, component, term_out, 0)
         give_back(node_f, component, nodes_out, 768)
@@ -574,7 +609,7 @@
 
 
 def shards(fine_state, fine_terms):
-    tables = [jnp.asarray(table) for table in constant_tables()]
+    matrices, turns = constant_tables()
     full, natural, wide = (ROWS, LANES), (768, LANES), (ROWS, 3 * LANES)
     dma = pltpu.SemaphoreType.DMA
     scratch = [
@@ -597,7 +632,9 @@
     scratch += [pltpu.VMEM(natural, F32)] * 6
     scratch += [pltpu.VMEM(full, F32)] * (7 + 6 + 9)
     scratch += [pltpu.VMEM(wide, F32)] * 3
-    scratch += [dma((3,)), dma((2,)), dma((2,)), dma((2,)), dma((2,)), dma((4,)), dma((2,))]
+    scratch += [pltpu.VMEM((2304, LANES), F32)] * 2
+    scratch += [pltpu.VMEM(matrices.shape, BF16), pltpu.VMEM(turns.shape, F32)]
+    scratch += [dma((count,)) for count in (3, 2, 2, 2, 2, 4, 2, 7)]
     outs = pl.pallas_call(
         iterate,
         out_shape=(
@@ -605,14 +642,14 @@
             jax.ShapeDtypeStruct((768, LANES), F32),
             jax.ShapeDtypeStruct((384, LANES), F32),
         ),
-        in_specs=[pl.BlockSpec(memory_space=pltpu.VMEM)] * (2 + len(tables)),
+        in_specs=[pl.BlockSpec(memory_space=pltpu.HBM)] * 4,
         out_specs=[pl.BlockSpec(memory_space=pltpu.VMEM)] * 3,
         scratch_shapes=scratch,
         compiler_params=pltpu.CompilerParams(
-            collective_id=0, has_side_effects=True, vmem_limit_bytes=44 * 1024 * 1024
+            collective_id=0, has_side_effects=True, vmem_limit_bytes=62 * 1024 * 1024
         ),
         name="iterate",
-    )(fine_state.reshape(2304, LANES), fine_terms.reshape(2304, LANES), *tables)
+    )(fine_state.reshape(2304, LANES), fine_terms.reshape(2304, LANES), jnp.asarray(matrices), jnp.asarray(turns))
     return (
         outs[0].reshape(1, 2, 2, 16, 1, 3, 1, 1024),
         outs[1].reshape(1, 2, 16, 1, 3, 1, 1024),

time: 178 us -> 160 us (0.90)
  local copies, waits for them, and re-layouts: 23.1 us -> 4.04 us
    unnamed x47 -> x7, local copies, waits for them, and re-layouts: 23.1 us -> 4.04 us
where the time goes in v2:
time: 160 us
  Pallas kernels  155 us (97%)
  local copies, waits for them, and re-layouts  4.04 us (3%)
    pallas_call x1, Pallas kernels, shards(): pl.pallas_call(iterate, out_shape=(jax.ShapeDtypeStruct((1536, LANES), F3...  155 us
    unnamed x7, local copies, waits for them, and re-layouts  4.04 us

profile of v2, /device:TPU:33, one launch (start us, length us, event | category | flops | bytes accessed | tf_op | source)
XLA Modules:
  0.0 160.0 jit_solution(16541013141142250365)
XLA Ops:
  0.6 155.3 %iterate.1 = (f32[1536,128]{1,0:T(8,128)}, f32[768,128]{1,0:T(8,128)}, f32[384,128]{1,0:T(8,128)}) custom-call(f32[2304,128]{1,0:T(8,128)} %bitcast.5, f32[2304,128]{1,0:T(8,128)} %bitcast.6, bf16[2176,512]{1,0:T(8,128)(2,1)} %constant.4.clone.matrices_hbm, f32[2048,128]{1,0:T(8,128)} %constant.5.clone.turns_hbm), custom_call_target="tpu_custom_call" | custom-call | tf_op jit(solution)/shard_map/iterate/pallas_call | solution.py:638
  155.9 0.0 copy-start
  155.9 0.0 copy-start.1
  155.9 2.6 %copy.16 = f32[1,2,2,16,1,3,1,1024]{7,6,5,4,3,2,1,0:T(1,128)} copy(f32[1,2,2,16,1,3,1,1024]{7,6,5,4,3,2,1,0:T(1,128)} %bitcast.7) | data formatting | bytes 1572864
  158.5 0.0 copy-done
  158.5 0.7 copy.17
  159.3 0.0 copy-done.1
  159.3 0.7 copy.18
Async XLA Ops:
  155.9 2.6 %copy-start = (f32[768,128]{1,0:T(8,128)S(1)}, f32[768,128]{1,0:T(8,128)}, u32[]{:S(2)}) copy-start(f32[768,128]{1,0:T(8,128)} %get-tuple-element.7) | copy-start | bytes 1179652
  155.9 3.4 %copy-start.1 = (f32[384,128]{1,0:T(8,128)S(1)}, f32[384,128]{1,0:T(8,128)}, u32[]{:S(2)}) copy-start(f32[384,128]{1,0:T(8,128)} %get-tuple-element.8) | copy-start | bytes 589828

commit v3 on v2

--- a/solution.py
+++ b/solution.py
@@ -29,6 +29,13 @@
 STATE_ONE[1] += HALF_STEP
 STATE_TWO = [-TIME_STEP * w for w in WEIGHTS[1]]
 STATE_TWO[2] += HALF_STEP
+
+
+HOPS = (0, 1, 2, 1)
+OFFSETS = sorted(
+    ((y, z, x) for y in range(4) for z in range(2) for x in range(4)),
+    key=lambda step: -(HOPS[step[0]] + 2 * step[1] + HOPS[step[2]]),
+)
 
 
 def halves(table):
@@ -68,6 +75,47 @@
     return fore, back
 
 
+def real_form(table):
+    return np.block([[table.real, table.imag], [-table.imag, table.real]])
+
+
+def doubled(table):
+    return np.concatenate([table, table], axis=0)
+
+
+def lane_maps():
+    sign = np.array([[1.0, 1.0], [1.0, -1.0]])
+    curl_y, curl_x, partner = np.zeros((4, 4)), np.zeros((4, 4)), np.zeros((4, 4))
+    curl_y[2, 0] = curl_y[2, 3] = 1.0
+    curl_y[0, 2] = -1.0
+    curl_x[2, 1] = -1.0
+    curl_x[1, 2] = 1.0
+    partner[1, 0] = partner[1, 3] = partner[0, 1] = 1.0
+
+    def coarse(slots):
+        table = np.kron(np.kron(slots, sign), np.eye(8)).astype(complex)
+        return real_form(table), real_form(1j * table)
+
+    same = coarse(np.eye(4))
+    spread_c = doubled(np.concatenate(same, axis=1))
+    curl_c = np.concatenate([np.concatenate(coarse(slots), axis=1) for slots in (curl_y, curl_x)], axis=0)
+    finish_c = doubled(np.concatenate([same[0], coarse(partner)[0]], axis=1))
+    quarters, powers = np.arange(4), np.array([0, 2, 1, 3])
+    table = np.kron(1j ** (np.outer(quarters, powers) % 4), np.eye(16))
+    spread_f = doubled(np.concatenate([real_form(table), real_form(1j * table)], axis=1))
+    finish_f = doubled(real_form(np.conj(table).T))
+    place = np.zeros((3, 4, 2, 8, 4, 16))
+    for component in range(3):
+        for a in range(8):
+            place[component, component, 0, a, 0, a] = 1.0
+            place[component, component, 1, a, 3, a] = 1.0
+    place_f = doubled(np.concatenate([real_form(table.reshape(64, 64).astype(complex)) for table in place], axis=1))
+    return [
+        np.concatenate(pair, axis=1).astype(ml_dtypes.bfloat16)
+        for pair in ((spread_c, curl_c), (finish_c, spread_f), (place_f, finish_f))
+    ]
+
+
 def constant_tables():
     index = np.arange(ROWS)
     phase = 2.0 * math.pi * np.outer(index, index) / ROWS
@@ -75,7 +123,8 @@
     small = 2.0 * math.pi * np.outer(np.arange(GROUP), np.arange(GROUP)) / GROUP
     eye = np.eye(8)
     along_x = np.concatenate([np.kron(np.cos(small), eye), -np.kron(np.sin(small), eye)], axis=1)
-    matrices = list(halves(along_y)) + list(halves(along_x))
+    maps = lane_maps()
+    matrices = list(halves(along_y)) + [maps[0]] + list(halves(along_x))
     matrices.append(np.concatenate(halves(along_x.T), axis=1))
     lane = np.arange(LANES)
     turns, inner_parts = [], []
@@ -96,6 +145,7 @@
         turn = 2.0 * math.pi * np.outer(index, offset) / extent
         turns += [np.cos(turn), np.sin(turn)]
     matrices.append(np.concatenate(inner_parts, axis=1))
+    matrices += maps[1:]
     return np.concatenate(matrices, axis=0), np.concatenate(turns, axis=0).astype(np.float32)
 
 
@@ -116,16 +166,6 @@
     return lax.broadcasted_iota(jnp.int32, value.shape, 1)
 
 
-def swap(value, distance):
-    bit = (lanes_like(value) // distance) % 2
-    return jnp.where(bit == 1, roll(value, distance), roll(value, -distance))
-
-
-def butterfly(value, distance):
-    bit = (lanes_like(value) // distance) % 2
-    return jnp.where(bit == 1, -value, value) + swap(value, distance)
-
-
 def turned(value):
     other = roll(value, 64)
     return jnp.where(lanes_like(value) < 64, -other, other)
@@ -142,7 +182,7 @@
 def iterate(
     state_hbm, terms_hbm, matrices_hbm, turns_hbm,
     nodes_out, term_out, coarse_out,
-    rhs_high, rhs_low, grid_buf, cross_high, cross_low,
+    rhs_high, rhs_low, grid_buf,
     fore_send, fore_recv, back_send, back_recv, hand_send, hand_recv,
     fine_send, fine_recv, fine_back_send, fine_back_recv, start_send, start_recv,
     right_one, right_two, mix_one, mix_two,
@@ -151,16 +191,17 @@
     ky_f, damp_f, stiff_f, cos_f, sin_f, same_x, same_y, cross_f, mask_f,
     right_one_f, right_two_f, node_f,
     state_ref, terms_ref, matrices, turns,
-    fore_sent, fore_got, back_sent, back_got, hand_sems, fine_sems, start_sems, load_sems,
+    fore_sent, fore_got, back_sent, back_got, hand_sems, fine_sent, fine_got, fine_back_sent, fine_back_got, start_sems,
+    load_sems,
 ):
     loads = []
     for source, target, start, size in (
         (state_hbm, state_ref, 0, 768),
-        (matrices_hbm, matrices, 0, 512),
+        (matrices_hbm, matrices, 0, 768),
         (turns_hbm, turns, 0, 1024),
         (state_hbm, state_ref, 768, 1536),
         (terms_hbm, terms_ref, 0, 2304),
-        (matrices_hbm, matrices, 512, 1664),
+        (matrices_hbm, matrices, 768, 2176),
         (turns_hbm, turns, 1024, 1024),
     ):
         rows = pl.ds(start, size)
@@ -171,10 +212,13 @@
         return matrices.at[pl.ds(start, size), pl.ds(first, width)]
 
     y_high, y_low = matrix(0, 256), matrix(256, 256)
-    x_high, x_low = matrix(512, 256), matrix(768, 256)
-    xt_high, xt_low = matrix(1024, 512, 0, 256), matrix(1024, 512, 256, 256)
-    fore_high_c, fore_low_c, back_c = (matrix(*rows, 0, 256) for rows in ((1536, 256), (1792, 128), (1920, 256)))
-    fore_high_f, fore_low_f, back_f = (matrix(*rows, 256, 256) for rows in ((1536, 256), (1792, 128), (1920, 256)))
+    spread_map, curl_map = matrix(512, 256, 0, 256), matrix(512, 256, 256, 256)
+    x_high, x_low = matrix(768, 256), matrix(1024, 256)
+    xt_high, xt_low = matrix(1280, 512, 0, 256), matrix(1280, 512, 256, 256)
+    fore_high_c, fore_low_c, back_c = (matrix(*rows, 0, 256) for rows in ((1792, 256), (2048, 128), (2176, 256)))
+    fore_high_f, fore_low_f, back_f = (matrix(*rows, 256, 256) for rows in ((1792, 256), (2048, 128), (2176, 256)))
+    finish_map, spread_map_f = matrix(2432, 256, 0, 256), matrix(2432, 256, 256, 256)
+    place_map, finish_map_f = matrix(2688, 256, 0, 384), matrix(2688, 256, 384, 128)
     turn_xc_c, turn_xs_c, turn_yc_c, turn_ys_c, turn_xc_f, turn_xs_f, turn_yc_f, turn_ys_f = (
         turns.at[pl.ds(start, ROWS), :] for start in range(0, 8 * ROWS, ROWS)
     )
@@ -207,22 +251,24 @@
     def block(position):
         return pl.ds(pl.multiple_of(position * 8, 8), 8)
 
+    at_y, at_z, at_x = lax.axis_index("py"), lax.axis_index("pz") // 4, lax.axis_index("pz") % 4
+    spots_y = [(at_y + step) % 4 for step in range(4)]
+    spots_z = [(at_z + step) % 2 for step in range(2)]
+    spots_x = [(at_x + step) % 4 for step in range(4)]
+
     def post(source, target, sent, got, time_rank, first):
-        def one(step, carry):
-            position = (place + step) % GROUP
+        for step_y, step_z, step_x in OFFSETS[: GROUP - first]:
+            spot_y, spot_pz = spots_y[step_y], spots_z[step_z] * 4 + spots_x[step_x]
             pltpu.make_async_remote_copy(
-                src_ref=source.at[block(position)],
+                src_ref=source.at[block(spot_y * 8 + spot_pz)],
                 dst_ref=target.at[block(place)],
                 send_sem=sent,
                 recv_sem=got,
-                device_id=device(time_rank, position),
+                device_id=(time_rank, spot_y, spot_pz),
                 device_id_type=MESH,
             ).start()
-            return carry
-
         if first == 1:
             pltpu.make_async_copy(source.at[block(place)], target.at[block(place)], got).start()
-        lax.fori_loop(first, GROUP, one, 0)
 
     def receive(target, got):
         pltpu.make_async_copy(target, target, got).wait()
@@ -250,8 +296,8 @@
     mode_x = (lane % 8).astype(F32) * GROUP + place_f32
     mode_y = (row - 256 * ((lane % 16) // 8)).astype(F32)
     wave_x, wave_y, wave_sq, mask, inverse, damp = wave_tables(EDGE // 2, mode_x, mode_y)
-    curl_one[...] = jnp.where(slot == 1, -wave_x, jnp.where(slot == 2, wave_x, wave_y))
-    curl_two[...] = jnp.where(slot == 2, -wave_y, 0.0)
+    curl_one[...] = wave_y
+    curl_two[...] = wave_x
     same = jnp.where(slot == 2, mask, jnp.where(slot == 1, wave_x * wave_x, wave_y * wave_y) * inverse)
     keep_same[...] = same * (HALF_STEP * damp)
     keep_cross[...] = jnp.where(slot == 2, 0.0, -wave_x * wave_y * inverse) * (HALF_STEP * damp)
@@ -279,12 +325,16 @@
                     pieces.append(ref[pl.ds(start, 16, stride=24), :])
             target[pl.ds(half * 128, 128), tile(component)] = jnp.concatenate(pieces, axis=0).T
 
-    def y_product(count, target):
-        for start in range(0, count * LANES, 256):
-            width = min(256, count * LANES - start)
-            part = pl.ds(start, width)
-            high, low = rhs_high[:, part], rhs_low[:, part]
-            target[:, part] = dot(y_high[...], high) + dot(y_high[...], low) + dot(y_low[...], high)
+    def y_product(first, count, target):
+        part = pl.ds(first * LANES, count * LANES)
+        high, low = rhs_high[:, part], rhs_low[:, part]
+        target[...] = dot(y_high[...], high) + dot(y_high[...], low) + dot(y_low[...], high)
+
+    def pair(high, low):
+        return jnp.concatenate([high, low], axis=1)
+
+    def twisted(rows, index, value, value_turned, cosine, sine):
+        stack(rows, index, value * cosine + value_turned * sine, value_turned * cosine - value * sine)
 
     def stack(rows, index, first, second):
         high, low = split(first)
@@ -296,75 +346,55 @@
         rhs_low[lower, tile(index)] = low
 
     def spread_coarse(source, target):
-        for rows in chunks(64):
+        for rows in chunks(128):
             velocity = source[rows, :]
-            rotated = turned(velocity)
-            back_two, back_one, ahead = roll(rotated, -32), roll(rotated, -16), roll(rotated, 16)
-            position = (lanes_like(velocity) % 64) // 16
-            chosen = jnp.where(position == 0, back_two, jnp.where(position == 1, back_one, ahead))
-            vorticity = curl_one[rows, :] * chosen + curl_two[rows, :] * back_one
-            for index, field in enumerate((velocity, vorticity)):
-                mixed = butterfly(field, 8)
-                mixed_turned = turned(mixed)
-                cosine, sine = cos_c[rows, :], sin_c[rows, :]
-                stack(
-                    rows,
-                    index,
-                    mixed * cosine + mixed_turned * sine,
-                    mixed_turned * cosine - mixed * sine,
-                )
-        y_product(2, target)
-
-    def grid_stage(source, count, target, fore_high, fore_low, back, cosine_ref, sine_ref):
-        cosine, sine = cosine_ref[...], sine_ref[...]
+            high_y, low_y = split(velocity * curl_one[rows, :])
+            high_x, low_x = split(velocity * curl_two[rows, :])
+            mixed = dot(pair(*split(velocity)), spread_map[...])
+            curled = dot(pair(high_y, high_x), curl_map[...]) + dot(pair(low_y, low_x), curl_map[...])
+            cosine, sine = cos_c[rows, :], sin_c[rows, :]
+            twisted(rows, 0, mixed[:, :LANES], mixed[:, LANES:], cosine, sine)
+            twisted(rows, 1, curled[:, LANES:], -curled[:, :LANES], cosine, sine)
+        y_product(0, 2, target)
+
+    def to_grid(source, first, fore_high, fore_low, cosine, sine):
         every = pl.ds(0, ROWS)
-        for index in range(count):
+        for index in range(2):
             high, low = split(source[:, tile(index)])
-            inner = dot(jnp.concatenate([high, low], axis=1), fore_high[...]) + dot(high, fore_low[...])
+            inner = dot(pair(high, low), fore_high[...]) + dot(high, fore_low[...])
             real, imag = inner[:, :LANES], inner[:, LANES:]
-            stack(every, index, real * cosine - imag * sine, real * sine + imag * cosine)
-        for start in range(0, count * LANES, 256):
-            part = pl.ds(start, 256)
-            high, low = rhs_high[:, part], rhs_low[:, part]
-            grid_buf[:, part] = dot(x_high[...], high) + dot(x_high[...], low) + dot(x_low[...], high)
-        if count == 2:
-            speed, spin = grid_buf[:, tile(0)], grid_buf[:, tile(1)]
-            crossed = [speed * roll(spin, -32) - roll(speed, -32) * spin]
-        else:
-            fields = [grid_buf[:, tile(index)] for index in range(6)]
-            crossed = [
-                fields[1] * fields[5] - fields[2] * fields[4],
-                fields[2] * fields[3] - fields[0] * fields[5],
-                fields[0] * fields[4] - fields[1] * fields[3],
-            ]
-        for index, value in enumerate(crossed):
-            high, low = split(value)
-            both = dot(xt_high[...], jnp.concatenate([high, low], axis=1))
-            outer = both[:, :LANES] + both[:, LANES:] + dot(xt_low[...], high)
-            real, imag = outer[:ROWS], outer[ROWS:]
-            ready = jnp.concatenate([real * cosine + imag * sine, imag * cosine - real * sine], axis=1)
-            high, low = split(ready)
-            both = dot(high, back[...])
-            target[:, tile(index)] = both[:, :LANES] + both[:, LANES:] + dot(low, back[:, :LANES])
-
-    def gather_y(source, count):
-        for index in range(count):
-            for rows in chunks(128):
-                value = source[rows, tile(index)]
-                stack(rows, index, value, -turned(value))
-        y_product(count, grid_buf)
-
-    def finish_coarse(start_ref, right_ref, target):
-        gather_y(back_recv.at[0] if start_ref is begin else back_recv.at[1], 1)
+            stack(every, first + index, real * cosine - imag * sine, real * sine + imag * cosine)
+        part = pl.ds(first * LANES, 2 * LANES)
+        high, low = rhs_high[:, part], rhs_low[:, part]
+        grid_buf[:, part] = dot(x_high[...], high) + dot(x_high[...], low) + dot(x_low[...], high)
+
+    def from_grid(value, target, back, cosine, sine):
+        high, low = split(value)
+        both = dot(xt_high[...], pair(high, low))
+        outer = both[:, :LANES] + both[:, LANES:] + dot(xt_low[...], high)
+        real, imag = outer[:ROWS], outer[ROWS:]
+        high, low = split(pair(real * cosine + imag * sine, imag * cosine - real * sine))
+        both = dot(high, back[...])
+        target[...] = both[:, :LANES] + both[:, LANES:] + dot(low, back[:, :LANES])
+
+    def grid_coarse(source, target):
+        cosine, sine = turn_xc_c[...], turn_xs_c[...]
+        to_grid(source, 0, fore_high_c, fore_low_c, cosine, sine)
+        speed, spin = grid_buf[:, tile(0)], grid_buf[:, tile(1)]
+        crossed = speed * roll(spin, -32) - roll(speed, -32) * spin
+        from_grid(crossed, target, back_c, cosine, sine)
+
+    def finish_coarse(source, start_ref, right_ref, target):
         for rows in chunks(128):
-            value = grid_buf[rows, tile(0)]
-            value = value * turn_yc_c[rows, :] - turned(value) * turn_ys_c[rows, :]
-            value = butterfly(value, 8)
-            position = (lanes_like(value) % 64) // 16
-            partner = jnp.where(
-                position == 0, roll(value, -16), jnp.where(position == 1, roll(value, 16), roll(value, 32))
-            )
-            term = keep_same[rows, :] * value + keep_cross[rows, :] * partner
+            value = source[rows, :]
+            other = turned(value)
+            stack(rows, 0, value, -other)
+            stack(rows, 1, other, value)
+        y_product(0, 2, grid_buf.at[:, pl.ds(0, 2 * LANES)])
+        for rows in chunks(128):
+            value = grid_buf[rows, tile(0)] * turn_yc_c[rows, :] - grid_buf[rows, tile(1)] * turn_ys_c[rows, :]
+            modes = dot(pair(*split(value)), finish_map[...])
+            term = keep_same[rows, :] * modes[:, :LANES] + keep_cross[rows, :] * modes[:, LANES:]
             target[rows, :] = damp_c[rows, :] * start_ref[rows, :] + right_ref[rows, :] + term
 
     loads[0].wait()
@@ -426,9 +456,8 @@
     coarse_tile(right_one, 0, 0.5, pre_one)
     pre_one[...] = pre_one[...] * damp_c[...]
 
-    coarse_tables = (fore_high_c, fore_low_c, back_c, turn_xc_c, turn_xs_c)
     receive(fore_recv.at[0], fore_got.at[0])
-    grid_stage(fore_recv.at[0], 2, back_send.at[0], *coarse_tables)
+    grid_coarse(fore_recv.at[0], back_send.at[0])
     post(back_send.at[0], back_recv.at[0], back_sent.at[0], back_got.at[0], rank, 1)
 
     @pl.when(rank > 0)
@@ -439,14 +468,14 @@
     coarse_tile(right_two, 0, 0.5, pre_two)
     pre_two[...] = pre_two[...] * damp_c[...]
     receive(back_recv.at[0], back_got.at[0])
-    finish_coarse(begin, pre_one, node_c)
+    finish_coarse(back_recv.at[0], begin, pre_one, node_c)
     spread_coarse(node_c, fore_send.at[1])
     post(fore_send.at[1], fore_recv.at[1], fore_sent.at[1], fore_got.at[1], rank, 1)
 
     coarse_tile(mix_one, 0, 0.5, old_one)
     coarse_tile(mix_two, 0, 0.5, old_two)
     receive(fore_recv.at[1], fore_got.at[1])
-    grid_stage(fore_recv.at[1], 2, back_send.at[1], *coarse_tables)
+    grid_coarse(fore_recv.at[1], back_send.at[1])
     post(back_send.at[1], back_recv.at[1], back_sent.at[1], back_got.at[1], rank, 1)
 
     quarter = (lane % 64) // 16
@@ -465,7 +494,7 @@
     sin_f[...] = turn_ys_f[...] * weight
 
     receive(back_recv.at[1], back_got.at[1])
-    finish_coarse(node_c, pre_two, hand_send)
+    finish_coarse(back_recv.at[1], node_c, pre_two, hand_send)
 
     @pl.when(rank < 3)
     def _():
@@ -494,44 +523,47 @@
         fine_tile(right_one, component, right_one_f)
         fine_tile(right_two, component, right_two_f)
 
-    def spread_fine():
-        for rows in chunks(64):
+    def correct_fine():
+        for rows in chunks(128):
             news = [begin[rows, :], node_c[rows, :], hand_send[rows, :]]
             change_one = sum(w * n for w, n in zip(STATE_ONE, news)) - old_one[rows, :]
             change_two = sum(w * n for w, n in zip(STATE_TWO, news)) - old_two[rows, :]
-            inner = lanes_like(change_one) % 64
+            placed_one = dot(pair(*split(change_one)), place_map[...])
+            placed_two = dot(pair(*split(change_two)), place_map[...])
             stiff, damping = stiff_f[rows, :], damp_f[rows, :]
-            fields = []
             for component in range(3):
-
-                def placed(change):
-                    low = jnp.where(inner < 8, roll(change, -16 * component), 0.0)
-                    high = roll(change, 40 - 16 * component)
-                    return jnp.where((inner >= 48) & (inner < 56), high, low)
-
-                value = right_one_f[rows, tile(component)] + stiff * placed(change_one)
-                value = value * damping
-                node_f[rows, tile(component)] = value
-                right_two_f[rows, tile(component)] = right_two_f[rows, tile(component)] + stiff * placed(change_two)
-                fields.append(value)
-            rotated = [turned(value) for value in fields]
-            ky = ky_f[rows, :]
-            kx = UNIT * ((lanes_like(ky) % 16).astype(F32) * GROUP + place_f32)
-            fields += [ky * rotated[2], -kx * rotated[2], kx * rotated[1] - ky * rotated[0]]
-            position = (lanes_like(ky) % 64) // 16
+                part = tile(component)
+                lanes = slice(component * LANES, (component + 1) * LANES)
+                node_f[rows, part] = (right_one_f[rows, part] + stiff * placed_one[:, lanes]) * damping
+                right_two_f[rows, part] = right_two_f[rows, part] + stiff * placed_two[:, lanes]
+
+    def fine_field(index, rows):
+        x, y, z = (node_f.at[rows, tile(component)] for component in range(3))
+        if index < 3:
+            return (x, y, z)[index][...]
+        ky = ky_f[rows, :]
+        kx = UNIT * ((lanes_like(ky) % 16).astype(F32) * GROUP + place_f32)
+        if index == 3:
+            return ky * z[...]
+        if index == 4:
+            return -kx * z[...]
+        return kx * y[...] - ky * x[...]
+
+    def spread_fine(first):
+        for rows in chunks(128):
             cosine, sine = cos_f[rows, :], sin_f[rows, :]
-            for index, field in enumerate(fields):
-                mixed = butterfly(field, 32)
-                mixed = jnp.where(position == 3, turned(mixed), mixed)
-                mixed = butterfly(mixed, 16)
-                mixed_turned = turned(mixed)
-                stack(
-                    rows, index, mixed * cosine + mixed_turned * sine, mixed_turned * cosine - mixed * sine
-                )
-
-    spread_fine()
-    y_product(6, fine_send)
-    post(fine_send, fine_recv, fine_sems.at[0], fine_sems.at[1], rank, 1)
+            for index in (first, first + 1):
+                mixed = dot(pair(*split(fine_field(index, rows))), spread_map_f[...])
+                if index < 3:
+                    twisted(rows, index, mixed[:, :LANES], mixed[:, LANES:], cosine, sine)
+                else:
+                    twisted(rows, index, mixed[:, LANES:], -mixed[:, :LANES], cosine, sine)
+        y_product(first, 2, fine_send.at[first // 2])
+
+    correct_fine()
+    for part in range(3):
+        spread_fine(2 * part)
+        post(fine_send.at[part], fine_recv.at[part], fine_sent.at[part], fine_got.at[part], rank, 1)
 
     def give_back(source, component, target, base):
         for half in range(2):
@@ -554,26 +586,40 @@
 
     give_back_coarse(node_c, 0)
     give_back_coarse(hand_send, 192)
-    receive(fine_recv, fine_sems.at[1])
-    grid_stage(
-        fine_recv, 6, fine_back_send, fore_high_f, fore_low_f, back_f, turn_xc_f, turn_xs_f
-    )
-    post(fine_back_send, fine_back_recv, fine_sems.at[2], fine_sems.at[3], rank, 1)
+    def cross_fine(component):
+        second, third = (component + 1) % 3, (component + 2) % 3
+        fields = [grid_buf[:, tile(index)] for index in (second, third, second + 3, third + 3)]
+        return fields[0] * fields[3] - fields[1] * fields[2]
+
+    for part in range(3):
+        receive(fine_recv.at[part], fine_got.at[part])
+        to_grid(fine_recv.at[part], 2 * part, fore_high_f, fore_low_f, turn_xc_f[...], turn_xs_f[...])
+    for part in range(3):
+        from_grid(cross_fine(part), fine_back_send.at[part], back_f, turn_xc_f[...], turn_xs_f[...])
+        post(
+            fine_back_send.at[part],
+            fine_back_recv.at[part],
+            fine_back_sent.at[part],
+            fine_back_got.at[part],
+            rank,
+            1,
+        )
     for component in range(3):
         give_back(node_f, component, nodes_out, 0)
-    receive(fine_back_recv, fine_sems.at[3])
-    gather_y(fine_back_recv, 3)
+
+    def gather_fine(component):
+        for rows in chunks(128):
+            value = fine_back_recv[component, rows, :]
+            stack(rows, component, value, -turned(value))
+        y_product(component, 1, grid_buf.at[:, tile(component)])
+        for rows in chunks(128):
+            value = grid_buf[rows, tile(component)]
+            value = value * turn_yc_f[rows, :] - turned(value) * turn_ys_f[rows, :]
+            right_one_f[rows, tile(component)] = dot(pair(*split(value)), finish_map_f[...])
+
     def finish_fine():
         for rows in chunks(64):
-            cosine, sine = turn_yc_f[rows, :], turn_ys_f[rows, :]
-            modes = []
-            for component in range(3):
-                value = grid_buf[rows, tile(component)]
-                value = value * cosine - turned(value) * sine
-                value = butterfly(value, 16)
-                position = (lanes_like(value) % 64) // 16
-                value = jnp.where(position == 3, -turned(value), value)
-                modes.append(butterfly(value, 32))
+            modes = [right_one_f[rows, tile(component)] for component in range(3)]
             cross = cross_f[rows, :]
             results = [
                 same_x[rows, :] * modes[0] + cross * modes[1],
@@ -586,6 +632,9 @@
                 total = node_f[rows, part] + HALF_STEP * value + right_two_f[rows, part]
                 node_f[rows, part] = total * damp_f[rows, :]
 
+    for part in range(3):
+        receive(fine_back_recv.at[part], fine_back_got.at[part])
+        gather_fine(part)
     finish_fine()
     for component in range(3):
         give_back(right_one_f, component, term_out, 0)
@@ -598,8 +647,9 @@
     drain(fore_send.at[1], fore_sent.at[1], 1)
     for index in range(2):
         drain(back_send.at[index], back_sent.at[index], 1)
-    drain(fine_send, fine_sems.at[0], 1)
-    drain(fine_back_send, fine_sems.at[2], 1)
+    for part in range(3):
+        drain(fine_send.at[part], fine_sent.at[part], 1)
+        drain(fine_back_send.at[part], fine_back_sent.at[part], 1)
 
     @pl.when(rank < 3)
     def _():
@@ -616,25 +666,23 @@
         pltpu.VMEM((2 * ROWS, 6 * LANES), BF16),
         pltpu.VMEM((2 * ROWS, 6 * LANES), BF16),
         pltpu.VMEM((ROWS, 6 * LANES), F32),
-        pltpu.VMEM(wide, BF16),
-        pltpu.VMEM(wide, BF16),
         pltpu.VMEM((3, ROWS, 2 * LANES), F32),
         pltpu.VMEM((2, ROWS, 2 * LANES), F32),
         pltpu.VMEM((2, ROWS, LANES), F32),
         pltpu.VMEM((2, ROWS, LANES), F32),
         pltpu.VMEM(full, F32),
         pltpu.VMEM(full, F32),
-        pltpu.VMEM((ROWS, 6 * LANES), F32),
-        pltpu.VMEM((ROWS, 6 * LANES), F32),
-        pltpu.VMEM(wide, F32),
-        pltpu.VMEM(wide, F32),
+        pltpu.VMEM((3, ROWS, 2 * LANES), F32),
+        pltpu.VMEM((3, ROWS, 2 * LANES), F32),
+        pltpu.VMEM((3, ROWS, LANES), F32),
+        pltpu.VMEM((3, ROWS, LANES), F32),
     ]
     scratch += [pltpu.VMEM(natural, F32)] * 6
     scratch += [pltpu.VMEM(full, F32)] * (7 + 6 + 9)
     scratch += [pltpu.VMEM(wide, F32)] * 3
     scratch += [pltpu.VMEM((2304, LANES), F32)] * 2
     scratch += [pltpu.VMEM(matrices.shape, BF16), pltpu.VMEM(turns.shape, F32)]
-    scratch += [dma((count,)) for count in (3, 2, 2, 2, 2, 4, 2, 7)]
+    scratch += [dma((count,)) for count in (3, 2, 2, 2, 2, 3, 3, 3, 3, 2, 7)]
     outs = pl.pallas_call(
         iterate,
         out_shape=(

time: 160 us -> 146 us (0.912)
  Pallas kernels: 155 us -> 141 us
    pallas_call x1, Pallas kernels: 155 us -> 141 us  [shards(): pl.pallas_call(iterate, out_shape=(jax.ShapeDtypeStruct((1536, LANES), F3...]
where the time goes in v3:
time: 146 us
  Pallas kernels  141 us (97%)
  local copies, waits for them, and re-layouts  4.04 us (3%)
    pallas_call x1, Pallas kernels, shards(): pl.pallas_call(iterate, out_shape=(jax.ShapeDtypeStruct((1536, LANES), F3...  141 us
    unnamed x7, local copies, waits for them, and re-layouts  4.04 us

profile of v3, /device:TPU:33, one launch (start us, length us, event | category | flops | bytes accessed | tf_op | source)
XLA Modules:
  0.0 145.8 jit_solution(11344035508617074030)
XLA Ops:
  0.6 141.1 %iterate.1 = (f32[1536,128]{1,0:T(8,128)}, f32[768,128]{1,0:T(8,128)}, f32[384,128]{1,0:T(8,128)}) custom-call(f32[2304,128]{1,0:T(8,128)} %bitcast.5, f32[2304,128]{1,0:T(8,128)} %bitcast.6, bf16[2944,512]{1,0:T(8,128)(2,1)} %constant.4.clone.matrices_hbm, f32[2048,128]{1,0:T(8,128)} %constant.5.clone.turns_hbm), custom_call_target="tpu_custom_call" | custom-call | tf_op jit(solution)/shard_map/iterate/pallas_call | solution.py:686
  141.7 0.0 copy-start
  141.8 0.0 copy-start.1
  141.8 2.6 %copy.16 = f32[1,2,2,16,1,3,1,1024]{7,6,5,4,3,2,1,0:T(1,128)} copy(f32[1,2,2,16,1,3,1,1024]{7,6,5,4,3,2,1,0:T(1,128)} %bitcast.7) | data formatting | bytes 1572864
  144.4 0.0 copy-done
  144.4 0.7 copy.17
  145.1 0.0 copy-done.1
  145.1 0.7 copy.18
Async XLA Ops:
  141.7 2.6 %copy-start = (f32[768,128]{1,0:T(8,128)S(1)}, f32[768,128]{1,0:T(8,128)}, u32[]{:S(2)}) copy-start(f32[768,128]{1,0:T(8,128)} %get-tuple-element.7) | copy-start | bytes 1179652
  141.8 3.4 %copy-start.1 = (f32[384,128]{1,0:T(8,128)S(1)}, f32[384,128]{1,0:T(8,128)}, u32[]{:S(2)}) copy-start(f32[384,128]{1,0:T(8,128)} %get-tuple-element.8) | copy-start | bytes 589828

commit v4 on v3

--- a/solution.py
+++ b/solution.py
@@ -18,6 +18,7 @@
 GROUP = 32
 ROWS = 256
 LANES = 128
+PIECES = 4
 F32 = jnp.float32
 BF16 = jnp.bfloat16
 MESH = pl.DeviceIdType.MESH
@@ -32,9 +33,12 @@
 
 
 HOPS = (0, 1, 2, 1)
-OFFSETS = sorted(
-    ((y, z, x) for y in range(4) for z in range(2) for x in range(4)),
-    key=lambda step: -(HOPS[step[0]] + 2 * step[1] + HOPS[step[2]]),
+DUTY, RANK = (
+    sorted(
+        ((y, z, x) for y in range(4) for z in range(2) for x in range(4)),
+        key=lambda step: -(HOPS[step[0]] + apart * step[1] + HOPS[step[2]]),
+    )
+    for apart in (1, 2)
 )
 
 
@@ -183,16 +187,16 @@
     state_hbm, terms_hbm, matrices_hbm, turns_hbm,
     nodes_out, term_out, coarse_out,
     rhs_high, rhs_low, grid_buf,
-    fore_send, fore_recv, back_send, back_recv, hand_send, hand_recv,
+    fore_send, fore_recv, back_send, back_recv, last_recv, hand_recv,
+    parcel_send, parcel_recv, sweep, news,
     fine_send, fine_recv, fine_back_send, fine_back_recv, start_send, start_recv,
     right_one, right_two, mix_one, mix_two,
-    curl_one, curl_two, keep_same, keep_cross, damp_c, cos_c, sin_c,
-    pre_one, pre_two, old_one, old_two, begin, node_c,
+    curl_y, keep_same, keep_cross, damp_c, keep_same_r, keep_cross_r, damp_r, old_one, old_two,
     ky_f, damp_f, stiff_f, cos_f, sin_f, same_x, same_y, cross_f, mask_f,
     right_one_f, right_two_f, node_f,
     state_ref, terms_ref, matrices, turns,
-    fore_sent, fore_got, back_sent, back_got, hand_sems, fine_sent, fine_got, fine_back_sent, fine_back_got, start_sems,
-    load_sems,
+    fore_sent, fore_got, back_sent, back_got, hand_sems, parcel_sems, news_sent, news_got,
+    fine_sent, fine_got, fine_back_sent, fine_back_got, start_sems, load_sems,
 ):
     loads = []
     for source, target, start, size in (
@@ -223,61 +227,109 @@
         turns.at[pl.ds(start, ROWS), :] for start in range(0, 8 * ROWS, ROWS)
     )
     rank = lax.axis_index("tm")
-    place = lax.axis_index("py") * 8 + lax.axis_index("pz")
-
-    def device(time_rank, position):
-        return (time_rank, position // 8, position % 8)
+    at_y, at_pz = lax.axis_index("py"), lax.axis_index("pz")
+    low_z, core, high_z, at_x = rank // 2, rank % 2, at_pz // 4, at_pz % 4
+    place = at_y * 8 + at_pz
+    duty = high_z * 2 + core
+    spot = at_y * 8 + low_z * 4 + at_x
+    alone = high_z == low_z
+    partner = (duty, at_y, low_z * 4 + at_x)
 
     barrier = pltpu.get_barrier_semaphore()
-
-    @pl.when(rank > 0)
-    def _():
-        def greet_back(step, carry):
-            pl.semaphore_signal(
-                barrier, inc=1, device_id=device(rank - 1, (place + step) % GROUP), device_id_type=MESH
-            )
-            return carry
-
-        lax.fori_loop(0, GROUP, greet_back, 0)
+    number = rank * GROUP + place
 
     def greet(step, carry):
-        pl.semaphore_signal(
-            barrier, inc=1, device_id=device(rank, (place + step) % GROUP), device_id_type=MESH
-        )
+        other = (number + step) % (4 * GROUP)
+        target = (other // GROUP, (other // 8) % 4, other % 8)
+        pl.semaphore_signal(barrier, inc=1, device_id=target, device_id_type=MESH)
         return carry
 
-    lax.fori_loop(1, GROUP, greet, 0)
+    lax.fori_loop(1, 4 * GROUP, greet, 0)
 
     def block(position):
         return pl.ds(pl.multiple_of(position * 8, 8), 8)
 
-    at_y, at_z, at_x = lax.axis_index("py"), lax.axis_index("pz") // 4, lax.axis_index("pz") % 4
     spots_y = [(at_y + step) % 4 for step in range(4)]
-    spots_z = [(at_z + step) % 2 for step in range(2)]
     spots_x = [(at_x + step) % 4 for step in range(4)]
-
-    def post(source, target, sent, got, time_rank, first):
-        for step_y, step_z, step_x in OFFSETS[: GROUP - first]:
-            spot_y, spot_pz = spots_y[step_y], spots_z[step_z] * 4 + spots_x[step_x]
+    duty_z = [(low_z + step) % 2 for step in range(2)]
+    rank_z = [(high_z + step) % 2 for step in range(2)]
+
+    def spot_of(steps, step):
+        spot_y, spot_x = spots_y[step[0]], spots_x[step[2]]
+        if steps is DUTY:
+            spot_z = duty_z[step[1]]
+            address = lambda group: (spot_z * 2 + group % 2, spot_y, (group // 2) * 4 + spot_x)
+        else:
+            spot_z = rank_z[step[1]]
+            address = lambda group: (group, spot_y, spot_z * 4 + spot_x)
+        return spot_y * 8 + spot_z * 4 + spot_x, address
+
+    def post(source, target, sent, got, steps, group, mine, count):
+        for step in steps[:count]:
+            index, address = spot_of(steps, step)
             pltpu.make_async_remote_copy(
-                src_ref=source.at[block(spot_y * 8 + spot_pz)],
-                dst_ref=target.at[block(place)],
+                src_ref=source.at[block(index)],
+                dst_ref=target.at[block(mine)],
                 send_sem=sent,
                 recv_sem=got,
-                device_id=(time_rank, spot_y, spot_pz),
+                device_id=address(group),
                 device_id_type=MESH,
             ).start()
-        if first == 1:
-            pltpu.make_async_copy(source.at[block(place)], target.at[block(place)], got).start()
+
+    def post_own(source, target, sent, got, steps, group, mine):
+        post(source, target, sent, got, steps, group, mine, GROUP - 1)
+        pltpu.make_async_copy(source.at[block(mine)], target.at[block(mine)], got).start()
+
+    def post_other(source, target, sent, got, steps, group, mine):
+        post(source, target, sent, got, steps, group, mine, GROUP - 1)
+        index, address = spot_of(steps, steps[-1])
+
+        @pl.when(alone)
+        def _():
+            pltpu.make_async_copy(source.at[block(index)], target.at[block(mine)], got).start()
+
+        @pl.when(jnp.logical_not(alone))
+        def _():
+            pltpu.make_async_remote_copy(
+                src_ref=source.at[block(index)],
+                dst_ref=target.at[block(mine)],
+                send_sem=sent,
+                recv_sem=got,
+                device_id=address(group),
+                device_id_type=MESH,
+            ).start()
+
+    def send_one(source, target, sent, got, address):
+        return pltpu.make_async_remote_copy(
+            src_ref=source, dst_ref=target, send_sem=sent, recv_sem=got, device_id=address, device_id_type=MESH
+        )
+
+    def to_partner(source, target, sent, got):
+        @pl.when(alone)
+        def _():
+            pltpu.make_async_copy(source, target, got).start()
+
+        @pl.when(jnp.logical_not(alone))
+        def _():
+            send_one(source, target, sent, got, partner).start()
 
     def receive(target, got):
         pltpu.make_async_copy(target, target, got).wait()
 
-    def drain(source, sent, first):
-        part = source.at[pl.ds(0, (GROUP - first) * 8)]
+    def drain(source, sent, count):
+        part = source.at[pl.ds(0, count * 8)]
         pltpu.make_async_copy(part, part, sent).wait()
 
-    place_f32 = place.astype(F32)
+    def drain_other(source, sent):
+        @pl.when(alone)
+        def _():
+            drain(source, sent, GROUP - 1)
+
+        @pl.when(jnp.logical_not(alone))
+        def _():
+            drain(source, sent, GROUP)
+
+    place_f32, spot_f32 = place.astype(F32), spot.astype(F32)
     row = lax.broadcasted_iota(jnp.int32, (ROWS, LANES), 0)
     lane = lax.broadcasted_iota(jnp.int32, (ROWS, LANES), 1)
 
@@ -291,20 +343,17 @@
         damp = 1.0 / (1.0 + HALF_STEP * VISCOSITY * wave_sq)
         return wave_x, wave_y, wave_sq, mask, inverse, damp
 
-    loads[2].wait()
-    slot = (lane % 64) // 16
-    mode_x = (lane % 8).astype(F32) * GROUP + place_f32
-    mode_y = (row - 256 * ((lane % 16) // 8)).astype(F32)
-    wave_x, wave_y, wave_sq, mask, inverse, damp = wave_tables(EDGE // 2, mode_x, mode_y)
-    curl_one[...] = wave_y
-    curl_two[...] = wave_x
-    same = jnp.where(slot == 2, mask, jnp.where(slot == 1, wave_x * wave_x, wave_y * wave_y) * inverse)
-    keep_same[...] = same * (HALF_STEP * damp)
-    keep_cross[...] = jnp.where(slot == 2, 0.0, -wave_x * wave_y * inverse) * (HALF_STEP * damp)
-    damp_c[...] = damp
-    weight = jnp.where(mode_x == 0, 0.5, 1.0)
-    cos_c[...] = turn_yc_c[...] * weight
-    sin_c[...] = turn_ys_c[...] * weight
+    def coarse_tables(position, same_ref, cross_ref, damp_ref):
+        slot = (lane % 64) // 16
+        mode_x = (lane % 8).astype(F32) * GROUP + position
+        mode_y = (row - 256 * ((lane % 16) // 8)).astype(F32)
+        wave_x, wave_y, wave_sq, mask, inverse, damp = wave_tables(EDGE // 2, mode_x, mode_y)
+        same = jnp.where(slot == 2, mask, jnp.where(slot == 1, wave_x * wave_x, wave_y * wave_y) * inverse)
+        same_ref[...] = same * (HALF_STEP * damp)
+        cross_ref[...] = jnp.where(slot == 2, 0.0, -wave_x * wave_y * inverse) * (HALF_STEP * damp)
+        damp_ref[...] = damp
+
+    curl_y[...] = UNIT * (row - 256 * ((lane % 16) // 8)).astype(F32)
 
     def coarse_tile(ref, base, scale, target):
         for half in range(2):
@@ -345,14 +394,17 @@
         rhs_high[lower, tile(index)] = high
         rhs_low[lower, tile(index)] = low
 
-    def spread_coarse(source, target):
+    def spread_coarse(source, target, position):
+        lanes = lax.broadcasted_iota(jnp.int32, (1, LANES), 1) % 8
+        mode_x = lanes.astype(F32) * GROUP + position
+        weight = jnp.where(mode_x == 0, 0.5, 1.0)
         for rows in chunks(128):
-            velocity = source[rows, :]
-            high_y, low_y = split(velocity * curl_one[rows, :])
-            high_x, low_x = split(velocity * curl_two[rows, :])
+            velocity = source[rows, :] * weight
+            high_y, low_y = split(velocity * curl_y[rows, :])
+            high_x, low_x = split(velocity * (UNIT * mode_x))
             mixed = dot(pair(*split(velocity)), spread_map[...])
             curled = dot(pair(high_y, high_x), curl_map[...]) + dot(pair(low_y, low_x), curl_map[...])
-            cosine, sine = cos_c[rows, :], sin_c[rows, :]
+            cosine, sine = turn_yc_c[rows, :], turn_ys_c[rows, :]
             twisted(rows, 0, mixed[:, :LANES], mixed[:, LANES:], cosine, sine)
             twisted(rows, 1, curled[:, LANES:], -curled[:, :LANES], cosine, sine)
         y_product(0, 2, target)
@@ -384,7 +436,7 @@
         crossed = speed * roll(spin, -32) - roll(speed, -32) * spin
         from_grid(crossed, target, back_c, cosine, sine)
 
-    def finish_coarse(source, start_ref, right_ref, target):
+    def finish_coarse(source, start_ref, right_ref, target, same_ref, cross_ref, damp_ref):
         for rows in chunks(128):
             value = source[rows, :]
             other = turned(value)
@@ -394,28 +446,23 @@
         for rows in chunks(128):
             value = grid_buf[rows, tile(0)] * turn_yc_c[rows, :] - grid_buf[rows, tile(1)] * turn_ys_c[rows, :]
             modes = dot(pair(*split(value)), finish_map[...])
-            term = keep_same[rows, :] * modes[:, :LANES] + keep_cross[rows, :] * modes[:, LANES:]
-            target[rows, :] = damp_c[rows, :] * start_ref[rows, :] + right_ref[rows, :] + term
+            term = same_ref[rows, :] * modes[:, :LANES] + cross_ref[rows, :] * modes[:, LANES:]
+            target[rows, :] = damp_ref[rows, :] * (start_ref[rows, :] + right_ref[rows, :]) + term
 
     loads[0].wait()
-    coarse_tile(state_ref, 0, 0.5, begin)
+    coarse_tile(state_ref, 0, 0.5, parcel_send.at[0])
     loads[1].wait()
+    loads[2].wait()
 
     @pl.when(rank == 0)
     def _():
-        spread_coarse(begin, fore_send.at[0])
-
-    @pl.when(rank < 3)
-    def _():
-        pl.semaphore_wait(barrier, 2 * GROUP - 1)
-
-    @pl.when(rank == 3)
-    def _():
-        pl.semaphore_wait(barrier, GROUP - 1)
+        spread_coarse(parcel_send.at[0], fore_send.at[0], place_f32)
+
+    pl.semaphore_wait(barrier, 4 * GROUP - 1)
 
     @pl.when(rank == 0)
     def _():
-        post(fore_send.at[0], fore_recv.at[0], fore_sent.at[0], fore_got.at[0], rank, 1)
+        post_other(fore_send.at[0], fore_recv.at[0], fore_sent.at[0], fore_got.at[0], DUTY, 0, place)
 
     def combine(a, carry):
         wave_x = UNIT * (a.astype(F32) * GROUP + place_f32)
@@ -442,42 +489,59 @@
         loads[index].wait()
     lax.fori_loop(0, 16, combine, 0, unroll=2)
 
+    following = (rank + 1, at_y, at_pz)
+
     @pl.when(rank < 3)
     def _():
-        pltpu.make_async_remote_copy(
-            src_ref=start_send,
-            dst_ref=start_recv,
-            send_sem=start_sems.at[0],
-            recv_sem=start_sems.at[1],
-            device_id=device(rank + 1, place),
-            device_id_type=MESH,
-        ).start()
-
-    coarse_tile(right_one, 0, 0.5, pre_one)
-    pre_one[...] = pre_one[...] * damp_c[...]
-
-    receive(fore_recv.at[0], fore_got.at[0])
-    grid_coarse(fore_recv.at[0], back_send.at[0])
-    post(back_send.at[0], back_recv.at[0], back_sent.at[0], back_got.at[0], rank, 1)
-
-    @pl.when(rank > 0)
-    def _():
-        pltpu.make_async_copy(hand_recv, hand_recv, hand_sems.at[1]).wait()
-        begin[...] = hand_recv[...]
-
-    coarse_tile(right_two, 0, 0.5, pre_two)
-    pre_two[...] = pre_two[...] * damp_c[...]
-    receive(back_recv.at[0], back_got.at[0])
-    finish_coarse(back_recv.at[0], begin, pre_one, node_c)
-    spread_coarse(node_c, fore_send.at[1])
-    post(fore_send.at[1], fore_recv.at[1], fore_sent.at[1], fore_got.at[1], rank, 1)
+        send_one(start_send, start_recv, start_sems.at[0], start_sems.at[1], following).start()
+
+    coarse_tile(right_one, 0, 0.5, parcel_send.at[1])
+    coarse_tile(right_two, 0, 0.5, parcel_send.at[2])
+    to_partner(parcel_send, parcel_recv, parcel_sems.at[0], parcel_sems.at[1])
+    coarse_tables(spot_f32, keep_same, keep_cross, damp_c)
+
+    def coarse_sweep():
+        receive(fore_recv.at[0], fore_got.at[0])
+        grid_coarse(fore_recv.at[0], back_send.at[0])
+        post_own(back_send.at[0], back_recv.at[0], back_sent.at[0], back_got.at[0], DUTY, duty, spot)
+        receive(parcel_recv, parcel_sems.at[1])
+
+        @pl.when(duty == 0)
+        def _():
+            sweep[0] = parcel_recv[0]
+
+        @pl.when(duty > 0)
+        def _():
+            receive(hand_recv, hand_sems.at[1])
+            sweep[0] = hand_recv[...]
+
+        receive(back_recv.at[0], back_got.at[0])
+        tables = (keep_same, keep_cross, damp_c)
+        finish_coarse(back_recv.at[0], sweep.at[0], parcel_recv.at[1], sweep.at[1], *tables)
+        spread_coarse(sweep.at[1], fore_send.at[1], spot_f32)
+        post_own(fore_send.at[1], fore_recv.at[1], fore_sent.at[1], fore_got.at[1], DUTY, duty, spot)
+        to_partner(sweep.at[pl.ds(0, 2)], news.at[pl.ds(0, 2)], news_sent.at[0], news_got.at[0])
+        receive(fore_recv.at[1], fore_got.at[1])
+        grid_coarse(fore_recv.at[1], back_send.at[1])
+
+        @pl.when(duty == 3)
+        def _():
+            post_other(back_send.at[1], last_recv, back_sent.at[1], back_got.at[2], RANK, 3, spot)
+
+        @pl.when(duty < 3)
+        def _():
+            post_own(back_send.at[1], back_recv.at[1], back_sent.at[1], back_got.at[1], DUTY, duty, spot)
+            receive(back_recv.at[1], back_got.at[1])
+            finish_coarse(back_recv.at[1], sweep.at[1], parcel_recv.at[2], sweep.at[2], *tables)
+            spread_coarse(sweep.at[2], fore_send.at[2], spot_f32)
+            after = duty + 1
+            post(fore_send.at[2], fore_recv.at[0], fore_sent.at[2], fore_got.at[0], DUTY, after, spot, GROUP)
+            address = (low_z * 2 + after % 2, at_y, (after // 2) * 4 + at_x)
+            send_one(sweep.at[2], hand_recv, hand_sems.at[0], hand_sems.at[1], address).start()
+            to_partner(sweep.at[2], news.at[2], news_sent.at[1], news_got.at[1])
 
     coarse_tile(mix_one, 0, 0.5, old_one)
     coarse_tile(mix_two, 0, 0.5, old_two)
-    receive(fore_recv.at[1], fore_got.at[1])
-    grid_coarse(fore_recv.at[1], back_send.at[1])
-    post(back_send.at[1], back_recv.at[1], back_sent.at[1], back_got.at[1], rank, 1)
-
     quarter = (lane % 64) // 16
     mode_x = (lane % 16).astype(F32) * GROUP + place_f32
     mode_y = (row + 256 * quarter - jnp.where(quarter >= 2, EDGE, 0)).astype(F32)
@@ -493,41 +557,15 @@
     cos_f[...] = turn_yc_f[...] * weight
     sin_f[...] = turn_ys_f[...] * weight
 
-    receive(back_recv.at[1], back_got.at[1])
-    finish_coarse(back_recv.at[1], node_c, pre_two, hand_send)
-
-    @pl.when(rank < 3)
+    @pl.when(rank == 3)
     def _():
-        spread_coarse(hand_send, fore_send.at[2])
-        post(fore_send.at[2], fore_recv.at[0], fore_sent.at[2], fore_got.at[0], rank + 1, 0)
-        pltpu.make_async_remote_copy(
-            src_ref=hand_send,
-            dst_ref=hand_recv,
-            send_sem=hand_sems.at[0],
-            recv_sem=hand_sems.at[1],
-            device_id=device(rank + 1, place),
-            device_id_type=MESH,
-        ).start()
-
-    @pl.when(rank == 0)
-    def _():
-        first = pl.ds(0, 768)
-        right_one[...] = right_one[...] + state_ref[first, :] + HALF_STEP * terms_ref[first, :]
-
-    @pl.when(rank > 0)
-    def _():
-        pltpu.make_async_copy(start_recv, start_recv, start_sems.at[1]).wait()
-        right_one[...] = right_one[...] + start_recv[...]
-
-    for component in range(3):
-        fine_tile(right_one, component, right_one_f)
-        fine_tile(right_two, component, right_two_f)
+        coarse_tables(place_f32, keep_same_r, keep_cross_r, damp_r)
 
     def correct_fine():
         for rows in chunks(128):
-            news = [begin[rows, :], node_c[rows, :], hand_send[rows, :]]
-            change_one = sum(w * n for w, n in zip(STATE_ONE, news)) - old_one[rows, :]
-            change_two = sum(w * n for w, n in zip(STATE_TWO, news)) - old_two[rows, :]
+            nodes = [news[node, rows, :] for node in range(3)]
+            change_one = sum(w * n for w, n in zip(STATE_ONE, nodes)) - old_one[rows, :]
+            change_two = sum(w * n for w, n in zip(STATE_TWO, nodes)) - old_two[rows, :]
             placed_one = dot(pair(*split(change_one)), place_map[...])
             placed_two = dot(pair(*split(change_two)), place_map[...])
             stiff, damping = stiff_f[rows, :], damp_f[rows, :]
@@ -560,11 +598,6 @@
                     twisted(rows, index, mixed[:, LANES:], -mixed[:, :LANES], cosine, sine)
         y_product(first, 2, fine_send.at[first // 2])
 
-    correct_fine()
-    for part in range(3):
-        spread_fine(2 * part)
-        post(fine_send.at[part], fine_recv.at[part], fine_sent.at[part], fine_got.at[part], rank, 1)
-
     def give_back(source, component, target, base):
         for half in range(2):
             block_t = source[pl.ds(half * 128, 128), tile(component)].T
@@ -584,28 +617,10 @@
                         first = part * 64 + component * 16 + quarter * 8
                         coarse_out[pl.ds(start, 8, stride=12), :] = block_t[first : first + 8]
 
-    give_back_coarse(node_c, 0)
-    give_back_coarse(hand_send, 192)
     def cross_fine(component):
         second, third = (component + 1) % 3, (component + 2) % 3
         fields = [grid_buf[:, tile(index)] for index in (second, third, second + 3, third + 3)]
         return fields[0] * fields[3] - fields[1] * fields[2]
-
-    for part in range(3):
-        receive(fine_recv.at[part], fine_got.at[part])
-        to_grid(fine_recv.at[part], 2 * part, fore_high_f, fore_low_f, turn_xc_f[...], turn_xs_f[...])
-    for part in range(3):
-        from_grid(cross_fine(part), fine_back_send.at[part], back_f, turn_xc_f[...], turn_xs_f[...])
-        post(
-            fine_back_send.at[part],
-            fine_back_recv.at[part],
-            fine_back_sent.at[part],
-            fine_back_got.at[part],
-            rank,
-            1,
-        )
-    for component in range(3):
-        give_back(node_f, component, nodes_out, 0)
 
     def gather_fine(component):
         for rows in chunks(128):
@@ -632,57 +647,133 @@
                 total = node_f[rows, part] + HALF_STEP * value + right_two_f[rows, part]
                 node_f[rows, part] = total * damp_f[rows, :]
 
-    for part in range(3):
-        receive(fine_back_recv.at[part], fine_back_got.at[part])
-        gather_fine(part)
-    finish_fine()
-    for component in range(3):
-        give_back(right_one_f, component, term_out, 0)
-        give_back(node_f, component, nodes_out, 768)
+    def fine_sweep():
+        @pl.when(rank == 0)
+        def _():
+            first = pl.ds(0, 768)
+            right_one[...] = right_one[...] + state_ref[first, :] + HALF_STEP * terms_ref[first, :]
+
+        @pl.when(rank > 0)
+        def _():
+            receive(start_recv, start_sems.at[1])
+            right_one[...] = right_one[...] + start_recv[...]
+
+        for component in range(3):
+            fine_tile(right_one, component, right_one_f)
+            fine_tile(right_two, component, right_two_f)
+        receive(news.at[pl.ds(0, 2)], news_got.at[0])
+
+        @pl.when(rank < 3)
+        def _():
+            receive(news.at[2], news_got.at[1])
+
+        @pl.when(rank == 3)
+        def _():
+            receive(last_recv, back_got.at[2])
+            tables = (keep_same_r, keep_cross_r, damp_r)
+            finish_coarse(last_recv, news.at[1], parcel_send.at[2], news.at[2], *tables)
+
+        correct_fine()
+        for part in range(3):
+            spread_fine(2 * part)
+            pairs = (fine_send.at[part], fine_recv.at[part], fine_sent.at[part], fine_got.at[part])
+            post_own(*pairs, RANK, rank, place)
+        give_back_coarse(news.at[1], 0)
+        give_back_coarse(news.at[2], 192)
+        for part in range(3):
+            receive(fine_recv.at[part], fine_got.at[part])
+            to_grid(fine_recv.at[part], 2 * part, fore_high_f, fore_low_f, turn_xc_f[...], turn_xs_f[...])
+        for part in range(3):
+            from_grid(cross_fine(part), fine_back_send.at[part], back_f, turn_xc_f[...], turn_xs_f[...])
+            pairs = (fine_back_send.at[part], fine_back_recv.at[part])
+            post_own(*pairs, fine_back_sent.at[part], fine_back_got.at[part], RANK, rank, place)
+        for component in range(3):
+            give_back(node_f, component, nodes_out, 0)
+        for part in range(3):
+            receive(fine_back_recv.at[part], fine_back_got.at[part])
+            gather_fine(part)
+        finish_fine()
+        for component in range(3):
+            give_back(right_one_f, component, term_out, 0)
+            give_back(node_f, component, nodes_out, 768)
+
+    early = high_z * (1 - low_z)
+
+    def phase(step, carry):
+        fine_now = (step + early) % 2
+
+        @pl.when(fine_now == 0)
+        def _():
+            coarse_sweep()
+
+        @pl.when(fine_now == 1)
+        def _():
+            fine_sweep()
+
+        return carry
+
+    lax.fori_loop(0, 2, phase, 0)
 
     @pl.when(rank == 0)
     def _():
-        drain(fore_send.at[0], fore_sent.at[0], 1)
-
-    drain(fore_send.at[1], fore_sent.at[1], 1)
-    for index in range(2):
-        drain(back_send.at[index], back_sent.at[index], 1)
+        drain_other(fore_send.at[0], fore_sent.at[0])
+
+    drain(fore_send.at[1], fore_sent.at[1], GROUP - 1)
+    drain(back_send.at[0], back_sent.at[0], GROUP - 1)
     for part in range(3):
-        drain(fine_send.at[part], fine_sent.at[part], 1)
-        drain(fine_back_send.at[part], fine_back_sent.at[part], 1)
+        drain(fine_send.at[part], fine_sent.at[part], GROUP - 1)
+        drain(fine_back_send.at[part], fine_back_sent.at[part], GROUP - 1)
+
+    @pl.when(duty == 3)
+    def _():
+        drain_other(back_send.at[1], back_sent.at[1])
+
+    @pl.when(duty < 3)
+    def _():
+        drain(back_send.at[1], back_sent.at[1], GROUP - 1)
+        drain(fore_send.at[2], fore_sent.at[2], GROUP)
+        receive(sweep.at[2], hand_sems.at[0])
+
+    @pl.when(jnp.logical_not(alone))
+    def _():
+        receive(parcel_send, parcel_sems.at[0])
+        receive(sweep.at[pl.ds(0, 2)], news_sent.at[0])
+
+        @pl.when(duty < 3)
+        def _():
+            receive(sweep.at[2], news_sent.at[1])
 
     @pl.when(rank < 3)
     def _():
-        drain(fore_send.at[2], fore_sent.at[2], 0)
-        pltpu.make_async_copy(hand_send, hand_send, hand_sems.at[0]).wait()
-        pltpu.make_async_copy(start_send, start_send, start_sems.at[0]).wait()
+        receive(start_send, start_sems.at[0])
+
+
+def hand_out(*refs):
+    sources, targets, sems = refs[:3], refs[3:6], refs[6]
+    copies = []
+    for source, target in zip(sources, targets):
+        size = source.shape[0] // PIECES
+        for piece in range(PIECES):
+            rows = pl.ds(piece * size, size)
+            copies.append(pltpu.make_async_copy(source.at[rows], target.at[rows], sems.at[len(copies)]))
+    for copy in copies:
+        copy.start()
+    for copy in copies:
+        copy.wait()
 
 
 def shards(fine_state, fine_terms):
     matrices, turns = constant_tables()
     full, natural, wide = (ROWS, LANES), (768, LANES), (ROWS, 3 * LANES)
     dma = pltpu.SemaphoreType.DMA
-    scratch = [
-        pltpu.VMEM((2 * ROWS, 6 * LANES), BF16),
-        pltpu.VMEM((2 * ROWS, 6 * LANES), BF16),
-        pltpu.VMEM((ROWS, 6 * LANES), F32),
-        pltpu.VMEM((3, ROWS, 2 * LANES), F32),
-        pltpu.VMEM((2, ROWS, 2 * LANES), F32),
-        pltpu.VMEM((2, ROWS, LANES), F32),
-        pltpu.VMEM((2, ROWS, LANES), F32),
-        pltpu.VMEM(full, F32),
-        pltpu.VMEM(full, F32),
-        pltpu.VMEM((3, ROWS, 2 * LANES), F32),
-        pltpu.VMEM((3, ROWS, 2 * LANES), F32),
-        pltpu.VMEM((3, ROWS, LANES), F32),
-        pltpu.VMEM((3, ROWS, LANES), F32),
-    ]
-    scratch += [pltpu.VMEM(natural, F32)] * 6
-    scratch += [pltpu.VMEM(full, F32)] * (7 + 6 + 9)
-    scratch += [pltpu.VMEM(wide, F32)] * 3
-    scratch += [pltpu.VMEM((2304, LANES), F32)] * 2
+    tiles = (3, ROWS, LANES)
+    shapes = [(ROWS, 6 * LANES)]
+    shapes += [(3, ROWS, 2 * LANES), (2, ROWS, 2 * LANES), (2, ROWS, LANES), (2, ROWS, LANES), full, full]
+    shapes += [tiles] * 4 + [(3, ROWS, 2 * LANES)] * 2 + [tiles] * 2
+    shapes += [natural] * 6 + [full] * (9 + 9) + [wide] * 3 + [(2304, LANES)] * 2
+    scratch = [pltpu.VMEM((2 * ROWS, 6 * LANES), BF16)] * 2 + [pltpu.VMEM(shape, F32) for shape in shapes]
     scratch += [pltpu.VMEM(matrices.shape, BF16), pltpu.VMEM(turns.shape, F32)]
-    scratch += [dma((count,)) for count in (3, 2, 2, 2, 2, 3, 3, 3, 3, 2, 7)]
+    scratch += [dma((count,)) for count in (3, 2, 2, 3, 2, 2, 2, 2, 3, 3, 3, 3, 2, 7)]
     outs = pl.pallas_call(
         iterate,
         out_shape=(
@@ -698,6 +789,14 @@
         ),
         name="iterate",
     )(fine_state.reshape(2304, LANES), fine_terms.reshape(2304, LANES), jnp.asarray(matrices), jnp.asarray(turns))
+    outs = pl.pallas_call(
+        hand_out,
+        out_shape=[jax.ShapeDtypeStruct(out.shape, F32) for out in outs],
+        in_specs=[pl.BlockSpec(memory_space=pltpu.VMEM)] * 3,
+        out_specs=[pl.BlockSpec(memory_space=pl.ANY)] * 3,
+        scratch_shapes=[dma((3 * PIECES,))],
+        name="hand_out",
+    )(*outs)
     return (
         outs[0].reshape(1, 2, 2, 16, 1, 3, 1, 1024),
         outs[1].reshape(1, 2, 16, 1, 3, 1, 1024),

time: 146 us -> 140 us (0.959)
  local copies, waits for them, and re-layouts: 4.04 us -> 0 us
    unnamed x7 -> x0, local copies, waits for them, and re-layouts: 4.04 us -> none
    pallas_call x1, Pallas kernels: 141 us -> 137 us  [shards(): pl.pallas_call(iterate, out_shape=(jax.ShapeDtypeStruct((1536, LANES), F3...]
    pallas_call x0 -> x1, Pallas kernels: none -> 2.44 us  [shards(): pl.pallas_call(hand_out, out_shape=[jax.ShapeDtypeStruct(out.shape, F32)...]
where the time goes in v4:
time: 140 us
  Pallas kernels  140 us (100%)
    pallas_call x1, Pallas kernels, shards(): pl.pallas_call(iterate, out_shape=(jax.ShapeDtypeStruct((1536, LANES), F3...  137 us

profile of v4, /device:TPU:33, one launch (start us, length us, event | category | flops | bytes accessed | tf_op | source)
XLA Modules:
  0.0 140.3 jit_solution(16653572260596326819)
XLA Ops:
  0.6 137.2 %iterate.1 = (f32[1536,128]{1,0:T(8,128)}, f32[768,128]{1,0:T(8,128)}, f32[384,128]{1,0:T(8,128)}) custom-call(f32[2304,128]{1,0:T(8,128)} %bitcast.5, f32[2304,128]{1,0:T(8,128)} %bitcast.6, bf16[2944,512]{1,0:T(8,128)(2,1)} %constant.4.clone.matrices_hbm, f32[2048,128]{1,0:T(8,128)} %constant.5.clone.turns_hbm), custom_call_target="tpu_custom_call" | custom-call | tf_op jit(solution)/shard_map/iterate/pallas_call | solution.py:777
  137.9 2.4 %hand_out.1 = (f32[1536,128]{1,0:T(8,128)}, f32[768,128]{1,0:T(8,128)}, f32[384,128]{1,0:T(8,128)}) custom-call(f32[1536,128]{1,0:T(8,128)} %get-tuple-element.9.refs_0_, f32[768,128]{1,0:T(8,128)} %get-tuple-element.10.refs_1_, f32[384,128]{1,0:T(8,128)} %get-tuple-element.11.refs_2_), custom_call_target="tpu_custom_call" | custom-call | tf_op jit(solution)/shard_map/hand_out/pallas_call | solution.py:792

commit v5 on v4

--- a/solution.py
+++ b/solution.py
@@ -122,14 +122,18 @@
 
 def constant_tables():
     index = np.arange(ROWS)
-    phase = 2.0 * math.pi * np.outer(index, index) / ROWS
+    phase = 2.0 * math.pi * np.outer(np.arange(ROWS // 2) + 0.5, index) / ROWS
     along_y = np.concatenate([np.cos(phase), np.sin(phase)], axis=1)
-    small = 2.0 * math.pi * np.outer(np.arange(GROUP), np.arange(GROUP)) / GROUP
-    eye = np.eye(8)
-    along_x = np.concatenate([np.kron(np.cos(small), eye), -np.kron(np.sin(small), eye)], axis=1)
+    back_y = np.concatenate([np.cos(phase).T, np.sin(phase).T], axis=1)
+    small = 2.0 * math.pi * np.outer(np.arange(GROUP) + 0.5, np.arange(GROUP)) / GROUP
+    along_x = np.concatenate([np.cos(small), -np.sin(small)], axis=1).reshape(GROUP, 2, GROUP)
+    half = GROUP // 2
+    order = np.stack([np.arange(half), GROUP - 1 - np.arange(half)], axis=1).reshape(-1)
+    back_x = np.kron(along_x[order].transpose(1, 2, 0).reshape(2 * GROUP, GROUP), np.eye(8))
+    along_x = np.kron(along_x[:half].reshape(half, 2 * GROUP), np.eye(8))
     maps = lane_maps()
-    matrices = list(halves(along_y)) + [maps[0]] + list(halves(along_x))
-    matrices.append(np.concatenate(halves(along_x.T), axis=1))
+    matrices = list(halves(along_y)) + [np.concatenate(halves(back_y), axis=1), maps[0]]
+    matrices += list(halves(along_x)) + [np.concatenate(halves(back_x), axis=1)]
     lane = np.arange(LANES)
     turns, inner_parts = [], []
     for extent in (EDGE // 2, EDGE):
@@ -140,13 +144,13 @@
             np.concatenate([fore_high, fore_high, fore_low, np.concatenate([back_high, back_low], axis=1)], axis=0)
         )
         inner = extent // GROUP
-        turn = 2.0 * math.pi * np.outer(index // 8, lane % inner) / extent
+        turn = 2.0 * math.pi * np.outer(index // 8, lane % inner / extent - 0.5 / GROUP)
         turns += [np.cos(turn), np.sin(turn)]
         if extent < EDGE:
             offset = (lane % 16) // 8
         else:
             offset = np.array([0, 2, 1, 3])[(lane % 64) // 16]
-        turn = 2.0 * math.pi * np.outer(index, offset) / extent
+        turn = 2.0 * math.pi * np.outer(index, offset / extent - 0.5 / ROWS)
         turns += [np.cos(turn), np.sin(turn)]
     matrices.append(np.concatenate(inner_parts, axis=1))
     matrices += maps[1:]
@@ -205,7 +209,7 @@
         (turns_hbm, turns, 0, 1024),
         (state_hbm, state_ref, 768, 1536),
         (terms_hbm, terms_ref, 0, 2304),
-        (matrices_hbm, matrices, 768, 2176),
+        (matrices_hbm, matrices, 768, 1920),
         (turns_hbm, turns, 1024, 1024),
     ):
         rows = pl.ds(start, size)
@@ -215,14 +219,15 @@
     def matrix(start, size, first=0, width=512):
         return matrices.at[pl.ds(start, size), pl.ds(first, width)]
 
-    y_high, y_low = matrix(0, 256), matrix(256, 256)
+    y_halves = (matrix(0, 256, 0, 256), matrix(0, 256, 256, 256))
+    yt_high, yt_low = matrix(256, 256, 0, 256), matrix(256, 256, 256, 256)
     spread_map, curl_map = matrix(512, 256, 0, 256), matrix(512, 256, 256, 256)
-    x_high, x_low = matrix(768, 256), matrix(1024, 256)
-    xt_high, xt_low = matrix(1280, 512, 0, 256), matrix(1280, 512, 256, 256)
-    fore_high_c, fore_low_c, back_c = (matrix(*rows, 0, 256) for rows in ((1792, 256), (2048, 128), (2176, 256)))
-    fore_high_f, fore_low_f, back_f = (matrix(*rows, 256, 256) for rows in ((1792, 256), (2048, 128), (2176, 256)))
-    finish_map, spread_map_f = matrix(2432, 256, 0, 256), matrix(2432, 256, 256, 256)
-    place_map, finish_map_f = matrix(2688, 256, 0, 384), matrix(2688, 256, 384, 128)
+    x_halves = (matrix(768, 256, 0, 256), matrix(768, 256, 256, 256))
+    xt_high, xt_low = matrix(1024, 512, 0, 256), matrix(1024, 512, 256, 256)
+    fore_high_c, fore_low_c, back_c = (matrix(*rows, 0, 256) for rows in ((1536, 256), (1792, 128), (1920, 256)))
+    fore_high_f, fore_low_f, back_f = (matrix(*rows, 256, 256) for rows in ((1536, 256), (1792, 128), (1920, 256)))
+    finish_map, spread_map_f = matrix(2176, 256, 0, 256), matrix(2176, 256, 256, 256)
+    place_map, finish_map_f = matrix(2432, 256, 0, 384), matrix(2432, 256, 384, 128)
     turn_xc_c, turn_xs_c, turn_yc_c, turn_ys_c, turn_xc_f, turn_xs_f, turn_yc_f, turn_ys_f = (
         turns.at[pl.ds(start, ROWS), :] for start in range(0, 8 * ROWS, ROWS)
     )
@@ -374,10 +379,36 @@
                     pieces.append(ref[pl.ds(start, 16, stride=24), :])
             target[pl.ds(half * 128, 128), tile(component)] = jnp.concatenate(pieces, axis=0).T
 
-    def y_product(first, count, target):
+    def half_products(matrices_two, first, count, target):
         part = pl.ds(first * LANES, count * LANES)
-        high, low = rhs_high[:, part], rhs_low[:, part]
-        target[...] = dot(y_high[...], high) + dot(y_high[...], low) + dot(y_low[...], high)
+        halves_two = []
+        for index, both_parts in enumerate(matrices_two):
+            rows = pl.ds(index * ROWS, ROWS)
+            both = dot(both_parts[...], rhs_high[rows, part])
+            rest = dot(both_parts[pl.ds(0, 128), :], rhs_low[rows, part])
+            halves_two.append(both[:128] + both[128:] + rest)
+        even, odd = halves_two
+        total, difference = even + odd, even - odd
+        for step in range(16):
+            lines = slice(step * 8, step * 8 + 8)
+            target[pl.ds(step * 16, 8), :] = total[lines]
+            target[pl.ds(step * 16 + 8, 8), :] = difference[lines]
+
+    def y_back(first, count):
+        part = pl.ds(first * LANES, count * LANES)
+        high, low = rhs_high[pl.ds(0, ROWS), part], rhs_low[pl.ds(0, ROWS), part]
+        grid_buf[:, part] = dot(yt_high[...], high) + dot(yt_high[...], low) + dot(yt_low[...], high)
+
+    def folded(value):
+        mirrored = value.reshape(16, 2, 8, LANES)
+        first, second = mirrored[:, 0].reshape(128, LANES), mirrored[:, 1].reshape(128, LANES)
+        return first + second, first - second
+
+    def stack_back(index, upper, lower):
+        for start, value in ((0, upper), (128, lower)):
+            high, low = split(value)
+            rhs_high[pl.ds(start, 128), tile(index)] = high
+            rhs_low[pl.ds(start, 128), tile(index)] = low
 
     def pair(high, low):
         return jnp.concatenate([high, low], axis=1)
@@ -407,7 +438,7 @@
             cosine, sine = turn_yc_c[rows, :], turn_ys_c[rows, :]
             twisted(rows, 0, mixed[:, :LANES], mixed[:, LANES:], cosine, sine)
             twisted(rows, 1, curled[:, LANES:], -curled[:, :LANES], cosine, sine)
-        y_product(0, 2, target)
+        half_products(y_halves, 0, 2, target)
 
     def to_grid(source, first, fore_high, fore_low, cosine, sine):
         every = pl.ds(0, ROWS)
@@ -417,8 +448,7 @@
             real, imag = inner[:, :LANES], inner[:, LANES:]
             stack(every, first + index, real * cosine - imag * sine, real * sine + imag * cosine)
         part = pl.ds(first * LANES, 2 * LANES)
-        high, low = rhs_high[:, part], rhs_low[:, part]
-        grid_buf[:, part] = dot(x_high[...], high) + dot(x_high[...], low) + dot(x_low[...], high)
+        half_products(x_halves, first, 2, grid_buf.at[:, part])
 
     def from_grid(value, target, back, cosine, sine):
         high, low = split(value)
@@ -437,12 +467,10 @@
         from_grid(crossed, target, back_c, cosine, sine)
 
     def finish_coarse(source, start_ref, right_ref, target, same_ref, cross_ref, damp_ref):
-        for rows in chunks(128):
-            value = source[rows, :]
-            other = turned(value)
-            stack(rows, 0, value, -other)
-            stack(rows, 1, other, value)
-        y_product(0, 2, grid_buf.at[:, pl.ds(0, 2 * LANES)])
+        even, odd = folded(source[...])
+        stack_back(0, even, -turned(odd))
+        stack_back(1, turned(even), odd)
+        y_back(0, 2)
         for rows in chunks(128):
             value = grid_buf[rows, tile(0)] * turn_yc_c[rows, :] - grid_buf[rows, tile(1)] * turn_ys_c[rows, :]
             modes = dot(pair(*split(value)), finish_map[...])
@@ -596,7 +624,7 @@
                     twisted(rows, index, mixed[:, :LANES], mixed[:, LANES:], cosine, sine)
                 else:
                     twisted(rows, index, mixed[:, LANES:], -mixed[:, :LANES], cosine, sine)
-        y_product(first, 2, fine_send.at[first // 2])
+        half_products(y_halves, first, 2, fine_send.at[first // 2])
 
     def give_back(source, component, target, base):
         for half in range(2):
@@ -623,10 +651,9 @@
         return fields[0] * fields[3] - fields[1] * fields[2]
 
     def gather_fine(component):
-        for rows in chunks(128):
-            value = fine_back_recv[component, rows, :]
-            stack(rows, component, value, -turned(value))
-        y_product(component, 1, grid_buf.at[:, tile(component)])
+        even, odd = folded(fine_back_recv[component])
+        stack_back(component, even, -turned(odd))
+        y_back(component, 1)
         for rows in chunks(128):
             value = grid_buf[rows, tile(component)]
             value = value * turn_yc_f[rows, :] - turned(value) * turn_ys_f[rows, :]
@@ -749,17 +776,21 @@
 
 
 def hand_out(*refs):
-    sources, targets, sems = refs[:3], refs[3:6], refs[6]
-    copies = []
-    for source, target in zip(sources, targets):
+    sources, targets, buffers, load_sems, save_sems = refs[:3], refs[3:6], refs[6:9], refs[9], refs[10]
+    loads, saves = [], []
+    for source, target, buffer in zip(sources, targets, buffers):
         size = source.shape[0] // PIECES
         for piece in range(PIECES):
-            rows = pl.ds(piece * size, size)
-            copies.append(pltpu.make_async_copy(source.at[rows], target.at[rows], sems.at[len(copies)]))
-    for copy in copies:
-        copy.start()
-    for copy in copies:
-        copy.wait()
+            rows, number = pl.ds(piece * size, size), len(loads)
+            loads.append(pltpu.make_async_copy(source.at[rows], buffer.at[rows], load_sems.at[number]))
+            saves.append(pltpu.make_async_copy(buffer.at[rows], target.at[rows], save_sems.at[number]))
+    for load in loads:
+        load.start()
+    for load, save in zip(loads, saves):
+        load.wait()
+        save.start()
+    for save in saves:
+        save.wait()
 
 
 def shards(fine_state, fine_terms):
@@ -792,9 +823,10 @@
     outs = pl.pallas_call(
         hand_out,
         out_shape=[jax.ShapeDtypeStruct(out.shape, F32) for out in outs],
-        in_specs=[pl.BlockSpec(memory_space=pltpu.VMEM)] * 3,
+        in_specs=[pl.BlockSpec(memory_space=pl.ANY)] * 3,
         out_specs=[pl.BlockSpec(memory_space=pl.ANY)] * 3,
-        scratch_shapes=[dma((3 * PIECES,))],
+        scratch_shapes=[pltpu.VMEM(out.shape, F32) for out in outs] + [dma((3 * PIECES,))] * 2,
+        compiler_params=pltpu.CompilerParams(vmem_limit_bytes=62 * 1024 * 1024),
         name="hand_out",
     )(*outs)
     return (

time: 140 us -> 133 us (0.950)
  Pallas kernels: 140 us -> 132 us
    pallas_call x1, Pallas kernels: 137 us -> 130 us  [shards(): pl.pallas_call(iterate, out_shape=(jax.ShapeDtypeStruct((1536, LANES), F3...]
where the time goes in v5:
time: 133 us
  Pallas kernels  132 us (99%)
    pallas_call x1, Pallas kernels, shards(): pl.pallas_call(iterate, out_shape=(jax.ShapeDtypeStruct((1536, LANES), F3...  130 us

profile of v5, /device:TPU:33, one launch (start us, length us, event | category | flops | bytes accessed | tf_op | source)
XLA Modules:
  0.0 132.9 jit_solution(6732197882784075390)
XLA Ops:
  0.6 130.0 %iterate.1 = (f32[1536,128]{1,0:T(8,128)}, f32[768,128]{1,0:T(8,128)}, f32[384,128]{1,0:T(8,128)}) custom-call(f32[2304,128]{1,0:T(8,128)} %bitcast.5, f32[2304,128]{1,0:T(8,128)} %bitcast.6, bf16[2688,512]{1,0:T(8,128)(2,1)} %constant.4.clone.matrices_hbm, f32[2048,128]{1,0:T(8,128)} %constant.5.clone.turns_hbm), custom_call_target="tpu_custom_call" | custom-call | tf_op jit(solution)/shard_map/iterate/pallas_call | solution.py:808
  130.6 2.3 %hand_out.1 = (f32[1536,128]{1,0:T(8,128)}, f32[768,128]{1,0:T(8,128)}, f32[384,128]{1,0:T(8,128)}) custom-call(f32[1536,128]{1,0:T(8,128)} %get-tuple-element.9.refs_0_, f32[768,128]{1,0:T(8,128)} %get-tuple-element.10.refs_1_, f32[384,128]{1,0:T(8,128)} %get-tuple-element.11.refs_2_), custom_call_target="tpu_custom_call" | custom-call | tf_op jit(solution)/shard_map/hand_out/pallas_call | solution.py:823

commit v6 on v5

--- a/solution.py
+++ b/solution.py
@@ -18,7 +18,6 @@
 GROUP = 32
 ROWS = 256
 LANES = 128
-PIECES = 4
 F32 = jnp.float32
 BF16 = jnp.bfloat16
 MESH = pl.DeviceIdType.MESH
@@ -201,6 +200,7 @@
     state_ref, terms_ref, matrices, turns,
     fore_sent, fore_got, back_sent, back_got, hand_sems, parcel_sems, news_sent, news_got,
     fine_sent, fine_got, fine_back_sent, fine_back_got, start_sems, load_sems,
+    ready,
 ):
     loads = []
     for source, target, start, size in (
@@ -242,14 +242,33 @@
 
     barrier = pltpu.get_barrier_semaphore()
     number = rank * GROUP + place
+    near = (core == 0) & (high_z + low_z < 2)
+
+    def signal(semaphore, other):
+        target = (other // GROUP, (other // 8) % 4, other % 8)
+        pl.semaphore_signal(semaphore, inc=1, device_id=target, device_id_type=MESH)
+
+    def greet_first(step, carry):
+        signal(barrier, (place + step) % GROUP)
+        return carry
+
+    @pl.when(near)
+    def _():
+        @pl.when(rank > 0)
+        def _():
+            signal(barrier, place)
+
+        lax.fori_loop(1, GROUP, greet_first, 0)
 
     def greet(step, carry):
-        other = (number + step) % (4 * GROUP)
-        target = (other // GROUP, (other // 8) % 4, other % 8)
-        pl.semaphore_signal(barrier, inc=1, device_id=target, device_id_type=MESH)
+        signal(barrier, GROUP + (number + 2 * GROUP + step) % (3 * GROUP))
         return carry
 
-    lax.fori_loop(1, 4 * GROUP, greet, 0)
+    @pl.when(rank == 0)
+    def _():
+        greet(0, 0)
+
+    lax.fori_loop(1, 3 * GROUP, greet, 0)
 
     def block(position):
         return pl.ds(pl.multiple_of(position * 8, 8), 8)
@@ -486,10 +505,21 @@
     def _():
         spread_coarse(parcel_send.at[0], fore_send.at[0], place_f32)
 
-    pl.semaphore_wait(barrier, 4 * GROUP - 1)
+    @pl.when(rank > 0)
+    def _():
+        pl.semaphore_wait(barrier, 4 * GROUP - 1)
+
+    def greet_last(step, carry):
+        signal(ready, (place + step) % GROUP)
+        return carry
+
+    @pl.when(jnp.logical_not(near))
+    def _():
+        lax.fori_loop(0, GROUP, greet_last, 0)
 
     @pl.when(rank == 0)
     def _():
+        pl.semaphore_wait(barrier, 3 * GROUP // 2 - 1)
         post_other(fore_send.at[0], fore_recv.at[0], fore_sent.at[0], fore_got.at[0], DUTY, 0, place)
 
     def combine(a, carry):
@@ -519,6 +549,10 @@
 
     following = (rank + 1, at_y, at_pz)
 
+    @pl.when(rank == 0)
+    def _():
+        pl.semaphore_wait(ready, 5 * GROUP // 2)
+
     @pl.when(rank < 3)
     def _():
         send_one(start_send, start_recv, start_sems.at[0], start_sems.at[1], following).start()
@@ -589,19 +623,21 @@
     def _():
         coarse_tables(place_f32, keep_same_r, keep_cross_r, damp_r)
 
-    def correct_fine():
+    def correct_fine(weights, old_ref, target):
         for rows in chunks(128):
             nodes = [news[node, rows, :] for node in range(3)]
-            change_one = sum(w * n for w, n in zip(STATE_ONE, nodes)) - old_one[rows, :]
-            change_two = sum(w * n for w, n in zip(STATE_TWO, nodes)) - old_two[rows, :]
-            placed_one = dot(pair(*split(change_one)), place_map[...])
-            placed_two = dot(pair(*split(change_two)), place_map[...])
-            stiff, damping = stiff_f[rows, :], damp_f[rows, :]
+            change = sum(w * n for w, n in zip(weights, nodes)) - old_ref[rows, :]
+            placed = dot(pair(*split(change)), place_map[...])
+            stiff = stiff_f[rows, :]
             for component in range(3):
                 part = tile(component)
                 lanes = slice(component * LANES, (component + 1) * LANES)
-                node_f[rows, part] = (right_one_f[rows, part] + stiff * placed_one[:, lanes]) * damping
-                right_two_f[rows, part] = right_two_f[rows, part] + stiff * placed_two[:, lanes]
+                target[rows, part] = target[rows, part] + stiff * placed[:, lanes]
+
+    def start_fine():
+        correct_fine(STATE_ONE, old_one, right_one_f)
+        for component in range(3):
+            node_f[:, tile(component)] = right_one_f[:, tile(component)] * damp_f[...]
 
     def fine_field(index, rows):
         x, y, z = (node_f.at[rows, tile(component)] for component in range(3))
@@ -700,11 +736,12 @@
             tables = (keep_same_r, keep_cross_r, damp_r)
             finish_coarse(last_recv, news.at[1], parcel_send.at[2], news.at[2], *tables)
 
-        correct_fine()
+        start_fine()
         for part in range(3):
             spread_fine(2 * part)
             pairs = (fine_send.at[part], fine_recv.at[part], fine_sent.at[part], fine_got.at[part])
             post_own(*pairs, RANK, rank, place)
+        correct_fine(STATE_TWO, old_two, right_two_f)
         give_back_coarse(news.at[1], 0)
         give_back_coarse(news.at[2], 192)
         for part in range(3):
@@ -775,24 +812,6 @@
         receive(start_send, start_sems.at[0])
 
 
-def hand_out(*refs):
-    sources, targets, buffers, load_sems, save_sems = refs[:3], refs[3:6], refs[6:9], refs[9], refs[10]
-    loads, saves = [], []
-    for source, target, buffer in zip(sources, targets, buffers):
-        size = source.shape[0] // PIECES
-        for piece in range(PIECES):
-            rows, number = pl.ds(piece * size, size), len(loads)
-            loads.append(pltpu.make_async_copy(source.at[rows], buffer.at[rows], load_sems.at[number]))
-            saves.append(pltpu.make_async_copy(buffer.at[rows], target.at[rows], save_sems.at[number]))
-    for load in loads:
-        load.start()
-    for load, save in zip(loads, saves):
-        load.wait()
-        save.start()
-    for save in saves:
-        save.wait()
-
-
 def shards(fine_state, fine_terms):
     matrices, turns = constant_tables()
     full, natural, wide = (ROWS, LANES), (768, LANES), (ROWS, 3 * LANES)
@@ -805,6 +824,7 @@
     scratch = [pltpu.VMEM((2 * ROWS, 6 * LANES), BF16)] * 2 + [pltpu.VMEM(shape, F32) for shape in shapes]
     scratch += [pltpu.VMEM(matrices.shape, BF16), pltpu.VMEM(turns.shape, F32)]
     scratch += [dma((count,)) for count in (3, 2, 2, 3, 2, 2, 2, 2, 3, 3, 3, 3, 2, 7)]
+    scratch += [pltpu.SemaphoreType.REGULAR]
     outs = pl.pallas_call(
         iterate,
         out_shape=(
@@ -816,19 +836,10 @@
         out_specs=[pl.BlockSpec(memory_space=pltpu.VMEM)] * 3,
         scratch_shapes=scratch,
         compiler_params=pltpu.CompilerParams(
-            collective_id=0, has_side_effects=True, vmem_limit_bytes=62 * 1024 * 1024
+            collective_id=0, has_side_effects=True, vmem_limit_bytes=52 * 1024 * 1024
         ),
         name="iterate",
     )(fine_state.reshape(2304, LANES), fine_terms.reshape(2304, LANES), jnp.asarray(matrices), jnp.asarray(turns))
-    outs = pl.pallas_call(
-        hand_out,
-        out_shape=[jax.ShapeDtypeStruct(out.shape, F32) for out in outs],
-        in_specs=[pl.BlockSpec(memory_space=pl.ANY)] * 3,
-        out_specs=[pl.BlockSpec(memory_space=pl.ANY)] * 3,
-        scratch_shapes=[pltpu.VMEM(out.shape, F32) for out in outs] + [dma((3 * PIECES,))] * 2,
-        compiler_params=pltpu.CompilerParams(vmem_limit_bytes=62 * 1024 * 1024),
-        name="hand_out",
-    )(*outs)
     return (
         outs[0].reshape(1, 2, 2, 16, 1, 3, 1, 1024),
         outs[1].reshape(1, 2, 16, 1, 3, 1, 1024),

time: 133 us -> 131 us (0.985)
  Pallas kernels: 132 us -> 128 us
  local copies, waits for them, and re-layouts: 0 us -> 2.3 us
    unnamed x0 -> x3, local copies, waits for them, and re-layouts: none -> 2.3 us
    pallas_call x1 -> x0, Pallas kernels: 2.29 us -> none  [shards(): pl.pallas_call(hand_out, out_shape=[jax.ShapeDtypeStruct(out.shape, F32)...]
    pallas_call x1, Pallas kernels: 130 us -> 128 us  [shards(): pl.pallas_call(iterate, out_shape=(jax.ShapeDtypeStruct((1536, LANES), F3...]
where the time goes in v6:
time: 131 us
  Pallas kernels  128 us (98%)
  local copies, waits for them, and re-layouts  2.3 us (2%)
    pallas_call x1, Pallas kernels, shards(): pl.pallas_call(iterate, out_shape=(jax.ShapeDtypeStruct((1536, LANES), F3...  128 us

profile of v6, /device:TPU:33, one launch (start us, length us, event | category | flops | bytes accessed | tf_op | source)
XLA Modules:
  0.0 130.8 jit_solution(17566362080272605862)
XLA Ops:
  0.6 127.9 %iterate.1 = (f32[1536,128]{1,0:T(8,128)S(1)}, f32[768,128]{1,0:T(8,128)S(1)}, f32[384,128]{1,0:T(8,128)S(1)}) custom-call(f32[2304,128]{1,0:T(8,128)} %bitcast.8, f32[2304,128]{1,0:T(8,128)} %bitcast.9, bf16[2688,512]{1,0:T(8,128)(2,1)} %constant.4.clone.matrices_hbm, f32[2048,128]{1,0:T(8,128)} %constant.5.clone.turns_hbm), custom_call_target="tpu_custom_call" | custom-call | tf_op jit(solution)/shard_map/iterate/pallas_call | solution.py:828
  128.5 0.9 copy.16
  129.4 0.7 copy.17
  130.1 0.7 copy.18

commit v7 on v6

--- a/solution.py
+++ b/solution.py
@@ -403,6 +403,10 @@
         halves_two = []
         for index, both_parts in enumerate(matrices_two):
             rows = pl.ds(index * ROWS, ROWS)
+            if count == 1:
+                both = dot(both_parts[...], pair(rhs_high[rows, part], rhs_low[rows, part]))
+                halves_two.append(both[:128, :LANES] + both[128:, :LANES] + both[:128, LANES:])
+                continue
             both = dot(both_parts[...], rhs_high[rows, part])
             rest = dot(both_parts[pl.ds(0, 128), :], rhs_low[rows, part])
             halves_two.append(both[:128] + both[128:] + rest)
@@ -444,30 +448,42 @@
         rhs_high[lower, tile(index)] = high
         rhs_low[lower, tile(index)] = low
 
-    def spread_coarse(source, target, position):
+    def spread_coarse(source, target, position, deliver):
         lanes = lax.broadcasted_iota(jnp.int32, (1, LANES), 1) % 8
         mode_x = lanes.astype(F32) * GROUP + position
         weight = jnp.where(mode_x == 0, 0.5, 1.0)
-        for rows in chunks(128):
-            velocity = source[rows, :] * weight
-            high_y, low_y = split(velocity * curl_y[rows, :])
-            high_x, low_x = split(velocity * (UNIT * mode_x))
-            mixed = dot(pair(*split(velocity)), spread_map[...])
-            curled = dot(pair(high_y, high_x), curl_map[...]) + dot(pair(low_y, low_x), curl_map[...])
-            cosine, sine = turn_yc_c[rows, :], turn_ys_c[rows, :]
-            twisted(rows, 0, mixed[:, :LANES], mixed[:, LANES:], cosine, sine)
-            twisted(rows, 1, curled[:, LANES:], -curled[:, :LANES], cosine, sine)
-        half_products(y_halves, 0, 2, target)
-
-    def to_grid(source, first, fore_high, fore_low, cosine, sine):
+        for index in range(2):
+            for rows in chunks(128):
+                velocity = source[rows, :] * weight
+                cosine, sine = turn_yc_c[rows, :], turn_ys_c[rows, :]
+                if index == 0:
+                    mixed = dot(pair(*split(velocity)), spread_map[...])
+                    twisted(rows, 0, mixed[:, :LANES], mixed[:, LANES:], cosine, sine)
+                else:
+                    high_y, low_y = split(velocity * curl_y[rows, :])
+                    high_x, low_x = split(velocity * (UNIT * mode_x))
+                    curled = dot(pair(high_y, high_x), curl_map[...]) + dot(pair(low_y, low_x), curl_map[...])
+                    twisted(rows, 1, curled[:, LANES:], -curled[:, :LANES], cosine, sine)
+            half_products(y_halves, index, 1, target.at[:, tile(index)])
+            deliver(index)
+
+    def fields_to(slot, target, index):
+        return (
+            fore_send.at[slot].at[:, tile(index)],
+            fore_recv.at[target].at[:, tile(index)],
+            fore_sent.at[2 * slot + index],
+            fore_got.at[2 * target + index],
+        )
+
+    def to_grid(source, first, count, fore_high, fore_low, cosine, sine):
         every = pl.ds(0, ROWS)
-        for index in range(2):
+        for index in range(count):
             high, low = split(source[:, tile(index)])
             inner = dot(pair(high, low), fore_high[...]) + dot(high, fore_low[...])
             real, imag = inner[:, :LANES], inner[:, LANES:]
             stack(every, first + index, real * cosine - imag * sine, real * sine + imag * cosine)
-        part = pl.ds(first * LANES, 2 * LANES)
-        half_products(x_halves, first, 2, grid_buf.at[:, part])
+        part = pl.ds(first * LANES, count * LANES)
+        half_products(x_halves, first, count, grid_buf.at[:, part])
 
     def from_grid(value, target, back, cosine, sine):
         high, low = split(value)
@@ -478,9 +494,12 @@
         both = dot(high, back[...])
         target[...] = both[:, :LANES] + both[:, LANES:] + dot(low, back[:, :LANES])
 
-    def grid_coarse(source, target):
+    def grid_coarse(slot, target):
         cosine, sine = turn_xc_c[...], turn_xs_c[...]
-        to_grid(source, 0, fore_high_c, fore_low_c, cosine, sine)
+        for index in range(2):
+            source = fore_recv.at[slot].at[:, tile(index)]
+            receive(source, fore_got.at[2 * slot + index])
+            to_grid(source, index, 1, fore_high_c, fore_low_c, cosine, sine)
         speed, spin = grid_buf[:, tile(0)], grid_buf[:, tile(1)]
         crossed = speed * roll(spin, -32) - roll(speed, -32) * spin
         from_grid(crossed, target, back_c, cosine, sine)
@@ -503,7 +522,7 @@
 
     @pl.when(rank == 0)
     def _():
-        spread_coarse(parcel_send.at[0], fore_send.at[0], place_f32)
+        spread_coarse(parcel_send.at[0], fore_send.at[0], place_f32, lambda index: None)
 
     @pl.when(rank > 0)
     def _():
@@ -520,7 +539,8 @@
     @pl.when(rank == 0)
     def _():
         pl.semaphore_wait(barrier, 3 * GROUP // 2 - 1)
-        post_other(fore_send.at[0], fore_recv.at[0], fore_sent.at[0], fore_got.at[0], DUTY, 0, place)
+        for index in range(2):
+            post_other(*fields_to(0, 0, index), DUTY, 0, place)
 
     def combine(a, carry):
         wave_x = UNIT * (a.astype(F32) * GROUP + place_f32)
@@ -563,8 +583,7 @@
     coarse_tables(spot_f32, keep_same, keep_cross, damp_c)
 
     def coarse_sweep():
-        receive(fore_recv.at[0], fore_got.at[0])
-        grid_coarse(fore_recv.at[0], back_send.at[0])
+        grid_coarse(0, back_send.at[0])
         post_own(back_send.at[0], back_recv.at[0], back_sent.at[0], back_got.at[0], DUTY, duty, spot)
         receive(parcel_recv, parcel_sems.at[1])
 
@@ -580,11 +599,14 @@
         receive(back_recv.at[0], back_got.at[0])
         tables = (keep_same, keep_cross, damp_c)
         finish_coarse(back_recv.at[0], sweep.at[0], parcel_recv.at[1], sweep.at[1], *tables)
-        spread_coarse(sweep.at[1], fore_send.at[1], spot_f32)
-        post_own(fore_send.at[1], fore_recv.at[1], fore_sent.at[1], fore_got.at[1], DUTY, duty, spot)
+        spread_coarse(
+            sweep.at[1],
+            fore_send.at[1],
+            spot_f32,
+            lambda index: post_own(*fields_to(1, 1, index), DUTY, duty, spot),
+        )
         to_partner(sweep.at[pl.ds(0, 2)], news.at[pl.ds(0, 2)], news_sent.at[0], news_got.at[0])
-        receive(fore_recv.at[1], fore_got.at[1])
-        grid_coarse(fore_recv.at[1], back_send.at[1])
+        grid_coarse(1, back_send.at[1])
 
         @pl.when(duty == 3)
         def _():
@@ -595,9 +617,13 @@
             post_own(back_send.at[1], back_recv.at[1], back_sent.at[1], back_got.at[1], DUTY, duty, spot)
             receive(back_recv.at[1], back_got.at[1])
             finish_coarse(back_recv.at[1], sweep.at[1], parcel_recv.at[2], sweep.at[2], *tables)
-            spread_coarse(sweep.at[2], fore_send.at[2], spot_f32)
             after = duty + 1
-            post(fore_send.at[2], fore_recv.at[0], fore_sent.at[2], fore_got.at[0], DUTY, after, spot, GROUP)
+            spread_coarse(
+                sweep.at[2],
+                fore_send.at[2],
+                spot_f32,
+                lambda index: post(*fields_to(2, 0, index), DUTY, after, spot, GROUP),
+            )
             address = (low_z * 2 + after % 2, at_y, (after // 2) * 4 + at_x)
             send_one(sweep.at[2], hand_recv, hand_sems.at[0], hand_sems.at[1], address).start()
             to_partner(sweep.at[2], news.at[2], news_sent.at[1], news_got.at[1])
@@ -746,7 +772,7 @@
         give_back_coarse(news.at[2], 192)
         for part in range(3):
             receive(fine_recv.at[part], fine_got.at[part])
-            to_grid(fine_recv.at[part], 2 * part, fore_high_f, fore_low_f, turn_xc_f[...], turn_xs_f[...])
+            to_grid(fine_recv.at[part], 2 * part, 2, fore_high_f, fore_low_f, turn_xc_f[...], turn_xs_f[...])
         for part in range(3):
             from_grid(cross_fine(part), fine_back_send.at[part], back_f, turn_xc_f[...], turn_xs_f[...])
             pairs = (fine_back_send.at[part], fine_back_recv.at[part])
@@ -780,9 +806,11 @@
 
     @pl.when(rank == 0)
     def _():
-        drain_other(fore_send.at[0], fore_sent.at[0])
-
-    drain(fore_send.at[1], fore_sent.at[1], GROUP - 1)
+        for index in range(2):
+            drain_other(fore_send.at[0].at[:, tile(index)], fore_sent.at[index])
+
+    for index in range(2):
+        drain(fore_send.at[1].at[:, tile(index)], fore_sent.at[2 + index], GROUP - 1)
     drain(back_send.at[0], back_sent.at[0], GROUP - 1)
     for part in range(3):
         drain(fine_send.at[part], fine_sent.at[part], GROUP - 1)
@@ -795,7 +823,8 @@
     @pl.when(duty < 3)
     def _():
         drain(back_send.at[1], back_sent.at[1], GROUP - 1)
-        drain(fore_send.at[2], fore_sent.at[2], GROUP)
+        for index in range(2):
+            drain(fore_send.at[2].at[:, tile(index)], fore_sent.at[4 + index], GROUP)
         receive(sweep.at[2], hand_sems.at[0])
 
     @pl.when(jnp.logical_not(alone))
@@ -823,7 +852,7 @@
     shapes += [natural] * 6 + [full] * (9 + 9) + [wide] * 3 + [(2304, LANES)] * 2
     scratch = [pltpu.VMEM((2 * ROWS, 6 * LANES), BF16)] * 2 + [pltpu.VMEM(shape, F32) for shape in shapes]
     scratch += [pltpu.VMEM(matrices.shape, BF16), pltpu.VMEM(turns.shape, F32)]
-    scratch += [dma((count,)) for count in (3, 2, 2, 3, 2, 2, 2, 2, 3, 3, 3, 3, 2, 7)]
+    scratch += [dma((count,)) for count in (6, 4, 2, 3, 2, 2, 2, 2, 3, 3, 3, 3, 2, 7)]
     scratch += [pltpu.SemaphoreType.REGULAR]
     outs = pl.pallas_call(
         iterate,

time: 131 us -> 132 us (level)
  no operation moved by 1% of the time
where the time goes in v7:
time: 132 us
  Pallas kernels  129 us (98%)
  local copies, waits for them, and re-layouts  2.3 us (2%)
    pallas_call x1, Pallas kernels, shards(): pl.pallas_call(iterate, out_shape=(jax.ShapeDtypeStruct((1536, LANES), F3...  129 us

profile of v7, /device:TPU:33, one launch (start us, length us, event | category | flops | bytes accessed | tf_op | source)
XLA Modules:
  0.0 131.7 jit_solution(15993401956680801975)
XLA Ops:
  0.6 128.8 %iterate.1 = (f32[1536,128]{1,0:T(8,128)S(1)}, f32[768,128]{1,0:T(8,128)S(1)}, f32[384,128]{1,0:T(8,128)S(1)}) custom-call(f32[2304,128]{1,0:T(8,128)} %bitcast.8, f32[2304,128]{1,0:T(8,128)} %bitcast.9, bf16[2688,512]{1,0:T(8,128)(2,1)} %constant.4.clone.matrices_hbm, f32[2048,128]{1,0:T(8,128)} %constant.5.clone.turns_hbm), custom_call_target="tpu_custom_call" | custom-call | tf_op jit(solution)/shard_map/iterate/pallas_call | solution.py:857
  129.4 0.9 copy.16
  130.3 0.7 copy.17
  131.0 0.7 copy.18

commit v8 on v6

--- a/solution.py
+++ b/solution.py
@@ -107,6 +107,18 @@
     table = np.kron(1j ** (np.outer(quarters, powers) % 4), np.eye(16))
     spread_f = doubled(np.concatenate([real_form(table), real_form(1j * table)], axis=1))
     finish_f = doubled(real_form(np.conj(table).T))
+    phases = 1j ** (np.outer((0, 3), powers) % 4)
+
+    def change(sources):
+        moves = np.zeros((4, 2), dtype=complex)
+        for field, source, factor in sources:
+            moves[source, field] = factor
+        table = np.kron(np.kron(moves, phases), np.eye(8))
+        return np.concatenate([real_form(table), real_form(1j * table)], axis=1)
+
+    change_one = doubled(change(((0, 0, 1), (1, 1, 1))))
+    change_two = np.concatenate([change(((0, 2, 1),)), change(((1, 2, 1j),))], axis=0)
+    change_three = np.concatenate([change(((1, 0, -1j),)), change(((0, 2, -1j), (1, 1, 1j)))], axis=0)
     place = np.zeros((3, 4, 2, 8, 4, 16))
     for component in range(3):
         for a in range(8):
@@ -115,7 +127,13 @@
     place_f = doubled(np.concatenate([real_form(table.reshape(64, 64).astype(complex)) for table in place], axis=1))
     return [
         np.concatenate(pair, axis=1).astype(ml_dtypes.bfloat16)
-        for pair in ((spread_c, curl_c), (finish_c, spread_f), (place_f, finish_f))
+        for pair in (
+            (spread_c, curl_c),
+            (finish_c, spread_f),
+            (place_f, finish_f),
+            (change_one, change_two),
+            (change_three, 0.0 * change_three),
+        )
     ]
 
 
@@ -153,6 +171,19 @@
         turns += [np.cos(turn), np.sin(turn)]
     matrices.append(np.concatenate(inner_parts, axis=1))
     matrices += maps[1:]
+    inner = EDGE // GROUP
+    phase = 2.0 * math.pi * np.outer(np.arange(8), np.arange(inner)) / inner
+    table = np.zeros((2, 4, 8, 2, 2, 4, inner))
+    for field in range(2):
+        for position in range(4):
+            table[field, position, :, field, 0, position] = 2.0 / EDGE * np.cos(phase)
+            table[field, position, :, field, 1, position] = 2.0 / EDGE * np.sin(phase)
+    table = table.reshape(64, 2, 2, 128)
+    table = np.concatenate([table, np.stack([-table[:, :, 1], table[:, :, 0]], axis=2)], axis=0)
+    high, low = halves(table.reshape(128, 512))
+    matrices += [high, high, low]
+    turn = 2.0 * math.pi * np.outer(index, np.array([0, 2, 1, 3])[(lane % 32) // 8] / EDGE - 0.5 / ROWS)
+    turns += [np.cos(turn), np.sin(turn)]
     return np.concatenate(matrices, axis=0), np.concatenate(turns, axis=0).astype(np.float32)
 
 
@@ -197,10 +228,11 @@
     curl_y, keep_same, keep_cross, damp_c, keep_same_r, keep_cross_r, damp_r, old_one, old_two,
     ky_f, damp_f, stiff_f, cos_f, sin_f, same_x, same_y, cross_f, mask_f,
     right_one_f, right_two_f, node_f,
+    base_grid, change_send, change_recv, stiff_r,
     state_ref, terms_ref, matrices, turns,
     fore_sent, fore_got, back_sent, back_got, hand_sems, parcel_sems, news_sent, news_got,
     fine_sent, fine_got, fine_back_sent, fine_back_got, start_sems, load_sems,
-    ready,
+    change_sent, change_got, ready,
 ):
     loads = []
     for source, target, start, size in (
@@ -209,8 +241,8 @@
         (turns_hbm, turns, 0, 1024),
         (state_hbm, state_ref, 768, 1536),
         (terms_hbm, terms_ref, 0, 2304),
-        (matrices_hbm, matrices, 768, 1920),
-        (turns_hbm, turns, 1024, 1024),
+        (matrices_hbm, matrices, 768, 2816),
+        (turns_hbm, turns, 1024, 1536),
     ):
         rows = pl.ds(start, size)
         loads.append(pltpu.make_async_copy(source.at[rows], target.at[rows], load_sems.at[len(loads)]))
@@ -228,8 +260,10 @@
     fore_high_f, fore_low_f, back_f = (matrix(*rows, 256, 256) for rows in ((1536, 256), (1792, 128), (1920, 256)))
     finish_map, spread_map_f = matrix(2176, 256, 0, 256), matrix(2176, 256, 256, 256)
     place_map, finish_map_f = matrix(2432, 256, 0, 384), matrix(2432, 256, 384, 128)
-    turn_xc_c, turn_xs_c, turn_yc_c, turn_ys_c, turn_xc_f, turn_xs_f, turn_yc_f, turn_ys_f = (
-        turns.at[pl.ds(start, ROWS), :] for start in range(0, 8 * ROWS, ROWS)
+    change_maps = (matrix(2688, 256, 0, 256), matrix(2688, 256, 256, 256), matrix(2944, 256, 0, 256))
+    change_fore_high, change_fore_low = matrix(3200, 256), matrix(3456, 128)
+    turn_xc_c, turn_xs_c, turn_yc_c, turn_ys_c, turn_xc_f, turn_xs_f, turn_yc_f, turn_ys_f, turn_c, turn_s = (
+        turns.at[pl.ds(start, ROWS), :] for start in range(0, 10 * ROWS, ROWS)
     )
     rank = lax.axis_index("tm")
     at_y, at_pz = lax.axis_index("py"), lax.axis_index("pz")
@@ -367,7 +401,7 @@
         damp = 1.0 / (1.0 + HALF_STEP * VISCOSITY * wave_sq)
         return wave_x, wave_y, wave_sq, mask, inverse, damp
 
-    def coarse_tables(position, same_ref, cross_ref, damp_ref):
+    def coarse_tables(position, same_ref, cross_ref, damp_ref, stiff_ref=None):
         slot = (lane % 64) // 16
         mode_x = (lane % 8).astype(F32) * GROUP + position
         mode_y = (row - 256 * ((lane % 16) // 8)).astype(F32)
@@ -376,6 +410,8 @@
         same_ref[...] = same * (HALF_STEP * damp)
         cross_ref[...] = jnp.where(slot == 2, 0.0, -wave_x * wave_y * inverse) * (HALF_STEP * damp)
         damp_ref[...] = damp
+        if stiff_ref is not None:
+            stiff_ref[...] = (2.0 * VISCOSITY) * wave_sq * damp
 
     curl_y[...] = UNIT * (row - 256 * ((lane % 16) // 8)).astype(F32)
 
@@ -403,6 +439,10 @@
         halves_two = []
         for index, both_parts in enumerate(matrices_two):
             rows = pl.ds(index * ROWS, ROWS)
+            if count == 1:
+                both = dot(both_parts[...], pair(rhs_high[rows, part], rhs_low[rows, part]))
+                halves_two.append(both[:128, :LANES] + both[128:, :LANES] + both[:128, LANES:])
+                continue
             both = dot(both_parts[...], rhs_high[rows, part])
             rest = dot(both_parts[pl.ds(0, 128), :], rhs_low[rows, part])
             halves_two.append(both[:128] + both[128:] + rest)
@@ -621,7 +661,7 @@
 
     @pl.when(rank == 3)
     def _():
-        coarse_tables(place_f32, keep_same_r, keep_cross_r, damp_r)
+        coarse_tables(place_f32, keep_same_r, keep_cross_r, damp_r, stiff_r)
 
     def correct_fine(weights, old_ref, target):
         for rows in chunks(128):
@@ -634,8 +674,41 @@
                 lanes = slice(component * LANES, (component + 1) * LANES)
                 target[rows, part] = target[rows, part] + stiff * placed[:, lanes]
 
+    def spread_change(index):
+        mode_x = (lax.broadcasted_iota(jnp.int32, (1, LANES), 1) % 8).astype(F32) * GROUP + place_f32
+        weight = jnp.where(mode_x == 0, 0.5, 1.0)
+        for rows in chunks(128):
+            nodes = [news[node, rows, :] for node in range(3)]
+            value = sum(w * n for w, n in zip(STATE_ONE, nodes)) - old_one[rows, :]
+            value = value * stiff_r[rows, :] * weight
+            if index == 0:
+                mixed = dot(pair(*split(value)), change_maps[0][...])
+            else:
+                first, second = value, value * curl_y[rows, :]
+                if index == 2:
+                    first, second = second, value * (UNIT * mode_x)
+                first_high, first_low = split(first)
+                second_high, second_low = split(second)
+                mixed = dot(pair(first_high, second_high), change_maps[index][...])
+                mixed = mixed + dot(pair(first_low, second_low), change_maps[index][...])
+            twisted(rows, index, mixed[:, :LANES], mixed[:, LANES:], turn_c[rows, :], turn_s[rows, :])
+        half_products(y_halves, index, 1, change_send.at[index])
+
+    def change_to_grid(index, cosine, sine):
+        every = pl.ds(0, ROWS)
+        high, low = split(change_recv[index])
+        inner = dot(pair(high, low), change_fore_high[...]) + dot(high, change_fore_low[...])
+        for field in range(2):
+            real = inner[:, 2 * field * LANES : (2 * field + 1) * LANES]
+            imag = inner[:, (2 * field + 1) * LANES : (2 * field + 2) * LANES]
+            stack(every, 2 * index + field, real * cosine - imag * sine, real * sine + imag * cosine)
+        half_products(x_halves, 2 * index, 2, grid_buf.at[:, pl.ds(2 * index * LANES, 2 * LANES)])
+
     def start_fine():
         correct_fine(STATE_ONE, old_one, right_one_f)
+        set_node()
+
+    def set_node():
         for component in range(3):
             node_f[:, tile(component)] = right_one_f[:, tile(component)] * damp_f[...]
 
@@ -710,7 +783,7 @@
                 total = node_f[rows, part] + HALF_STEP * value + right_two_f[rows, part]
                 node_f[rows, part] = total * damp_f[rows, :]
 
-    def fine_sweep():
+    def prepare_fine():
         @pl.when(rank == 0)
         def _():
             first = pl.ds(0, 768)
@@ -724,29 +797,55 @@
         for component in range(3):
             fine_tile(right_one, component, right_one_f)
             fine_tile(right_two, component, right_two_f)
-        receive(news.at[pl.ds(0, 2)], news_got.at[0])
-
-        @pl.when(rank < 3)
-        def _():
-            receive(news.at[2], news_got.at[1])
-
-        @pl.when(rank == 3)
-        def _():
-            receive(last_recv, back_got.at[2])
-            tables = (keep_same_r, keep_cross_r, damp_r)
-            finish_coarse(last_recv, news.at[1], parcel_send.at[2], news.at[2], *tables)
-
-        start_fine()
+
+    def send_fine():
         for part in range(3):
             spread_fine(2 * part)
             pairs = (fine_send.at[part], fine_recv.at[part], fine_sent.at[part], fine_got.at[part])
             post_own(*pairs, RANK, rank, place)
+
+    def take_fine():
+        for part in range(3):
+            receive(fine_recv.at[part], fine_got.at[part])
+            to_grid(fine_recv.at[part], 2 * part, fore_high_f, fore_low_f, turn_xc_f[...], turn_xs_f[...])
+
+    def fine_sweep():
+        @pl.when(rank < 3)
+        def _():
+            prepare_fine()
+            receive(news.at[pl.ds(0, 2)], news_got.at[0])
+            receive(news.at[2], news_got.at[1])
+            start_fine()
+            send_fine()
+
+        @pl.when(rank == 3)
+        def _():
+            take_fine()
+            base_grid[...] = grid_buf[...]
+            receive(news.at[pl.ds(0, 2)], news_got.at[0])
+            receive(last_recv, back_got.at[2])
+            tables = (keep_same_r, keep_cross_r, damp_r)
+            finish_coarse(last_recv, news.at[1], parcel_send.at[2], news.at[2], *tables)
+            for part in range(3):
+                spread_change(part)
+                pairs = (change_send.at[part], change_recv.at[part], change_sent.at[part], change_got.at[part])
+                post_own(*pairs, RANK, rank, place)
+            start_fine()
+
         correct_fine(STATE_TWO, old_two, right_two_f)
         give_back_coarse(news.at[1], 0)
         give_back_coarse(news.at[2], 192)
-        for part in range(3):
-            receive(fine_recv.at[part], fine_got.at[part])
-            to_grid(fine_recv.at[part], 2 * part, fore_high_f, fore_low_f, turn_xc_f[...], turn_xs_f[...])
+        @pl.when(rank < 3)
+        def _():
+            take_fine()
+
+        @pl.when(rank == 3)
+        def _():
+            for part in range(3):
+                receive(change_recv.at[part], change_got.at[part])
+                change_to_grid(part, turn_xc_f[...], turn_xs_f[...])
+            grid_buf[...] = grid_buf[...] + base_grid[...]
+
         for part in range(3):
             from_grid(cross_fine(part), fine_back_send.at[part], back_f, turn_xc_f[...], turn_xs_f[...])
             pairs = (fine_back_send.at[part], fine_back_recv.at[part])
@@ -761,6 +860,12 @@
             give_back(right_one_f, component, term_out, 0)
             give_back(node_f, component, nodes_out, 768)
 
+    @pl.when(rank == 3)
+    def _():
+        prepare_fine()
+        set_node()
+        send_fine()
+
     early = high_z * (1 - low_z)
 
     def phase(step, carry):
@@ -806,6 +911,11 @@
         @pl.when(duty < 3)
         def _():
             receive(sweep.at[2], news_sent.at[1])
+
+    @pl.when(rank == 3)
+    def _():
+        for part in range(3):
+            drain(change_send.at[part], change_sent.at[part], GROUP - 1)
 
     @pl.when(rank < 3)
     def _():
@@ -820,10 +930,11 @@
     shapes = [(ROWS, 6 * LANES)]
     shapes += [(3, ROWS, 2 * LANES), (2, ROWS, 2 * LANES), (2, ROWS, LANES), (2, ROWS, LANES), full, full]
     shapes += [tiles] * 4 + [(3, ROWS, 2 * LANES)] * 2 + [tiles] * 2
-    shapes += [natural] * 6 + [full] * (9 + 9) + [wide] * 3 + [(2304, LANES)] * 2
+    shapes += [natural] * 6 + [full] * (9 + 9) + [wide] * 3
+    shapes += [(ROWS, 6 * LANES), tiles, tiles, full, (2304, LANES), (2304, LANES)]
     scratch = [pltpu.VMEM((2 * ROWS, 6 * LANES), BF16)] * 2 + [pltpu.VMEM(shape, F32) for shape in shapes]
     scratch += [pltpu.VMEM(matrices.shape, BF16), pltpu.VMEM(turns.shape, F32)]
-    scratch += [dma((count,)) for count in (3, 2, 2, 3, 2, 2, 2, 2, 3, 3, 3, 3, 2, 7)]
+    scratch += [dma((count,)) for count in (3, 2, 2, 3, 2, 2, 2, 2, 3, 3, 3, 3, 2, 7, 3, 3)]
     scratch += [pltpu.SemaphoreType.REGULAR]
     outs = pl.pallas_call(
         iterate,

time: 131 us -> 133 us (1.015)
  Pallas kernels: 128 us -> 130 us
    pallas_call x1, Pallas kernels: 128 us -> 130 us  [shards(): pl.pallas_call(iterate, out_shape=(jax.ShapeDtypeStruct((1536, LANES), F3...]
where the time goes in v8:
time: 133 us
  Pallas kernels  130 us (98%)
  local copies, waits for them, and re-layouts  2.3 us (2%)
    pallas_call x1, Pallas kernels, shards(): pl.pallas_call(iterate, out_shape=(jax.ShapeDtypeStruct((1536, LANES), F3...  130 us

profile of v8, /device:TPU:33, one launch (start us, length us, event | category | flops | bytes accessed | tf_op | source)
XLA Modules:
  0.0 132.6 jit_solution(10674995020659698285)
XLA Ops:
  0.6 129.7 %iterate.1 = (f32[1536,128]{1,0:T(8,128)S(1)}, f32[768,128]{1,0:T(8,128)S(1)}, f32[384,128]{1,0:T(8,128)S(1)}) custom-call(f32[2304,128]{1,0:T(8,128)} %bitcast.8, f32[2304,128]{1,0:T(8,128)} %bitcast.9, bf16[3584,512]{1,0:T(8,128)(2,1)} %constant.4.clone.matrices_hbm, f32[2560,128]{1,0:T(8,128)} %constant.5.clone.turns_hbm), custom_call_target="tpu_custom_call" | custom-call | tf_op jit(solution)/shard_map/iterate/pallas_call | solution.py:939
  130.3 0.9 copy.16
  131.2 0.7 copy.17
  131.9 0.7 copy.18

commit v9 on v6

--- a/solution.py
+++ b/solution.py
@@ -214,7 +214,8 @@
     ):
         rows = pl.ds(start, size)
         loads.append(pltpu.make_async_copy(source.at[rows], target.at[rows], load_sems.at[len(loads)]))
-        loads[-1].start()
+    for load in loads[:3]:
+        load.start()
 
     def matrix(start, size, first=0, width=512):
         return matrices.at[pl.ds(start, size), pl.ds(first, width)]
@@ -500,6 +501,8 @@
     coarse_tile(state_ref, 0, 0.5, parcel_send.at[0])
     loads[1].wait()
     loads[2].wait()
+    for load in loads[3:]:
+        load.start()
 
     @pl.when(rank == 0)
     def _():

time: 131 us -> 131 us (level)
  no operation moved by 1% of the time
where the time goes in v9:
time: 131 us
  Pallas kernels  128 us (98%)
  local copies, waits for them, and re-layouts  2.3 us (2%)
    pallas_call x1, Pallas kernels, shards(): pl.pallas_call(iterate, out_shape=(jax.ShapeDtypeStruct((1536, LANES), F3...  128 us

profile of v9, /device:TPU:33, one launch (start us, length us, event | category | flops | bytes accessed | tf_op | source)
XLA Modules:
  0.0 130.9 jit_solution(12207971730600231801)
XLA Ops:
  0.6 128.0 %iterate.1 = (f32[1536,128]{1,0:T(8,128)S(1)}, f32[768,128]{1,0:T(8,128)S(1)}, f32[384,128]{1,0:T(8,128)S(1)}) custom-call(f32[2304,128]{1,0:T(8,128)} %bitcast.8, f32[2304,128]{1,0:T(8,128)} %bitcast.9, bf16[2688,512]{1,0:T(8,128)(2,1)} %constant.4.clone.matrices_hbm, f32[2048,128]{1,0:T(8,128)} %constant.5.clone.turns_hbm), custom_call_target="tpu_custom_call" | custom-call | tf_op jit(solution)/shard_map/iterate/pallas_call | solution.py:831
  128.6 0.9 copy.16
  129.5 0.7 copy.17
  130.2 0.7 copy.18
